TPU v7x, 32 devices: a whole 2x2x4 slice. The times are simulated.
32 devices in a mesh: fsdp: 32 (over z, y, x, core).
Axes of the slice: x: 2, y: 2, z: 4, core: 2. Of those that a mesh axis runs over, the one named last changes fastest.
Arguments:
- inputs: bfloat16 [2, 32, 384, 1024], P(None, 'fsdp'), may hold values from -6 to 6
- cotangent: bfloat16 [2, 32, 384, 1024], P(None, 'fsdp'), may hold values from -6 to 6
- lengths: int32 [2, 32], replicated, may hold values from 96 to 384, as said below
- owners: int32 [2, 32], replicated, may hold values from 0 to 31, each once within a row
- attn_gain: bfloat16 [1024], P('fsdp'), may hold values from 0.25 to 1.75
- query_weight: bfloat16 [1024, 1024], P('fsdp'), may hold values from -0.1875 to 0.1875
- key_weight: bfloat16 [1024, 1024], P('fsdp'), may hold values from -0.1875 to 0.1875
- value_weight: bfloat16 [1024, 1024], P('fsdp'), may hold values from -0.1875 to 0.1875
- beta_weight: bfloat16 [1024, 8], P('fsdp'), may hold values from -0.1875 to 0.1875
- query_conv: bfloat16 [4, 1024], P(None, 'fsdp'), may hold values from -3 to 3
- key_conv: bfloat16 [4, 1024], P(None, 'fsdp'), may hold values from -3 to 3
- value_conv: bfloat16 [4, 1024], P(None, 'fsdp'), may hold values from -3 to 3
- out_gain: bfloat16 [128], P('fsdp'), may hold values from 0.25 to 1.75
- out_weight: bfloat16 [1024, 1024], P(None, 'fsdp'), may hold values from -0.1875 to 0.1875
- mlp_gain: bfloat16 [1024], P('fsdp'), may hold values from 0.25 to 1.75
- gate_weight: bfloat16 [1024, 2816], P('fsdp'), may hold values from -0.1875 to 0.1875
- up_weight: bfloat16 [1024, 2816], P('fsdp'), may hold values from -0.1875 to 0.1875
- down_weight: bfloat16 [2816, 1024], P(None, 'fsdp'), may hold values from -0.109375 to 0.109375
Outputs:
- block_out: bfloat16 [2, 32, 384, 1024], P(None, 'fsdp')
- input_gradient_rows: bfloat16 [2, 32, 384, 1024], P(None, 'fsdp')
- attn_gain_grad: float32 [1024], P('fsdp')
- query_weight_grad: float32 [1024, 1024], P('fsdp')
- key_weight_grad: float32 [1024, 1024], P('fsdp')
- value_weight_grad: float32 [1024, 1024], P('fsdp')
- beta_weight_grad: float32 [1024, 8], P('fsdp')
- query_conv_grad: float32 [4, 1024], P(None, 'fsdp')
- key_conv_grad: float32 [4, 1024], P(None, 'fsdp')
- value_conv_grad: float32 [4, 1024], P(None, 'fsdp')
- out_gain_grad: float32 [128], P('fsdp')
- out_weight_grad: float32 [1024, 1024], P(None, 'fsdp')
- mlp_gain_grad: float32 [1024], P('fsdp')
- gate_weight_grad: float32 [1024, 2816], P('fsdp')
- up_weight_grad: float32 [1024, 2816], P('fsdp')
- down_weight_grad: float32 [2816, 1024], P(None, 'fsdp')
Inputs may be any that keep to these rules, and one draw needn't show every extreme that they name: `lengths`: in every micro-batch one sequence has exactly 384 tokens. Each row of owners names every device once.
All inputs are finite; a program needn't handle non-finite values.
Results may differ from a plain program's by a relative error of at most 0.012.
Values may be sent and summed in bfloat16 or wider, within the bound.
A program may use at most 256 MiB of HBM per device.

v0:
```python
import jax
import jax.numpy as jnp
from jax import lax
from jax.sharding import PartitionSpec as P

HEADS = 8
HEAD = 128
SPAN = 64


NORM_EPS = 1e-05
UNIT_EPS = 1e-06
MIXER_PRECISION = lax.Precision.HIGH


def rms_norm(values, norm_gain):
    return (
        values * lax.rsqrt(jnp.mean(values * values, axis=-1, keepdims=True) + NORM_EPS) * norm_gain
    )


def unit_heads(values):
    by_head = values.reshape(values.shape[0], HEADS, HEAD)
    scaled = by_head * lax.rsqrt(jnp.sum(by_head * by_head, axis=-1, keepdims=True) + UNIT_EPS)
    return scaled.reshape(values.shape)


def causal_conv(values, conv_taps):
    running = values * conv_taps[0]
    for offset in range(1, conv_taps.shape[0]):
        shifted = jnp.pad(values, ((offset, 0), (0, 0)))[: values.shape[0]]
        running = running + shifted * conv_taps[offset]
    return running


def inverse_unit_lower(strict):
    eye_mat = jnp.eye(strict.shape[-1], dtype=strict.dtype)
    result = eye_mat - strict
    power_mat = strict
    for doubling in range(strict.shape[-1].bit_length() - 2):
        power_mat = jnp.einsum("bij,bjk->bik", power_mat, power_mat, precision=MIXER_PRECISION)
        result = result + jnp.einsum("bij,bjk->bik", result, power_mat, precision=MIXER_PRECISION)
    return result


def delta_rule(queries, key_rows, value_rows, strength):
    batch_size, length, key_depth = queries.shape
    blocks = length // SPAN

    def by_block(values):
        return jnp.moveaxis(values.reshape((batch_size, blocks, SPAN) + values.shape[2:]), 1, 0)

    def span_step(state_mat, block_in):
        query_blk, key_blk, value_blk, beta_blk = block_in
        scaled_keys = key_blk * beta_blk[..., None]
        strict = jnp.tril(
            jnp.einsum("bid,bjd->bij", scaled_keys, key_blk, precision=MIXER_PRECISION), -1
        )
        inverse = inverse_unit_lower(strict)
        weight_rows = jnp.einsum("bij,bjd->bid", inverse, scaled_keys, precision=MIXER_PRECISION)
        update_rows = jnp.einsum(
            "bij,bje->bie", inverse, value_blk * beta_blk[..., None], precision=MIXER_PRECISION
        )
        fresh_rows = update_rows - jnp.einsum(
            "bcd,bde->bce", weight_rows, state_mat, precision=MIXER_PRECISION
        )
        scores = jnp.tril(jnp.einsum("bid,bjd->bij", query_blk, key_blk, precision=MIXER_PRECISION))
        output = jnp.einsum("bcd,bde->bce", query_blk, state_mat, precision=MIXER_PRECISION)
        output = output + jnp.einsum("bij,bje->bie", scores, fresh_rows, precision=MIXER_PRECISION)
        state_mat = state_mat + jnp.einsum(
            "bcd,bce->bde", key_blk, fresh_rows, precision=MIXER_PRECISION
        )
        return (state_mat, output)

    initial = jnp.zeros((batch_size, key_depth, value_rows.shape[-1]), jnp.float32)
    final_state, outputs = lax.scan(
        jax.checkpoint(span_step),
        initial,
        (by_block(queries), by_block(key_rows), by_block(value_rows), by_block(strength)),
    )
    return jnp.moveaxis(outputs, 0, 1).reshape(batch_size, length, -1)


def prepare(query_pre, key_pre, value_pre, beta_pre, query_taps, key_taps, value_taps):
    queries = unit_heads(jax.nn.silu(causal_conv(query_pre, query_taps)))
    key_rows = unit_heads(jax.nn.silu(causal_conv(key_pre, key_taps)))
    value_rows = jax.nn.silu(causal_conv(value_pre, value_taps))
    return (queries, key_rows, value_rows, jax.nn.sigmoid(beta_pre))


def token_mixer(queries, key_rows, value_rows, strength, norm_gain):
    length = queries.shape[0]

    def to_heads(values):
        return values.reshape(length, HEADS, HEAD).transpose(1, 0, 2)

    mixed_rows = delta_rule(to_heads(queries), to_heads(key_rows), to_heads(value_rows), strength.T)
    normed = rms_norm(mixed_rows.transpose(1, 0, 2), norm_gain)
    return normed.reshape(length, HEADS * HEAD)


def swiglu(gate_pre, up_pre):
    return jax.nn.silu(gate_pre) * up_pre


def rounded(values):
    return lax.optimization_barrier(values.astype(jnp.bfloat16)).astype(jnp.float32)


def product(left_mat, right_mat):
    return jnp.dot(left_mat, right_mat, preferred_element_type=jnp.float32)


def contract_rows(left_mat, right_mat):
    return lax.dot_general(
        left_mat, right_mat, (((0,), (0,)), ((), ())), preferred_element_type=jnp.float32
    )


def contract_cols(left_mat, right_mat):
    return lax.dot_general(
        left_mat, right_mat, (((1,), (1,)), ((), ())), preferred_element_type=jnp.float32
    )


def ownership(length_row, owner_row, partition_count):
    seq_ends = jnp.cumsum(length_row)
    starts = seq_ends - length_row
    part_ids = jnp.arange(partition_count, dtype=jnp.int32)
    match_mat = (owner_row[None, :] == part_ids[:, None]).astype(jnp.int32)
    return (
        jnp.sum(match_mat * starts[None, :], axis=1),
        jnp.sum(match_mat * length_row[None, :], axis=1),
    )


def forward_pass(owned_rows, active_rows, gathered):
    (
        attn_gain,
        query_weight,
        key_weight,
        value_weight,
        beta_weight,
        query_conv,
        key_conv,
        value_conv,
        out_gain,
        out_weight,
        mlp_gain,
        gate_weight,
        up_weight,
        down_weight,
    ) = gathered
    own_float = owned_rows.astype(jnp.float32)
    attn_in, attn_norm_back = jax.vjp(rms_norm, own_float, attn_gain.astype(jnp.float32))
    attn_low = attn_in.astype(jnp.bfloat16)
    prepared, prepare_back = jax.vjp(
        prepare,
        product(attn_low, query_weight),
        product(attn_low, key_weight),
        product(attn_low, value_weight),
        product(attn_low, beta_weight),
        query_conv.astype(jnp.float32),
        key_conv.astype(jnp.float32),
        value_conv.astype(jnp.float32),
    )
    mixed_rows, mixer_back = jax.vjp(
        token_mixer,
        rounded(prepared[0]),
        rounded(prepared[1]),
        rounded(prepared[2]),
        prepared[3],
        out_gain.astype(jnp.float32),
    )
    mixed_low = mixed_rows.astype(jnp.bfloat16)
    hidden = own_float + product(mixed_low, out_weight)
    mlp_in, mlp_norm_back = jax.vjp(rms_norm, hidden, mlp_gain.astype(jnp.float32))
    mlp_low = mlp_in.astype(jnp.bfloat16)
    activated, swiglu_back = jax.vjp(
        swiglu, product(mlp_low, gate_weight), product(mlp_low, up_weight)
    )
    act_low = activated.astype(jnp.bfloat16)
    result = hidden + product(act_low, down_weight)
    result = jnp.where(active_rows[:, None], result, 0.0).astype(jnp.bfloat16)
    saved = (
        attn_low,
        mlp_low,
        mixed_low,
        act_low,
        attn_norm_back,
        prepare_back,
        mixer_back,
        mlp_norm_back,
        swiglu_back,
    )
    return (result, saved)


def backward_pass(grad_rows, active_rows, gathered, saved):
    (
        attn_gain,
        query_weight,
        key_weight,
        value_weight,
        beta_weight,
        query_conv,
        key_conv,
        value_conv,
        out_gain,
        out_weight,
        mlp_gain,
        gate_weight,
        up_weight,
        down_weight,
    ) = gathered
    (
        attn_low,
        mlp_low,
        mixed_low,
        act_low,
        attn_norm_back,
        prepare_back,
        mixer_back,
        mlp_norm_back,
        swiglu_back,
    ) = saved
    grad_out = jnp.where(active_rows[:, None], grad_rows, jnp.zeros((), jnp.bfloat16))
    down_grad = contract_rows(act_low, grad_out)
    grad_act = contract_cols(grad_out, down_weight)
    grad_gate, grad_up = swiglu_back(grad_act)
    gate_low = grad_gate.astype(jnp.bfloat16)
    up_low = grad_up.astype(jnp.bfloat16)
    gate_grad = contract_rows(mlp_low, gate_low)
    up_grad = contract_rows(mlp_low, up_low)
    grad_mlp_in = contract_cols(gate_low, gate_weight) + contract_cols(up_low, up_weight)
    grad_hidden, mlp_gain_grad = mlp_norm_back(grad_mlp_in)
    grad_hidden = grad_hidden + grad_out.astype(jnp.float32)
    attn_low_grad = grad_hidden.astype(jnp.bfloat16)
    out_grad = contract_rows(mixed_low, attn_low_grad)
    grad_mixed = contract_cols(attn_low_grad, out_weight)
    grad_query, grad_key, grad_value, grad_beta, out_gain_grad = mixer_back(grad_mixed)
    (
        grad_query_pre,
        grad_key_pre,
        grad_value_pre,
        grad_beta_pre,
        query_conv_grad,
        key_conv_grad,
        value_conv_grad,
    ) = prepare_back((grad_query, grad_key, grad_value, grad_beta))
    query_low = grad_query_pre.astype(jnp.bfloat16)
    key_low = grad_key_pre.astype(jnp.bfloat16)
    value_low = grad_value_pre.astype(jnp.bfloat16)
    beta_low = grad_beta_pre.astype(jnp.bfloat16)
    query_grad = contract_rows(attn_low, query_low)
    key_grad = contract_rows(attn_low, key_low)
    value_grad = contract_rows(attn_low, value_low)
    beta_grad = contract_rows(attn_low, beta_low)
    grad_attn_in = contract_cols(query_low, query_weight) + contract_cols(key_low, key_weight)
    grad_attn_in = (
        grad_attn_in + contract_cols(value_low, value_weight) + contract_cols(beta_low, beta_weight)
    )
    grad_norm, attn_gain_grad = attn_norm_back(grad_attn_in)
    token_grad = (grad_norm + grad_hidden).astype(jnp.bfloat16)
    grad_terms = (
        attn_gain_grad,
        query_grad,
        key_grad,
        value_grad,
        beta_grad,
        query_conv_grad,
        key_conv_grad,
        value_conv_grad,
        out_gain_grad,
        out_grad,
        mlp_gain_grad,
        gate_grad,
        up_grad,
        down_grad,
    )
    return (token_grad, grad_terms)


def local(
    inputs,
    cotangent,
    lengths,
    owners,
    attn_gain,
    query_weight,
    key_weight,
    value_weight,
    beta_weight,
    query_conv,
    key_conv,
    value_conv,
    out_gain,
    out_weight,
    mlp_gain,
    gate_weight,
    up_weight,
    down_weight,
):
    partition_count = lax.axis_size("fsdp")
    my_index = lax.axis_index("fsdp")
    microbatch_count = inputs.shape[0]
    total_row_count = inputs.shape[2]
    hidden_width = inputs.shape[3]
    slot_count = total_row_count // partition_count
    part_ids = jnp.arange(partition_count, dtype=jnp.int32)
    slot_ids = jnp.arange(slot_count, dtype=jnp.int32)
    row_ids = jnp.arange(total_row_count, dtype=jnp.int32)
    zero_low = jnp.zeros((), jnp.bfloat16)
    out_blocks = []
    grad_blocks = []
    totals = None
    for micro_step in range(microbatch_count):
        own_start, own_len = ownership(lengths[micro_step], owners[micro_step], partition_count)
        first_pos = own_start + (my_index - own_start) % partition_count
        stream_pos = first_pos[:, None] + partition_count * slot_ids[None, :]
        send_live = stream_pos < (own_start + own_len)[:, None]
        send_rows = jnp.where(send_live, stream_pos // partition_count, 0).reshape(-1)
        local_rows = inputs[micro_step, 0]
        outgoing = jnp.where(
            send_live.reshape(-1, 1), jnp.take(local_rows, send_rows, axis=0), zero_low
        )
        outgoing = outgoing.reshape(partition_count, slot_count, hidden_width)
        incoming = lax.all_to_all(outgoing, "fsdp", split_axis=0, concat_axis=0, tiled=True)
        my_start = jnp.sum(jnp.where(part_ids == my_index, own_start, 0))
        my_len = jnp.sum(jnp.where(part_ids == my_index, own_len, 0))
        active_rows = row_ids < my_len
        from_rows = (my_start + row_ids) % partition_count * slot_count + row_ids // partition_count
        owned_rows = jnp.where(
            active_rows[:, None],
            jnp.take(
                incoming.reshape(partition_count * slot_count, hidden_width), from_rows, axis=0
            ),
            zero_low,
        )
        gathered = (
            lax.all_gather(attn_gain, "fsdp", axis=0, tiled=True),
            lax.all_gather(query_weight, "fsdp", axis=0, tiled=True),
            lax.all_gather(key_weight, "fsdp", axis=0, tiled=True),
            lax.all_gather(value_weight, "fsdp", axis=0, tiled=True),
            lax.all_gather(beta_weight, "fsdp", axis=0, tiled=True),
            lax.all_gather(query_conv, "fsdp", axis=1, tiled=True),
            lax.all_gather(key_conv, "fsdp", axis=1, tiled=True),
            lax.all_gather(value_conv, "fsdp", axis=1, tiled=True),
            lax.all_gather(out_gain, "fsdp", axis=0, tiled=True),
            lax.all_gather(out_weight, "fsdp", axis=1, tiled=True),
            lax.all_gather(mlp_gain, "fsdp", axis=0, tiled=True),
            lax.all_gather(gate_weight, "fsdp", axis=0, tiled=True),
            lax.all_gather(up_weight, "fsdp", axis=0, tiled=True),
            lax.all_gather(down_weight, "fsdp", axis=1, tiled=True),
        )
        result, saved = forward_pass(owned_rows, active_rows, gathered)
        out_blocks.append(result)
        back_weights = (
            lax.all_gather(attn_gain, "fsdp", axis=0, tiled=True),
            lax.all_gather(query_weight, "fsdp", axis=0, tiled=True),
            lax.all_gather(key_weight, "fsdp", axis=0, tiled=True),
            lax.all_gather(value_weight, "fsdp", axis=0, tiled=True),
            lax.all_gather(beta_weight, "fsdp", axis=0, tiled=True),
            lax.all_gather(query_conv, "fsdp", axis=1, tiled=True),
            lax.all_gather(key_conv, "fsdp", axis=1, tiled=True),
            lax.all_gather(value_conv, "fsdp", axis=1, tiled=True),
            lax.all_gather(out_gain, "fsdp", axis=0, tiled=True),
            lax.all_gather(out_weight, "fsdp", axis=1, tiled=True),
            lax.all_gather(mlp_gain, "fsdp", axis=0, tiled=True),
            lax.all_gather(gate_weight, "fsdp", axis=0, tiled=True),
            lax.all_gather(up_weight, "fsdp", axis=0, tiled=True),
            lax.all_gather(down_weight, "fsdp", axis=1, tiled=True),
        )
        token_grad, grad_terms = backward_pass(
            cotangent[micro_step, 0], active_rows, back_weights, saved
        )
        back_pos = (
            slot_ids[None, :] * partition_count + (part_ids[:, None] - my_start) % partition_count
        )
        back_live = back_pos < my_len
        returning = jnp.where(
            back_live.reshape(-1, 1),
            jnp.take(token_grad, jnp.where(back_live, back_pos, 0).reshape(-1), axis=0),
            zero_low,
        )
        returning = returning.reshape(partition_count, slot_count, hidden_width)
        returned = lax.all_to_all(returning, "fsdp", split_axis=0, concat_axis=0, tiled=True)
        target_rows = jnp.where(send_live, stream_pos // partition_count, total_row_count).reshape(
            -1
        )
        input_rows = (
            jnp.zeros((total_row_count, hidden_width), jnp.bfloat16)
            .at[target_rows]
            .set(returned.reshape(partition_count * slot_count, hidden_width), mode="drop")
        )
        grad_blocks.append(input_rows)
        totals = grad_terms if totals is None else jax.tree.map(jnp.add, totals, grad_terms)
    (
        gain_a,
        grad_q,
        grad_k,
        grad_v,
        grad_b,
        grad_cq,
        grad_ck,
        grad_cv,
        gain_o,
        grad_o,
        gain_m,
        grad_g,
        grad_u,
        grad_d,
    ) = totals
    finals = (
        lax.psum_scatter(gain_a, "fsdp", scatter_dimension=0, tiled=True),
        lax.psum_scatter(grad_q, "fsdp", scatter_dimension=0, tiled=True),
        lax.psum_scatter(grad_k, "fsdp", scatter_dimension=0, tiled=True),
        lax.psum_scatter(grad_v, "fsdp", scatter_dimension=0, tiled=True),
        lax.psum_scatter(grad_b, "fsdp", scatter_dimension=0, tiled=True),
        lax.psum_scatter(grad_cq, "fsdp", scatter_dimension=1, tiled=True),
        lax.psum_scatter(grad_ck, "fsdp", scatter_dimension=1, tiled=True),
        lax.psum_scatter(grad_cv, "fsdp", scatter_dimension=1, tiled=True),
        lax.psum_scatter(gain_o, "fsdp", scatter_dimension=0, tiled=True),
        lax.psum_scatter(grad_o, "fsdp", scatter_dimension=1, tiled=True),
        lax.psum_scatter(gain_m, "fsdp", scatter_dimension=0, tiled=True),
        lax.psum_scatter(grad_g, "fsdp", scatter_dimension=0, tiled=True),
        lax.psum_scatter(grad_u, "fsdp", scatter_dimension=0, tiled=True),
        lax.psum_scatter(grad_d, "fsdp", scatter_dimension=1, tiled=True),
    )
    (
        attn_gain_grad,
        query_weight_grad,
        key_weight_grad,
        value_weight_grad,
        beta_weight_grad,
        query_conv_grad,
        key_conv_grad,
        value_conv_grad,
        out_gain_grad,
        out_weight_grad,
        mlp_gain_grad,
        gate_weight_grad,
        up_weight_grad,
        down_weight_grad,
    ) = finals
    block_out = jnp.stack(out_blocks)[:, None]
    input_gradient_rows = jnp.stack(grad_blocks)[:, None]
    return (
        block_out,
        input_gradient_rows,
        attn_gain_grad,
        query_weight_grad,
        key_weight_grad,
        value_weight_grad,
        beta_weight_grad,
        query_conv_grad,
        key_conv_grad,
        value_conv_grad,
        out_gain_grad,
        out_weight_grad,
        mlp_gain_grad,
        gate_weight_grad,
        up_weight_grad,
        down_weight_grad,
    )


def solution(mesh):
    placed = (
        P(None, "fsdp", None, None),
        P(None, "fsdp", None, None),
        P(),
        P(),
        P("fsdp"),
        P("fsdp", None),
        P("fsdp", None),
        P("fsdp", None),
        P("fsdp", None),
        P(None, "fsdp"),
        P(None, "fsdp"),
        P(None, "fsdp"),
        P("fsdp"),
        P(None, "fsdp"),
        P("fsdp"),
        P("fsdp", None),
        P("fsdp", None),
        P(None, "fsdp"),
    )
    return jax.shard_map(
        local,
        mesh=mesh,
        in_specs=placed,
        out_specs=(
            P(None, "fsdp", None, None),
            P(None, "fsdp", None, None),
            P("fsdp"),
            P("fsdp", None),
            P("fsdp", None),
            P("fsdp", None),
            P("fsdp", None),
            P(None, "fsdp"),
            P(None, "fsdp"),
            P(None, "fsdp"),
            P("fsdp"),
            P(None, "fsdp"),
            P("fsdp"),
            P("fsdp", None),
            P("fsdp", None),
            P(None, "fsdp"),
        ),
        check_vma=False,
    )
```

profile of v0, /device:TPU:0, one launch (start us, length us, event | category | flops | bytes accessed | tf_op | source)
XLA Modules:
  0.0 2454.5 jit_solution(8439042477069831555)
XLA Ops:
  23.4 7.3 all-to-all-start
  35.8 50.0 %all-gather = bf16[32,32,4]{1,2,0:T(4,128)(2,1)S(1)} all-gather(bf16[1,32,4]{1,2,0:T(4,128)(2,1)S(1)} %bitcast.1518), channel_id=1, replica_groups=mesh['fsdp'=32] {'fsdp'}, dimensions={0}, use_global_device_ids=true | all-gather | bytes 8448 | tf_op jit(solution)/shard_map/all_gather | solution.py:347
  85.8 38.0 %all-gather.2 = bf16[32,32,4]{1,2,0:T(4,128)(2,1)S(1)} all-gather(bf16[1,32,4]{1,2,0:T(4,128)(2,1)S(1)} %bitcast.1519), channel_id=1, replica_groups=mesh['fsdp'=32] {'fsdp'}, dimensions={0}, use_global_device_ids=true | all-gather | bytes 8448 | tf_op jit(solution)/shard_map/all_gather | solution.py:348
  123.8 36.6 %all-gather.3 = bf16[32,32,4]{1,2,0:T(4,128)(2,1)S(1)} all-gather(bf16[1,32,4]{1,2,0:T(4,128)(2,1)S(1)} %bitcast.1520), channel_id=1, replica_groups=mesh['fsdp'=32] {'fsdp'}, dimensions={0}, use_global_device_ids=true | all-gather | bytes 8448 | tf_op jit(solution)/shard_map/all_gather | solution.py:346
  170.0 50.0 %all-reduce.67 = (bf16[1024]{0:T(1024)(128)(2,1)S(1)}, bf16[128]{0:T(256)(128)(2,1)S(1)}, bf16[1024]{0:T(1024)(128)(2,1)S(1)}) all-reduce(bf16[1024]{0:T(1024)(128)(2,1)S(1)} %dynamic-update-slice, bf16[128]{0:T(256)(128)(2,1)S(1)} %dynamic-update-slice.1, bf16[1024]{0:T(1024)(128)(2,1)S(1)} %dynamic-update-slice.2), channel_id=1, replica_groups=mesh['fsdp'=32] {'fsdp'}, use_global_device_ids=true, to_apply=%add.60 | all-reduce | flops 2176 | bytes 8704
  220.0 40.8 %all-gather.1 = bf16[32,32,8]{1,2,0:T(8,128)(2,1)S(1)} all-gather(bf16[1,32,8]{1,2,0:T(8,128)(2,1)S(1)} %bitcast.1517), channel_id=1, replica_groups=mesh['fsdp'=32] {'fsdp'}, dimensions={0}, use_global_device_ids=true | all-gather | bytes 16896 | tf_op jit(solution)/shard_map/all_gather | solution.py:345
  311.6 61.2 %while.80 = (s32[]{:T(128)}, f32[8,128,128]{2,1,0:T(8,128)S(1)}, f32[6,8,64,128]{3,2,0,1:T(8,128)}, f32[6,8,128,128]{3,2,1,0:T(8,128)}, f32[6,8,64,128]{3,2,1,0:...) while((s32[]{:T(128)}, f32[8,128,128]{2,1,0:T(8,128)S(1)}, ...), condition=%wide.region_9.11_spmd.clone, body=%wide.region_8.10_spmd.clone.sunk | while | flops 403906560 | bytes 11993254 | solution.py:76
  390.6 60.9 %while.81 = (s32[]{:T(128)}, f32[8,128,128]{2,1,0:T(8,128)S(1)}, f32[6,8,64,128]{3,2,0,1:T(8,128)}, f32[6,8,128,128]{3,2,1,0:T(8,128)}, f32[6,8,64,128]{3,2,1,0:...) while((s32[]{:T(128)}, f32[8,128,128]{2,1,0:T(8,128)S(1)}, ...), condition=%wide.region_21.23_spmd.clone, body=%wide.region_20.22_spmd.clone.sunk | while | flops 403906560 | bytes 11993254 | solution.py:76
  466.6 7.3 fusion.373
  473.9 7.0 fusion.374
  480.9 10.3 multiply_convert_fusion.1
  491.2 6.7 fusion.377
  497.9 6.6 multiply_reduce_fusion.5
  509.1 7.2 fusion.376
  516.3 7.1 multiply_convert_fusion
  547.6 155.1 %while.83 = (s32[]{:T(128)}, f32[8,128,128]{2,1,0:T(8,128)S(1)}, f32[6,8,64,128]{3,2,0,1:T(8,128)}, f32[6,8,64,128]{3,2,0,1:T(8,128)}, f32[6,8,64,128]{3,2,0,1:T...) while((s32[]{:T(128)}, f32[8,128,128]{2,1,0:T(8,128)S(1)}, ...), condition=%wide.region_39.41_spmd.clone, body=%wide.region_36.40_spmd.clone.sunk | while | flops 1084833280 | bytes 36946636 | solution.py:76
  706.8 160.2 %while.82 = (s32[]{:T(128)}, f32[8,128,128]{2,1,0:T(8,128)S(1)}, f32[6,8,64,128]{3,2,0,1:T(8,128)}, f32[6,8,64,128]{3,2,0,1:T(8,128)}, f32[6,8,64,128]{3,2,0,1:T...) while((s32[]{:T(128)}, f32[8,128,128]{2,1,0:T(8,128)S(1)}, ...), condition=%wide.region_29.31_spmd.clone, body=%wide.region_26.30_spmd.clone.sunk | while | flops 1084833280 | bytes 36946636 | solution.py:76
  869.5 6.3 multiply_reduce_fusion.25
  900.0 6.8 multiply_reduce_fusion.9
  964.5 6.2 convolution_add_fusion.69
  977.3 7.2 convolution_add_fusion.68
  1012.1 41.5 %all-reduce.66 = (f32[1024]{0:T(1024)S(1)}, f32[128]{0:T(128)S(1)}, f32[1024]{0:T(1024)S(1)}) all-reduce(f32[1024]{0:T(1024)S(1)} %add.1025, f32[128]{0:T(128)S(1)} %add.1033, f32[1024]{0:T(1024)S(1)} %add.1035), channel_id=2, replica_groups=mesh['fsdp'=32] {'fsdp'}, use_global_device_ids=true, to_apply=%region_46.48.clone | all-reduce | flops 2176 | bytes 17408
  1073.9 91.1 %reduce-scatter.38.cloned.1.call-done = f32[32,4]{1,0:T(8,128)} async-done(((f32[1024,4]{1,0:T(8,128)}), f32[32,4]{1,0:T(8,128)}) %reduce-scatter.38.cloned.1.call-update) | async-done | bytes 528
  1166.4 130.4 %reduce-scatter.40.cloned.1.call-done = f32[32,4]{1,0:T(8,128)} async-done(((f32[1024,4]{1,0:T(8,128)}), f32[32,4]{1,0:T(8,128)}) %reduce-scatter.40.cloned.1.call-update) | async-done | bytes 528
  1298.2 130.6 %reduce-scatter.34.cloned.1.call-done = f32[32,8]{1,0:T(8,128)} async-done(((f32[1024,8]{1,0:T(8,128)}), f32[32,8]{1,0:T(8,128)}) %reduce-scatter.34.cloned.1.call-update) | async-done | bytes 1040
  1437.7 130.5 %reduce-scatter.20.cloned.1.call-done = f32[32,1024]{1,0:T(8,128)} async-done(((f32[1024,1024]{1,0:T(8,128)}), f32[32,1024]{1,0:T(8,128)}) %reduce-scatter.20.cloned.1.call-update) | async-done | bytes 131088 | tf_op jit(solution)/shard_map/reduce_scatter | solution.py:416
  1568.2 139.5 %reduce-scatter.22.cloned.1.call-done = f32[32,1024]{1,0:T(8,128)} async-done(((f32[1024,1024]{1,0:T(8,128)}), f32[32,1024]{1,0:T(8,128)}) %reduce-scatter.22.cloned.1.call-update) | async-done | bytes 131088 | tf_op jit(solution)/shard_map/reduce_scatter | solution.py:417
  1707.7 139.4 %reduce-scatter.24.cloned.1.call-done = f32[32,1024]{1,0:T(8,128)} async-done(((f32[1024,1024]{1,0:T(8,128)}), f32[32,1024]{1,0:T(8,128)}) %reduce-scatter.24.cloned.1.call-update) | async-done | bytes 131088 | tf_op jit(solution)/shard_map/reduce_scatter | solution.py:418
  1847.1 139.6 %reduce-scatter.26.cloned.1.call-done = f32[1024,32]{0,1:T(8,128)} async-done(((f32[1024,1024]{0,1:T(8,128)}), f32[1024,32]{0,1:T(8,128)}) %reduce-scatter.26.cloned.1.call-update) | async-done | bytes 131088 | tf_op jit(solution)/shard_map/reduce_scatter | solution.py:424
  1986.8 153.5 %reduce-scatter.28.cloned.1.call-done = f32[32,2816]{1,0:T(8,128)} async-done(((f32[1024,2816]{1,0:T(8,128)}), f32[32,2816]{1,0:T(8,128)}) %reduce-scatter.28.cloned.1.call-update) | async-done | bytes 360464 | tf_op jit(solution)/shard_map/reduce_scatter | solution.py:426
  2140.3 153.6 %reduce-scatter.30.cloned.1.call-done = f32[32,2816]{1,0:T(8,128)} async-done(((f32[1024,2816]{1,0:T(8,128)}), f32[32,2816]{1,0:T(8,128)}) %reduce-scatter.30.cloned.1.call-update) | async-done | bytes 360464 | tf_op jit(solution)/shard_map/reduce_scatter | solution.py:427
  2293.8 153.6 %reduce-scatter.32.cloned.1.call-done = f32[2816,32]{0,1:T(8,128)} async-done(((f32[2816,1024]{0,1:T(8,128)}), f32[2816,32]{0,1:T(8,128)}) %reduce-scatter.32.cloned.1.call-update) | async-done | bytes 360464 | tf_op jit(solution)/shard_map/reduce_scatter | solution.py:428
  (1685 shorter events, 724.6 us)
Async XLA Ops:
  7.2 264.3 %all-gather.12.cloned.1.call-start = ((), (), s32[]{:S(2)}) async-start(), calls=%async_computation.15 | async-start | bytes 2162688 | tf_op jit(solution)/shard_map/all_gather | solution.py:343
  7.9 277.4 %all-gather.14.cloned.1.call-start = ((), (), s32[]{:S(2)}) async-start(), calls=%async_computation.16 | async-start | bytes 2162688 | tf_op jit(solution)/shard_map/all_gather | solution.py:344
  8.7 285.9 %all-gather.16.cloned.1.call-start = ((), (), s32[]{:S(2)}) async-start(), calls=%async_computation.17 | async-start | bytes 2162688 | tf_op jit(solution)/shard_map/all_gather | solution.py:342
  9.4 451.6 %all-gather.18.cloned.1.call-start = ((), (), s32[]{:S(2)}) async-start(), calls=%async_computation.18 | async-start | bytes 2162688 | tf_op jit(solution)/shard_map/all_gather | solution.py:350
  10.0 456.6 %all-gather.20.cloned.1.call-start = ((), (), s32[]{:S(2)}) async-start(), calls=%async_computation.19 | async-start | bytes 5947392 | tf_op jit(solution)/shard_map/all_gather | solution.py:352
  10.6 463.3 %all-gather.22.cloned.1.call-start = ((), (), s32[]{:S(2)}) async-start(), calls=%async_computation.20 | async-start | bytes 5947392 | tf_op jit(solution)/shard_map/all_gather | solution.py:353
  23.4 140.9 %all-to-all-start = ((bf16[32,12,1024]{2,1,0:T(8,128)(2,1)}), bf16[32,12,1024]{2,1,0:T(8,128)(2,1)S(1)}, u32[]{:S(2)}, u32[]{:S(2)}) async-start(bf16[32,12,1024]{2,1,0:T(8,128)(2,1)} %reshape.957), calls=%async_computation | async-start | bytes 2097152 | tf_op jit(solution)/shard_map/all_to_all | solution.py:328
  30.8 450.1 %all-gather.24.cloned.1.call-start = ((), (), s32[]{:S(2)}) async-start(), calls=%async_computation.21 | async-start | bytes 5947392 | tf_op jit(solution)/shard_map/all_gather | solution.py:354
  34.4 51.4 %copy-start.161 = (bf16[4,32]{1,0:T(4,128)(2,1)S(1)}, bf16[4,32]{1,0:T(4,128)(2,1)}, u32[]{:S(2)}) copy-start(bf16[4,32]{1,0:T(4,128)(2,1)} %param.39) | copy-start | bytes 772
  34.4 89.4 %copy-start.162 = (bf16[4,32]{1,0:T(4,128)(2,1)S(1)}, bf16[4,32]{1,0:T(4,128)(2,1)}, u32[]{:S(2)}) copy-start(bf16[4,32]{1,0:T(4,128)(2,1)} %param.37) | copy-start | bytes 772
  35.7 133.5 %copy-start.173 = (bf16[32]{0:T(256)(128)(2,1)S(1)}, bf16[32]{0:T(256)(128)(2,1)}, u32[]{:S(2)}) copy-start(bf16[32]{0:T(256)(128)(2,1)} %param.32) | copy-start | bytes 196
  35.7 133.7 %copy-start.174 = (bf16[32]{0:T(256)(128)(2,1)S(1)}, bf16[32]{0:T(256)(128)(2,1)}, u32[]{:S(2)}) copy-start(bf16[32]{0:T(256)(128)(2,1)} %param.42) | copy-start | bytes 196
  35.7 134.0 %copy-start.175 = (bf16[4]{0:T(256)(128)(2,1)S(1)}, bf16[4]{0:T(256)(128)(2,1)}, u32[]{:S(2)}) copy-start(bf16[4]{0:T(256)(128)(2,1)} %param.40) | copy-start | bytes 28
  35.7 184.3 %copy-start.159 = (bf16[32,8]{0,1:T(8,128)(2,1)S(1)}, bf16[32,8]{0,1:T(8,128)(2,1)}, u32[]{:S(2)}) copy-start(bf16[32,8]{0,1:T(8,128)(2,1)} %param.36) | copy-start | bytes 1540
  164.4 100.6 %all-to-all-start.1 = ((bf16[32,12,1024]{2,1,0:T(8,128)(2,1)}), bf16[32,12,1024]{2,1,0:T(8,128)(2,1)}, u32[]{:S(2)}, u32[]{:S(2)}) async-start(bf16[32,12,1024]{2,1,0:T(8,128)(2,1)} %reshape.969), calls=%async_computation.1 | async-start | bytes 2097152 | tf_op jit(solution)/shard_map/all_to_all | solution.py:328
  167.8 904.8 %reduce-scatter.36.cloned.1.call-start = ((), (), s32[]{:S(2)}) async-start(), calls=%async_computation.30 | async-start | bytes 540672
  220.0 77.4 %copy-start.90 = (f32[1024]{0:T(1024)}, f32[1024]{0:T(1024)S(1)}, u32[]{:S(2)}) copy-start(f32[1024]{0:T(1024)S(1)} %convert_element_type.207) | copy-start | bytes 12292
  706.8 160.3 %copy-start.32 = (f32[48,8,8,128]{3,2,1,0:T(8,128)S(1)}, f32[48,8,8,128]{3,2,1,0:T(8,128)}, u32[]{:S(2)}) copy-start(f32[48,8,8,128]{3,2,1,0:T(8,128)} %get-tuple-element.1529) | copy-start | bytes 4718596
  706.8 162.3 %copy-start.120 = (f32[384,8]{0,1:T(8,128)S(1)}, f32[384,8]{0,1:T(8,128)}, u32[]{:S(2)}) copy-start(f32[384,8]{0,1:T(8,128)} %copy-done.119) | copy-start | bytes 36868
  899.9 265.1 %reduce-scatter.38.cloned.1.call-start = ((), (), s32[]{:S(2)}) async-start(), calls=%async_computation.31 | async-start | bytes 540672
  910.3 386.5 %reduce-scatter.40.cloned.1.call-start = ((), (), s32[]{:S(2)}) async-start(), calls=%async_computation.32 | async-start | bytes 540672
  911.4 517.3 %reduce-scatter.34.cloned.1.call-start = ((), (), s32[]{:S(2)}) async-start(), calls=%async_computation.29 | async-start | bytes 540672
  912.9 655.3 %reduce-scatter.20.cloned.1.call-start = ((), (), s32[]{:S(2)}) async-start(), calls=%async_computation.22 | async-start | bytes 4325376 | tf_op jit(solution)/shard_map/reduce_scatter | solution.py:416
  919.0 788.7 %reduce-scatter.22.cloned.1.call-start = ((), (), s32[]{:S(2)}) async-start(), calls=%async_computation.23 | async-start | bytes 4325376 | tf_op jit(solution)/shard_map/reduce_scatter | solution.py:417
  929.0 918.1 %reduce-scatter.24.cloned.1.call-start = ((), (), s32[]{:S(2)}) async-start(), calls=%async_computation.24 | async-start | bytes 4325376 | tf_op jit(solution)/shard_map/reduce_scatter | solution.py:418
  939.8 1047.0 %reduce-scatter.26.cloned.1.call-start = ((), (), s32[]{:S(2)}) async-start(), calls=%async_computation.25 | async-start | bytes 4325376 | tf_op jit(solution)/shard_map/reduce_scatter | solution.py:424
  947.1 1193.1 %reduce-scatter.28.cloned.1.call-start = ((), (), s32[]{:S(2)}) async-start(), calls=%async_computation.26 | async-start | bytes 11894784 | tf_op jit(solution)/shard_map/reduce_scatter | solution.py:426
  959.5 1334.3 %reduce-scatter.30.cloned.1.call-start = ((), (), s32[]{:S(2)}) async-start(), calls=%async_computation.27 | async-start | bytes 11894784 | tf_op jit(solution)/shard_map/reduce_scatter | solution.py:427
  970.8 1476.6 %reduce-scatter.32.cloned.1.call-start = ((), (), s32[]{:S(2)}) async-start(), calls=%async_computation.28 | async-start | bytes 11894784 | tf_op jit(solution)/shard_map/reduce_scatter | solution.py:428
  1002.4 53.0 %all-to-all-start.3 = ((bf16[32,12,1024]{2,1,0:T(8,128)(2,1)}), bf16[32,12,1024]{2,1,0:T(8,128)(2,1)S(1)}, u32[]{:S(2)}, u32[]{:S(2)}) async-start(bf16[32,12,1024]{2,1,0:T(8,128)(2,1)} %reshape.1001), calls=%async_computation.3 | async-start | bytes 2097152 | tf_op jit(solution)/shard_map/all_to_all | solution.py:387
  1009.8 50.6 %copy-start.67 = (bf16[384,2816]{1,0:T(8,128)(2,1)S(1)}, bf16[384,2816]{1,0:T(8,128)(2,1)}, u32[]{:S(2)}) copy-start(bf16[384,2816]{1,0:T(8,128)(2,1)} %get-tuple-element.1506) | copy-start | bytes 6488068
  1055.4 377.3 %all-to-all-start.2 = ((bf16[32,12,1024]{2,1,0:T(8,128)(2,1)}), bf16[32,12,1024]{2,1,0:T(8,128)(2,1)}, u32[]{:S(2)}, u32[]{:S(2)}) async-start(bf16[32,12,1024]{2,1,0:T(8,128)(2,1)} %reshape.990), calls=%async_computation.2 | async-start | bytes 2097152 | tf_op jit(solution)/shard_map/all_to_all | solution.py:387
  (170 other events, 888.3 us)
Sparse Core Ops, SparseCore 0:
  10.9 61.6 all-gather.11
  75.4 55.3 all-gather.13
  133.6 60.0 all-gather.15
  196.5 55.3 all-gather.17
  254.5 66.0 all-gather.19
  323.4 66.1 all-gather.21
  392.4 66.3 all-gather.23
  900.1 131.1 reduce-scatter.35
  1033.6 131.3 reduce-scatter.37
  1167.1 129.6 reduce-scatter.39
  1299.1 129.5 reduce-scatter.33
  1431.4 136.7 reduce-scatter.19
  1571.1 136.6 reduce-scatter.21
  1710.4 136.6 reduce-scatter.23
  1849.8 136.8 reduce-scatter.25
  1989.5 150.7 reduce-scatter.27
  2143.0 150.7 reduce-scatter.29
  2296.6 150.7 reduce-scatter.31
where the time goes:
time: 2470 us; the launch traced here: 2450 us
  waiting for transfers between devices  1370 us (55%)
  matrix products  528 us (21%)
  blocking collectives  257 us (10%)
  local copies, waits for them, and re-layouts  152 us (6%)
  other arithmetic  106 us (4%)
    unnamed x22, waiting for transfers between devices  357 us
    reduce_scatter x1, waiting for transfers between devices, local(): lax.psum_scatter(grad_d, 'fsdp', scatter_dimension=1, tiled=True)  154 us
    reduce_scatter x1, waiting for transfers between devices, local(): lax.psum_scatter(grad_u, 'fsdp', scatter_dimension=0, tiled=True)  154 us
    reduce_scatter x1, waiting for transfers between devices, local(): lax.psum_scatter(grad_g, 'fsdp', scatter_dimension=0, tiled=True)  154 us
    reduce_scatter x1, waiting for transfers between devices, local(): lax.psum_scatter(grad_o, 'fsdp', scatter_dimension=1, tiled=True)  140 us
    reduce_scatter x1, waiting for transfers between devices, local(): lax.psum_scatter(grad_k, 'fsdp', scatter_dimension=0, tiled=True)  140 us
    reduce_scatter x1, waiting for transfers between devices, local(): lax.psum_scatter(grad_v, 'fsdp', scatter_dimension=0, tiled=True)  139 us
    reduce_scatter x1, waiting for transfers between devices, local(): lax.psum_scatter(grad_q, 'fsdp', scatter_dimension=0, tiled=True)  131 us
  transfers between devices with their start and end apart: 22, of which 10 were waited for; matrix products, arithmetic and copies ran while one was open for 15% of the time, Pallas kernels for 0%

commit v1 on v0

v1 whole, which is shorter than its diff:
```python
import functools
import math

import jax
import jax.numpy as jnp
from jax import lax
from jax.experimental import pallas as pl
from jax.experimental.pallas import tpu as pltpu
from jax.sharding import PartitionSpec as P

HEADS = 8
HEAD = 128
SPAN = 128
NORM_EPS = 1e-05
UNIT_EPS = 1e-06
MESH = pl.DeviceIdType.MESH
F32, BF16 = jnp.float32, jnp.bfloat16
VMEM_LIMIT = 61440 * 1024
FFW = 256
Z, Y, X, C = 0, 1, 2, 3

ROW_CONV, ROW_ATTN, ROW_MLP, ROW_OUT, ROW_BETA, SMALL_ROWS = 0, 12, 13, 14, 16, 32


def grid_of(n):
    chips = n // 2
    a = 4 if chips % 4 == 0 else 1
    rest = chips // a
    b = 1
    while b * b < rest:
        b *= 2
    return (a, b, rest // b, 2)


def coords_of(dims, index):
    out = []
    for size in reversed(dims):
        out.append(lax.rem(index, size))
        index = index // size
    return out[::-1]


def index_of(dims, cs):
    total = 0
    for size, c in zip(dims, cs):
        total = total * size + c
    return total


def along(dims, cs, axis, delta):
    moved = list(cs)
    moved[axis] = lax.rem(cs[axis] + delta + dims[axis], dims[axis])
    return moved


def greet_all(n, me):
    barrier = pltpu.get_barrier_semaphore()

    def hello(d, carry):
        pl.semaphore_signal(
            barrier, inc=1, device_id=(lax.rem(me + d, n),), device_id_type=MESH
        )
        return carry

    lax.fori_loop(1, n, hello, 0)
    pl.semaphore_wait(barrier, n - 1)


def greet_axes(dims, cs):
    barrier = pltpu.get_barrier_semaphore()
    count = 0
    for axis in range(4):
        for delta in range(1, dims[axis]):
            to = index_of(dims, along(dims, cs, axis, delta))
            pl.semaphore_signal(barrier, inc=1, device_id=(to,), device_id_type=MESH)
            count += 1
    pl.semaphore_wait(barrier, count)


def hops(dims):
    return sum(d - 1 for d in dims)


class Gather:
    def __init__(self, dims, cs, shard, out, low, width, order, sems):
        self.dims, self.cs, self.order = dims, cs, order
        self.columns = pl.ds(low, width)
        self.shard, self.out = shard.at[:, self.columns], out
        self.send, self.recv, self.local = sems

    def slot(self, stage, delta):
        return sum(self.dims[a] - 1 for a in self.order[:stage]) + delta - 1

    def region(self, stage, cs):
        done = self.order[:stage]
        lead = tuple(slice(None) if k in done else cs[k] for k in range(4))
        return self.out.at[lead + (slice(None), self.columns)]

    def copies(self, stage, incoming):
        axis = self.order[stage]
        for delta in range(1, self.dims[axis]):
            frm = along(self.dims, self.cs, axis, -delta) if incoming else self.cs
            to = along(self.dims, self.cs, axis, delta)
            k = self.slot(stage, delta)
            yield pltpu.make_async_remote_copy(
                src_ref=self.shard if stage == 0 else self.region(stage, self.cs),
                dst_ref=self.region(stage, frm),
                send_sem=self.send.at[k],
                recv_sem=self.recv.at[k],
                device_id=(index_of(self.dims, to),),
                device_id_type=MESH,
            )

    def keep(self):
        return pltpu.make_async_copy(self.shard, self.region(0, self.cs), self.local)

    def step(self, stage):
        if stage == 0:
            self.keep().start()
        if stage == 1:
            self.keep().wait()
        if stage >= 1:
            for c in self.copies(stage - 1, True):
                c.wait_recv()
        if stage < 4:
            for c in self.copies(stage, False):
                c.start()

    def finish(self):
        for stage in range(4):
            for c in self.copies(stage, False):
                c.wait_send()


ZXY, ZYX, XYZ, YXZ = (Z, X, Y, C), (Z, Y, X, C), (X, Y, Z, C), (Y, X, Z, C)


def pipelined(jobs, stages, lag):
    for tick in range(len(jobs) + (stages - 1) * lag):
        for stage in range(stages):
            i = tick - stage * lag
            if 0 <= i < len(jobs):
                jobs[i].step(stage)


class Tokens:
    def __init__(self, n, me, a, b, send, recv, local):
        self.n, self.me, self.a, self.b = n, me, a, b
        self.send, self.recv, self.local = send, recv, local

    def copy(self, d, incoming):
        to = lax.rem(self.me + d, self.n)
        frm = lax.rem(self.me - d + self.n, self.n)
        return pltpu.make_async_remote_copy(
            src_ref=self.a.at[to],
            dst_ref=self.b.at[frm if incoming else self.me],
            send_sem=self.send.at[d],
            recv_sem=self.recv.at[d],
            device_id=(to,),
            device_id_type=MESH,
        )

    def keep(self):
        return pltpu.make_async_copy(self.a.at[self.me], self.b.at[self.me], self.local)

    def each(self, act):
        def body(d, carry):
            act(d)
            return carry

        lax.fori_loop(1, self.n, body, 0)

    def start(self):
        self.keep().start()
        self.each(lambda d: self.copy(d, False).start())

    def wait(self):
        self.keep().wait()
        self.each(lambda d: self.copy(d, True).wait_recv())
        self.each(lambda d: self.copy(d, False).wait_send())


def gather_kernel(dims, plan, lag, count, with_tokens, *refs):
    n = math.prod(dims)
    t = 1 if with_tokens else 0
    ins, outs, scr = refs[: count + t], refs[count + t : 2 * (count + t)], refs[2 * (count + t) :]
    send, recv, local = scr[:3]
    me = lax.axis_index("fsdp")
    cs = coords_of(dims, me)
    if with_tokens:
        greet_all(n, me)
        tokens = Tokens(n, me, ins[count], outs[count], *scr[3:])
        tokens.start()
    else:
        greet_axes(dims, cs)
    jobs = [
        Gather(dims, cs, ins[a], outs[a], low, width, order, (send.at[i], recv.at[i], local.at[i]))
        for i, (a, low, width, order) in enumerate(plan)
    ]
    pipelined(jobs, 5, lag)
    for j in jobs:
        j.finish()
    if with_tokens:
        tokens.wait()


def any_spec():
    return pl.BlockSpec(memory_space=pl.ANY)


def vmem_spec():
    return pl.BlockSpec(memory_space=pltpu.VMEM)


def token_sems(n):
    return [
        pltpu.SemaphoreType.DMA((n,)),
        pltpu.SemaphoreType.DMA((n,)),
        pltpu.SemaphoreType.DMA,
    ]


def gather_call(shards, tokens, plan, lag, collective_id):
    n = lax.axis_size("fsdp")
    dims = grid_of(n)
    k = hops(dims)
    ins = list(shards) + ([] if tokens is None else [tokens])
    outs = [jax.ShapeDtypeStruct(dims + s.shape, s.dtype) for s in shards]
    if tokens is not None:
        outs.append(jax.ShapeDtypeStruct(tokens.shape, tokens.dtype))
    m = len(plan)
    return pl.pallas_call(
        functools.partial(gather_kernel, dims, plan, lag, len(shards), tokens is not None),
        out_shape=outs,
        in_specs=[any_spec()] * len(ins),
        out_specs=[any_spec()] * len(outs),
        scratch_shapes=[
            pltpu.SemaphoreType.DMA((m, k)),
            pltpu.SemaphoreType.DMA((m, k)),
            pltpu.SemaphoreType.DMA((m,)),
        ]
        + ([] if tokens is None else token_sems(n)),
        compiler_params=pltpu.CompilerParams(
            collective_id=collective_id, has_side_effects=True, vmem_limit_bytes=VMEM_LIMIT
        ),
    )(*ins)


class Scatter:
    def __init__(self, dims, cs, terms, result, low, width, order, scratch, sems):
        self.dims, self.cs, self.order = dims, cs, order
        self.columns = pl.ds(low, width)
        self.terms, self.result = terms, result
        self.own, self.got = scratch[0], scratch[1:]
        self.send, self.recv, self.local = sems

    def slot(self, stage, delta):
        return sum(self.dims[a] - 1 for a in self.order[:stage]) + delta - 1

    def part(self, stage, at):
        axis = self.order[stage]
        if stage == 0:
            lead = tuple(at if k == axis else slice(None) for k in range(4))
            return self.terms.at[lead + (slice(None), self.columns)]
        left = [k for k in range(4) if k not in self.order[:stage]]
        return self.got[stage - 1].at[(0,) + tuple(at if k == axis else slice(None) for k in left)]

    def copies(self, stage):
        axis = self.order[stage]
        for delta in range(1, self.dims[axis]):
            to = along(self.dims, self.cs, axis, delta)
            k = self.slot(stage, delta)
            yield pltpu.make_async_remote_copy(
                src_ref=self.part(stage, to[axis]),
                dst_ref=self.got[stage].at[delta - 1],
                send_sem=self.send.at[k],
                recv_sem=self.recv.at[k],
                device_id=(index_of(self.dims, to),),
                device_id_type=MESH,
            )

    def keep(self):
        return pltpu.make_async_copy(self.part(0, self.cs[self.order[0]]), self.own, self.local)

    def total(self, stage):
        axis = self.order[stage]
        left = [k for k in range(4) if k not in self.order[: stage + 1]]
        shape = [self.dims[k] for k in left]
        got = self.got[stage]
        mine = self.own if stage == 0 else self.part(stage, self.cs[axis])

        def one(i, carry):
            at = tuple(coords_of(shape, i)) if shape else ()
            total = mine[at + (slice(None), slice(None))].astype(F32)
            for delta in range(1, self.dims[axis]):
                total += got[(delta - 1,) + at + (slice(None), slice(None))].astype(F32)
            if left:
                got[(0,) + at + (slice(None), slice(None))] = total.astype(got.dtype)
            else:
                self.result[:, self.columns] = total
            return carry

        lax.fori_loop(0, math.prod(shape), one, 0)

    def step(self, stage):
        if stage == 0:
            self.keep().start()
        if stage == 1:
            self.keep().wait()
        if stage >= 1:
            for c in self.copies(stage - 1):
                c.wait_recv()
            self.total(stage - 1)
        if stage < 4:
            for c in self.copies(stage):
                c.start()

    def finish(self):
        for stage in range(4):
            for c in self.copies(stage):
                c.wait_send()


CXYZ, CYXZ = (C, X, Y, Z), (C, Y, X, Z)


def scatter_scratch(dims, rows, width, order, dtype):
    left = list(dims)
    out = [pltpu.VMEM(tuple(d for k, d in enumerate(dims) if k != order[0]) + (rows, width), dtype)]
    for s, axis in enumerate(order):
        rest = tuple(dims[k] for k in range(4) if k not in order[: s + 1])
        out.append(pltpu.VMEM((dims[axis] - 1,) + rest + (rows, width), dtype))
    return out


def scatter_kernel(dims, plan, lag, count, with_tokens, *refs):
    n = math.prod(dims)
    t = 1 if with_tokens else 0
    ins, outs, scr = refs[: count + t], refs[count + t : 2 * (count + t)], refs[2 * (count + t) :]
    send, recv, local = scr[:3]
    scr = scr[3:]
    me = lax.axis_index("fsdp")
    cs = coords_of(dims, me)
    if with_tokens:
        greet_all(n, me)
        tokens = Tokens(n, me, ins[count], outs[count], *scr[:3])
        tokens.start()
        scr = scr[3:]
    else:
        greet_axes(dims, cs)
    jobs = [
        Scatter(
            dims, cs, ins[a], outs[a], low, width, order, scr[5 * i : 5 * i + 5],
            (send.at[i], recv.at[i], local.at[i]),
        )
        for i, (a, low, width, order) in enumerate(plan)
    ]
    pipelined(jobs, 5, lag)
    for j in jobs:
        j.finish()
    if with_tokens:
        tokens.wait()


def scatter_call(terms, tokens, plan, lag, collective_id):
    n = lax.axis_size("fsdp")
    dims = grid_of(n)
    k = hops(dims)
    ins = list(terms) + ([] if tokens is None else [tokens])
    outs = [jax.ShapeDtypeStruct(s.shape[4:], F32) for s in terms]
    out_specs = [vmem_spec()] * len(terms)
    if tokens is not None:
        outs.append(jax.ShapeDtypeStruct(tokens.shape, tokens.dtype))
        out_specs.append(any_spec())
    m = len(plan)
    scratch = []
    for a, low, width, order in plan:
        scratch += scatter_scratch(dims, terms[a].shape[4], width, order, terms[a].dtype)
    return pl.pallas_call(
        functools.partial(scatter_kernel, dims, plan, lag, len(terms), tokens is not None),
        out_shape=outs,
        in_specs=[any_spec()] * len(ins),
        out_specs=out_specs,
        scratch_shapes=[
            pltpu.SemaphoreType.DMA((m, k)),
            pltpu.SemaphoreType.DMA((m, k)),
            pltpu.SemaphoreType.DMA((m,)),
        ]
        + ([] if tokens is None else token_sems(n))
        + scratch,
        compiler_params=pltpu.CompilerParams(
            collective_id=collective_id, has_side_effects=True, vmem_limit_bytes=VMEM_LIMIT
        ),
    )(*ins)


def dot(a, b):
    return lax.dot_general(a, b, (((1,), (0,)), ((), ())), preferred_element_type=F32)


def dot_nt(a, b):
    return lax.dot_general(a, b, (((1,), (1,)), ((), ())), preferred_element_type=F32)


def dot_tn(a, b):
    return lax.dot_general(a, b, (((0,), (0,)), ((), ())), preferred_element_type=F32)


def low(v):
    return v.astype(BF16)


def lanes(i, width=HEAD):
    return slice(i * width, (i + 1) * width)


def shifted(values, by, row):
    if by == 0:
        return values
    rows = values.shape[0]
    moved = pltpu.roll(values, by % rows, 0)
    return jnp.where(row >= by if by > 0 else row < rows + by, moved, 0.0)


def conv(values, taps, row):
    total = values * taps[0:1]
    for c in range(1, taps.shape[0]):
        total += shifted(values, c, row) * taps[c : c + 1]
    return total


def head_sum(values):
    return jnp.sum(values, axis=-1, keepdims=True)


def iotas(shape):
    return lax.broadcasted_iota(jnp.int32, shape, 0), lax.broadcasted_iota(jnp.int32, shape, 1)


def level_masks():
    i, j = iotas((SPAN, SPAN))
    found = []
    for level in range(SPAN.bit_length() - 1):
        a, b = i >> level, j >> level
        found.append(((a >> 1) == (b >> 1)) & ((a & 1) == 1) & ((b & 1) == 0))
    return found


def project(own, small, weights, attn_low, pre, queries, keys, values, beta, micro, length):
    width = own.shape[1]
    row = lax.broadcasted_iota(jnp.int32, (length, 2 * HEAD), 0)
    gain = small[ROW_ATTN : ROW_ATTN + 1, :]
    beta_rows = low(small[ROW_BETA : ROW_BETA + 16, :])

    def one(m, carry):
        rows = pl.ds(m * length, length)
        v = own[rows, :].astype(F32)
        r = lax.rsqrt(jnp.mean(v * v, axis=-1, keepdims=True) + NORM_EPS)
        attn_low[rows, :] = low(v * r * gain)
        a = attn_low[rows, :]
        beta[rows, :] = jax.nn.sigmoid(dot_nt(a, beta_rows))
        for kind, out in enumerate((queries, keys, values)):
            for b in range(width // (2 * HEAD)):
                cols = lanes(b, 2 * HEAD)
                wide = slice(kind * width + cols.start, kind * width + cols.stop)
                x = dot(a, weights[:, wide])
                pre[rows, wide] = low(x)
                c = conv(x, small[4 * kind : 4 * kind + 4, cols], row)
                u = c * jax.nn.sigmoid(c)
                if kind == 2:
                    out[rows, cols] = low(u)
                    continue
                for h in range(2):
                    part = u[:, lanes(h)]
                    n = lax.rsqrt(head_sum(part * part) + UNIT_EPS)
                    out[rows, slice(cols.start + h * HEAD, cols.start + (h + 1) * HEAD)] = low(part * n)
        return carry

    lax.fori_loop(0, micro, one, 0)


def delta_block(base, first, refs, gain):
    queries, keys, values, beta, state, states, inverses, scores, fresh, mix, mixed, at = refs
    rows = pl.ds(base, SPAN)
    i, j = iotas((SPAN, SPAN))
    masks = level_masks()
    eye = jnp.where(i == j, 1.0, 0.0).astype(F32)
    heads = range(HEADS)

    @pl.when(first)
    def _():
        state[...] = jnp.zeros_like(state)

    strength = beta[rows, :]
    k = [keys[rows, lanes(h)] for h in heads]
    q = [queries[rows, lanes(h)] for h in heads]
    b = [strength[:, h : h + 1] for h in heads]
    strict = [low(jnp.where(i > j, dot_nt(k[h], k[h]) * b[h], 0.0)) for h in heads]
    for h in heads:
        scores[at, h] = low(jnp.where(i >= j, dot_nt(q[h], k[h]), 0.0))
    zero = jnp.zeros((), BF16)
    inv = [eye - jnp.where(masks[0], strict[h], zero).astype(F32) for h in heads]
    for level in range(1, len(masks)):
        t = [low(inv[h]) for h in heads]
        f = [low(dot(jnp.where(masks[level], strict[h], zero), t[h])) for h in heads]
        inv = [inv[h] - dot(t[h], f[h]) for h in heads]
    for h in heads:
        inverses[at, h] = low(inv[h])
    s = [low(state[h]) for h in heads]
    for h in heads:
        states[at, h] = s[h]
    rest = [low((values[rows, lanes(h)].astype(F32) - dot(k[h], s[h])) * b[h]) for h in heads]
    new = [low(dot(inverses[at, h], rest[h])) for h in heads]
    out = [dot(q[h], s[h]) + dot(scores[at, h], new[h]) for h in heads]
    for h in heads:
        fresh[rows, lanes(h)] = new[h]
        state[h] += dot_tn(k[h], new[h])
        r = lax.rsqrt(jnp.mean(out[h] * out[h], axis=-1, keepdims=True) + NORM_EPS)
        mix[rows, lanes(h)] = low(out[h])
        mixed[rows, lanes(h)] = low(out[h] * r * gain)


def forward_kernel(micro, length, *refs):
    (own, small, weights, out_weight, hidden, attn_low, pre, queries, keys, values, beta,
     states, inverses, scores, fresh, mix, mixed, state) = refs
    project(own, small, weights, attn_low, pre, queries, keys, values, beta, micro, length)
    gain = small[ROW_OUT : ROW_OUT + 1, :HEAD]
    blocks = length // SPAN

    def one(t, carry):
        delta_block(
            pl.multiple_of(t * SPAN, SPAN), lax.rem(t, blocks) == 0,
            (queries, keys, values, beta, state, states, inverses, scores, fresh, mix, mixed, t), gain,
        )
        rows = pl.ds(pl.multiple_of(t * SPAN, SPAN), SPAN)
        hidden[rows, :] = own[rows, :].astype(F32) + dot_nt(mixed[rows, :], out_weight[...])
        return carry

    lax.fori_loop(0, micro * blocks, one, 0)


def forward_call(own, small, weights, out_weight, micro):
    rows, width = own.shape
    length = rows // micro
    blocks = rows // SPAN
    square = jax.ShapeDtypeStruct((blocks, HEADS, SPAN, SPAN), BF16)
    wide = jax.ShapeDtypeStruct((rows, width), BF16)
    outs = [
        jax.ShapeDtypeStruct((rows, width), F32), wide, jax.ShapeDtypeStruct((rows, 3 * width), BF16),
        wide, wide, wide, jax.ShapeDtypeStruct((rows, 16), F32),
        jax.ShapeDtypeStruct((blocks, HEADS, HEAD, HEAD), BF16), square, square, wide, wide, wide,
    ]
    return pl.pallas_call(
        functools.partial(forward_kernel, micro, length),
        out_shape=outs,
        in_specs=[vmem_spec()] * 4,
        out_specs=[vmem_spec()] * len(outs),
        scratch_shapes=[pltpu.VMEM((HEADS, HEAD, HEAD), F32)],
        compiler_params=pltpu.CompilerParams(vmem_limit_bytes=VMEM_LIMIT),
    )(own, small, weights, out_weight)


def feed_kernel(steps, hidden, grad, small, active, w_ref, result, terms, d_hidden, gain_grad, norm, total, d_norm):
    t = pl.program_id(0)
    gain = small[ROW_MLP : ROW_MLP + 1, :]

    @pl.when(t == 0)
    def _():
        v = hidden[...]
        r = lax.rsqrt(jnp.mean(v * v, axis=-1, keepdims=True) + NORM_EPS)
        norm[...] = low(v * r * gain)
        total[...] = v
        d_norm[...] = jnp.zeros_like(d_norm)

    x, g = norm[...], grad[...]
    gw, uw, dw = (w_ref[:, lanes(i, FFW)] for i in range(3))
    gate, up = dot(x, gw), dot(x, uw)
    d_act = dot(g, dw)
    s = jax.nn.sigmoid(gate)
    silu = gate * s
    act = low(silu * up)
    d_gate = low(d_act * up * (s + silu * (1.0 - s)))
    d_up = low(d_act * silu)
    total[...] += dot_nt(act, dw)
    d_norm[...] += dot_nt(d_gate, gw) + dot_nt(d_up, uw)
    terms[:, lanes(0, FFW)] = low(dot_tn(x, d_gate))
    terms[:, lanes(1, FFW)] = low(dot_tn(x, d_up))
    terms[:, lanes(2, FFW)] = low(dot_tn(g, act))

    @pl.when(t == steps - 1)
    def _():
        result[...] = low(jnp.where(active[...] > 0.0, total[...], 0.0))
        v, d = hidden[...], d_norm[...]
        n = v.shape[1]
        r = lax.rsqrt(jnp.mean(v * v, axis=-1, keepdims=True) + NORM_EPS)
        vr = v * r
        gain_grad[...] = jnp.sum(d * vr, axis=0, keepdims=True)
        gd = d * gain
        d_hidden[...] = g.astype(F32) + r * (gd - vr * (jnp.sum(vr * gd, axis=-1, keepdims=True) / n))


def feed_call(hidden, grad, small, active, weights):
    rows, width = hidden.shape
    steps = weights.shape[1] // (3 * FFW)
    whole = lambda *shape: pl.BlockSpec(shape, lambda t: (0,) * len(shape))
    block = pl.BlockSpec((width, 3 * FFW), lambda t: (0, t))
    return pl.pallas_call(
        functools.partial(feed_kernel, steps),
        grid=(steps,),
        out_shape=[
            jax.ShapeDtypeStruct((rows, width), BF16),
            jax.ShapeDtypeStruct(weights.shape, BF16),
            jax.ShapeDtypeStruct((rows, width), F32),
            jax.ShapeDtypeStruct((1, width), F32),
        ],
        in_specs=[whole(rows, width), whole(rows, width), whole(*small.shape), whole(rows, 1), block],
        out_specs=[whole(rows, width), block, whole(rows, width), whole(1, width)],
        scratch_shapes=[
            pltpu.VMEM((rows, width), BF16),
            pltpu.VMEM((rows, width), F32),
            pltpu.VMEM((rows, width), F32),
        ],
        compiler_params=pltpu.CompilerParams(
            vmem_limit_bytes=VMEM_LIMIT, dimension_semantics=("arbitrary",)
        ),
    )(hidden, grad, small, active, weights)


def delta_back(base, last, refs, gain):
    (queries, keys, values, beta, states, inverses, scores, fresh, mix, d_mixed,
     d_state, d_out, d_q, d_k, d_v, d_beta, gain_grad, at) = refs
    rows = pl.ds(base, SPAN)
    i, j = iotas((SPAN, SPAN))
    lane = lax.broadcasted_iota(jnp.int32, (SPAN, 16), 1)
    heads = range(HEADS)

    @pl.when(last)
    def _():
        d_state[...] = jnp.zeros_like(d_state)

    strength = beta[rows, :]
    k = [keys[rows, lanes(h)] for h in heads]
    q = [queries[rows, lanes(h)] for h in heads]
    e = [fresh[rows, lanes(h)] for h in heads]
    b = [strength[:, h : h + 1] for h in heads]
    kb = [low(k[h].astype(F32) * b[h]) for h in heads]
    do = []
    for h in heads:
        v, d = mix[rows, lanes(h)].astype(F32), d_mixed[:, lanes(h)]
        r = lax.rsqrt(jnp.mean(v * v, axis=-1, keepdims=True) + NORM_EPS)
        vr, gd = v * r, d * gain
        gain_grad[...] += jnp.sum(d * vr, axis=0, keepdims=True)
        do.append(low(r * (gd - vr * jnp.mean(vr * gd, axis=-1, keepdims=True))))
    s = [states[at, h] for h in heads]
    p = [scores[at, h] for h in heads]
    ds = [low(d_state[h]) for h in heads]
    de = [low(dot_tn(p[h], do[h]) + dot(k[h], ds[h])) for h in heads]
    dx = [dot_tn(inverses[at, h], de[h]) for h in heads]
    dxl = [low(dx[h]) for h in heads]
    dp = [low(jnp.where(i >= j, dot_nt(do[h], e[h]), 0.0)) for h in heads]
    da = [low(jnp.where(i > j, -dot_nt(dxl[h], e[h]), 0.0)) for h in heads]
    dkb = [dot(da[h], k[h]) - dot_nt(dxl[h], s[h]) for h in heads]
    beta_grad = jnp.zeros((SPAN, 16), F32)
    for h in heads:
        d_q[rows, lanes(h)] = low(dot_nt(do[h], s[h]) + dot(dp[h], k[h]))
        d_k[rows, lanes(h)] = low(
            dkb[h] * b[h] + dot_tn(da[h], kb[h]) + dot_tn(dp[h], q[h]) + dot_nt(e[h], ds[h])
        )
        d_v[rows, lanes(h)] = low(dx[h] * b[h])
        d_state[h] += dot_tn(q[h], do[h]) - dot_tn(kb[h], dxl[h])
        db = head_sum(dkb[h] * k[h].astype(F32) + dx[h] * values[rows, lanes(h)].astype(F32))
        beta_grad += jnp.where(lane == h, db, 0.0)
    d_beta[rows, :] = low(beta_grad * strength * (1.0 - strength))


def backward_kernel(micro, length, *refs):
    (d_hidden, own, small, weights, out_weight, attn_low, pre, queries, keys, values, beta,
     states, inverses, scores, fresh, mix, mixed,
     d_own, qkv_grad, out_grad, small_grad,
     d_state, d_out, d_q, d_k, d_v, d_beta, d_pre, d_attn, gain_grad) = refs
    width = own.shape[1]
    blocks = length // SPAN
    total = micro * blocks
    gain = small[ROW_OUT : ROW_OUT + 1, :HEAD]
    gain_grad[...] = jnp.zeros_like(gain_grad)
    small_grad[...] = jnp.zeros_like(small_grad)
    d_attn[...] = low(d_hidden[...])

    def one(step, carry):
        t = total - 1 - step
        base = pl.multiple_of(t * SPAN, SPAN)
        d_out[...] = dot(d_attn[pl.ds(base, SPAN), :], out_weight[...])
        delta_back(
            base, lax.rem(step, blocks) == 0,
            (queries, keys, values, beta, states, inverses, scores, fresh, mix, d_out,
             d_state, None, d_q, d_k, d_v, d_beta, gain_grad, t), gain,
        )
        return carry

    lax.fori_loop(0, total, one, 0)
    row = lax.broadcasted_iota(jnp.int32, (length, HEAD), 0)

    def conv_back(m, carry):
        rows = pl.ds(m * length, length)
        for kind, grads in enumerate((d_q, d_k, d_v)):
            for h in range(width // HEAD):
                cols = lanes(h)
                wide = slice(kind * width + cols.start, kind * width + cols.stop)
                taps = small[4 * kind : 4 * kind + 4, cols]
                x = pre[rows, wide].astype(F32)
                moved = [shifted(x, c, row) for c in range(4)]
                c = moved[0] * taps[0:1]
                for o in range(1, 4):
                    c += moved[o] * taps[o : o + 1]
                s = jax.nn.sigmoid(c)
                u = c * s
                d = grads[rows, cols].astype(F32)
                if kind < 2:
                    n = lax.rsqrt(head_sum(u * u) + UNIT_EPS)
                    un = u * n
                    d = (d - un * head_sum(un * d)) * n
                d = d * (s + u * (1.0 - s))
                for o in range(4):
                    at = slice(4 * kind + o, 4 * kind + o + 1)
                    small_grad[at, cols] += jnp.sum(moved[o] * d, axis=0, keepdims=True)
                back = d * taps[0:1]
                for o in range(1, 4):
                    back += shifted(d, -o, row) * taps[o : o + 1]
                d_pre[rows, wide] = low(back)
        return carry

    lax.fori_loop(0, micro, conv_back, 0)
    for b in range(width // 256):
        cols = lanes(b, 256)
        out_grad[:, cols] = low(dot_tn(d_attn[...], mixed[:, cols]))
    for b in range(3 * width // 256):
        cols = lanes(b, 256)
        qkv_grad[:, cols] = low(dot_tn(attn_low[...], d_pre[:, cols]))
    beta_rows = low(small[ROW_BETA : ROW_BETA + 16, :])
    small_grad[ROW_BETA : ROW_BETA + 16, :] = dot_tn(d_beta[...], attn_low[...])
    small_grad[ROW_OUT : ROW_OUT + 1, :HEAD] = gain_grad[...]
    attn_gain = small[ROW_ATTN : ROW_ATTN + 1, :]

    def finish(t, carry):
        rows = pl.ds(pl.multiple_of(t * SPAN, SPAN), SPAN)
        d = dot_nt(d_pre[rows, :], weights[...]) + dot(d_beta[rows, :], beta_rows)
        v = own[rows, :].astype(F32)
        r = lax.rsqrt(jnp.mean(v * v, axis=-1, keepdims=True) + NORM_EPS)
        vr, gd = v * r, d * attn_gain
        small_grad[ROW_ATTN : ROW_ATTN + 1, :] += jnp.sum(d * vr, axis=0, keepdims=True)
        d_own[rows, :] = low(d_hidden[rows, :] + r * (gd - vr * jnp.mean(vr * gd, axis=-1, keepdims=True)))
        return carry

    lax.fori_loop(0, total, finish, 0)


def backward_call(d_hidden, own, small, weights, out_weight, saved, micro):
    rows, width = own.shape
    length = rows // micro
    return pl.pallas_call(
        functools.partial(backward_kernel, micro, length),
        out_shape=[
            jax.ShapeDtypeStruct((rows, width), BF16),
            jax.ShapeDtypeStruct((width, 3 * width), BF16),
            jax.ShapeDtypeStruct((width, width), BF16),
            jax.ShapeDtypeStruct((SMALL_ROWS, width), F32),
        ],
        in_specs=[vmem_spec()] * (5 + len(saved)),
        out_specs=[vmem_spec()] * 4,
        scratch_shapes=[
            pltpu.VMEM((HEADS, HEAD, HEAD), F32),
            pltpu.VMEM((SPAN, width), F32),
            pltpu.VMEM((rows, width), BF16),
            pltpu.VMEM((rows, width), BF16),
            pltpu.VMEM((rows, width), BF16),
            pltpu.VMEM((rows, 16), BF16),
            pltpu.VMEM((rows, 3 * width), BF16),
            pltpu.VMEM((rows, width), BF16),
            pltpu.VMEM((1, HEAD), F32),
        ],
        compiler_params=pltpu.CompilerParams(vmem_limit_bytes=VMEM_LIMIT),
    )(d_hidden, own, small, weights, out_weight, *saved)


def picked(index, source):
    hot = index[:, None] == jnp.arange(source.shape[0], dtype=jnp.int32)[None, :]
    return jnp.dot(low(hot), source, preferred_element_type=F32).astype(BF16)


def split_rows(values, parts):
    cut = values.reshape(values.shape[:-1] + (parts, values.shape[-1] // parts))
    return jnp.moveaxis(cut, -2, 0)


def spans(width, size):
    at = 0
    while at < width:
        yield at, min(size, width - at)
        at += size


def local(
    inputs, cotangent, lengths, owners, attn_gain, query_weight, key_weight, value_weight, beta_weight,
    query_conv, key_conv, value_conv, out_gain, out_weight, mlp_gain, gate_weight, up_weight, down_weight,
):
    n = lax.axis_size("fsdp")
    dims = grid_of(n)
    me = lax.axis_index("fsdp")
    micro, _, length, width = inputs.shape
    hidden_units = gate_weight.shape[1]
    share = width // n
    slots = length // n
    per = micro * slots
    parts = 16 // math.gcd(per, 16)
    thin = width // parts
    i32 = jnp.int32
    devices = jnp.arange(n, dtype=i32)
    slot_ids = jnp.arange(slots, dtype=i32)
    row_ids = jnp.arange(length, dtype=i32)
    micros = jnp.arange(micro, dtype=i32)
    part_ids = jnp.arange(parts, dtype=i32)

    before = devices[:, None] < devices[None, :]
    starts = jnp.sum(jnp.where(before[None], lengths[:, :, None], 0), axis=1)
    match = owners[:, None, :] == devices[None, :, None]
    own_start = jnp.sum(jnp.where(match, starts[:, None, :], 0), axis=2)
    own_len = jnp.sum(jnp.where(match, lengths[:, None, :], 0), axis=2)
    mine = devices == me
    my_start = jnp.sum(jnp.where(mine, own_start, 0), axis=1)
    my_len = jnp.sum(jnp.where(mine, own_len, 0), axis=1)

    first = own_start + (me - own_start) % n
    pos = first[:, :, None] + n * slot_ids
    live = pos < (own_start + own_len)[:, :, None]
    send = jnp.where(live, micros[:, None, None] * length + pos // n, -1)
    send = jnp.moveaxis(send, 0, 1)[:, None] + jnp.zeros((1, parts, 1, 1), i32)
    send = jnp.where(send >= 0, send + (part_ids * micro * length)[None, :, None, None], -1)
    rows_in = split_rows(inputs[:, 0].reshape(micro * length, width), parts).reshape(-1, thin)
    outgoing = picked(send.reshape(-1), rows_in).reshape(n, parts * per, thin)

    def row_of(v):
        return jnp.pad(v, ((0, 0), (0, share - v.shape[1])))

    packed = jnp.concatenate([
        query_conv, key_conv, value_conv, attn_gain[None], mlp_gain[None], row_of(out_gain[None]),
        jnp.zeros((1, share), BF16), beta_weight.T, jnp.zeros((SMALL_ROWS - 16 - HEADS, share), BF16),
    ])
    count = SMALL_ROWS * share // HEAD
    packed = jnp.pad(packed.reshape(count, HEAD), ((0, -count % 16), (0, 0)))

    attn_shard = jnp.concatenate([query_weight, key_weight, value_weight, out_weight.T], axis=1)
    steps = hidden_units // FFW
    feed_shard = jnp.stack(
        [w.reshape(share, steps, FFW) for w in (gate_weight, up_weight, down_weight.T)], axis=2
    ).reshape(share, 3 * hidden_units)

    plan = [(0, 0, HEAD, ZXY)]
    for a, (w, size) in enumerate(((4 * width, 512), (3 * hidden_units, 768)), 1):
        for at, wide in spans(w, size):
            plan.append((a, at, wide, (ZXY, ZYX)[len(plan) % 2]))
    small_all, attn_all, feed_all, incoming = gather_call(
        [packed, attn_shard, feed_shard], outgoing, tuple(plan), 2, 1
    )
    small = small_all.reshape(n, -1)[:, : SMALL_ROWS * share].reshape(n, SMALL_ROWS, share)
    small = jnp.moveaxis(small, 1, 0)
    gain_row = small[ROW_OUT, :, : HEAD // n].reshape(1, HEAD)
    small = small.reshape(SMALL_ROWS, width).astype(F32)
    small = lax.dynamic_update_slice(small, gain_row.astype(F32), (ROW_OUT, 0))
    attn_all = attn_all.reshape(width, 4 * width)
    feed_all = feed_all.reshape(width, 3 * hidden_units)
    qkv, out_t = attn_all[:, : 3 * width], attn_all[:, 3 * width :]

    active = row_ids[None] < my_len[:, None]
    block = (my_start[:, None] + row_ids) % n
    at = block * (parts * per) + micros[:, None] * slots + row_ids // n
    take = jnp.where(active, at, -1).reshape(-1)
    flat = incoming.reshape(n * parts * per, thin)
    own = jnp.concatenate(
        [picked(jnp.where(take >= 0, take + p * per, -1), flat) for p in range(parts)], axis=1
    )
    active = active.reshape(-1, 1)
    grad = jnp.where(active, cotangent[:, 0].reshape(-1, width), jnp.zeros((), BF16))

    hidden, *saved = forward_call(own, small, qkv, out_t, micro)
    result, feed_terms, d_hidden, mlp_gain_grad = feed_call(
        hidden, grad, small, active.astype(F32), feed_all
    )
    d_own, qkv_terms, out_terms, small_terms = backward_call(
        d_hidden, own, small, qkv, out_t, saved, micro
    )

    back = slot_ids * n + (devices[:, None, None] - my_start[None, :, None]) % n
    back = jnp.where(back < my_len[None, :, None], back + (micros * length)[None, :, None], -1)
    back = back[:, None] + jnp.zeros((1, parts, 1, 1), i32)
    back = jnp.where(back >= 0, back + (part_ids * micro * length)[None, :, None, None], -1)
    returning = picked(back.reshape(-1), split_rows(d_own, parts).reshape(-1, thin))
    returning = returning.reshape(n, parts * per, thin)

    small_terms = lax.dynamic_update_slice(small_terms, mlp_gain_grad, (ROW_MLP, 0))
    out_gain_terms = jnp.pad(small_terms[ROW_OUT, :HEAD].reshape(n, -1), ((0, 0), (0, share - HEAD // n)))
    small_terms = jnp.concatenate(
        [small_terms[:ROW_OUT].reshape(ROW_OUT, n, share), out_gain_terms[None],
         small_terms[ROW_OUT + 1 :].reshape(SMALL_ROWS - ROW_OUT - 1, n, share)]
    )
    small_terms = jnp.moveaxis(small_terms, 1, 0).reshape(n, count, HEAD)
    small_terms = jnp.pad(small_terms, ((0, 0), (0, -count % 16), (0, 0)))
    terms = [
        small_terms.reshape(dims + small_terms.shape[1:]),
        qkv_terms.reshape(dims + (share, 3 * width)),
        out_terms.reshape(dims + (share, width)),
        feed_terms.reshape(dims + (share, 3 * hidden_units)),
    ]
    plan = []
    for a, size in ((3, 768), (2, 512), (1, 512), (0, HEAD)):
        for lo, wide in spans(terms[a].shape[5], size):
            plan.append((a, lo, wide, (CXYZ, CYXZ)[len(plan) % 2]))
    small_grad, qkv_grad, out_grad, feed_grad, returned = scatter_call(
        terms, returning, tuple(plan), 2, 2
    )

    place = row_ids * n + me
    inside = (place[None, :, None] >= own_start[:, None, :]) & (
        place[None, :, None] < (own_start + own_len)[:, None, :]
    )
    at = devices * (parts * per) + micros[:, None, None] * slots + (place[None, :, None] - first[:, None, :]) // n
    take = (jnp.sum(jnp.where(inside, at + 1, 0), axis=2) - 1).reshape(-1)
    flat = returned.reshape(n * parts * per, thin)
    input_rows = jnp.concatenate(
        [picked(jnp.where(take >= 0, take + p * per, -1), flat) for p in range(parts)], axis=1
    )

    small_grad = small_grad.reshape(-1)[: SMALL_ROWS * share].reshape(SMALL_ROWS, share)
    feed_grad = feed_grad.reshape(share, steps, 3, FFW)
    gate_grad, up_grad, down_grad = (
        feed_grad[:, :, i].reshape(share, hidden_units) for i in range(3)
    )
    return (
        result.reshape(micro, 1, length, width),
        input_rows.reshape(micro, 1, length, width),
        small_grad[ROW_ATTN],
        qkv_grad[:, :width],
        qkv_grad[:, width : 2 * width],
        qkv_grad[:, 2 * width :],
        small_grad[ROW_BETA : ROW_BETA + HEADS].T,
        small_grad[0:4],
        small_grad[4:8],
        small_grad[8:12],
        small_grad[ROW_OUT, : HEAD // n],
        out_grad.T,
        small_grad[ROW_MLP],
        gate_grad,
        up_grad,
        down_grad.T,
    )


def solution(mesh):
    rows, cols, flat = P("fsdp", None), P(None, "fsdp"), P("fsdp")
    data = P(None, "fsdp", None, None)
    return jax.shard_map(
        local,
        mesh=mesh,
        in_specs=(
            data, data, P(), P(), flat, rows, rows, rows, rows, cols, cols, cols, flat, cols, flat, rows, rows, cols,
        ),
        out_specs=(
            data, data, flat, rows, rows, rows, rows, cols, cols, cols, flat, cols, flat, rows, rows, cols,
        ),
        check_vma=False,
    )
```

time: 2470 us -> 543 us (0.22)
  waiting for transfers between devices: 1370 us -> 0 us
  matrix products: 528 us -> 15.6 us
  Pallas kernels: 0 us -> 471 us
  blocking collectives: 257 us -> 0 us
  local copies, waits for them, and re-layouts: 152 us -> 38.8 us
  other arithmetic: 106 us -> 7.45 us
    reduce_scatter x7 -> x0, waiting for transfers between devices: 1010 us -> none  [the longest x1 154 us: local(): lax.psum_scatter(grad_d, 'fsdp', scatter_dimension=1, tiled=True)]
    dot_general x876 -> x6, matrix products: 528 us -> 15.6 us  [picked(): return jnp.dot(low(hot), source, preferred_element_type=F32).astype(BF16)]
    pallas_call x0 -> x5, Pallas kernels: none -> 471 us  [the longest x1 163 us: gather_call(): pl.pallas_call(functools.partial(gather_kernel, dims, plan, lag, len(shar...]
    unnamed x22 -> x0, waiting for transfers between devices: 357 us -> none
    all_gather x4 -> x0, blocking collectives: 166 us -> none  [the longest x1 50 us: local(): lax.all_gather(key_conv, 'fsdp', axis=1, tiled=True)]
    unnamed x2 -> x0, blocking collectives: 91.5 us -> none
    squeeze x61 -> x2, local copies, waits for them, and re-layouts: 54.6 us -> 1.03 us  [the longest x1 0.52 us: local(): small_grad[ROW_OUT, :HEAD // n]]
    reduce_sum x34 -> x4, other arithmetic: 39.9 us -> 1.93 us  [the longest x1 0.84 us: local(): own_start = jnp.sum(jnp.where(match, starts[:, None, :], 0), axis=2)]
  transfers between devices with their start and end apart: 22 -> 0, of which waited for: 10 -> 0; matrix products, arithmetic and copies ran while one was open for 15% -> 0% of each run, Pallas kernels for 0% -> 0%
where the time goes in v1:
time: 543 us; the launch traced here: 534 us
  Pallas kernels  471 us (87%)
  local copies, waits for them, and re-layouts  38.8 us (7%)
  matrix products  15.6 us (3%)
  other arithmetic  7.45 us (1%)
    pallas_call x1, Pallas kernels, gather_call(): pl.pallas_call(functools.partial(gather_kernel, dims, plan, lag, len(shar...  163 us
    pallas_call x1, Pallas kernels, scatter_call(): pl.pallas_call(functools.partial(scatter_kernel, dims, plan, lag, len(ter...  144 us
    pallas_call x1, Pallas kernels, backward_call(): pl.pallas_call(functools.partial(backward_kernel, micro, length), out_sha...  68.6 us
    pallas_call x1, Pallas kernels, feed_call(): pl.pallas_call(functools.partial(feed_kernel, steps), grid=(steps,), out_...  52.2 us
    pallas_call x1, Pallas kernels, forward_call(): pl.pallas_call(functools.partial(forward_kernel, micro, length), out_shap...  43.6 us
    dot_general x6, matrix products, picked(): return jnp.dot(low(hot), source, preferred_element_type=F32).astype(BF16)  15.6 us

profile of v1, /device:TPU:0, one launch (start us, length us, event | category | flops | bytes accessed | tf_op | source)
XLA Modules:
  0.0 534.4 jit_solution(12413049213479156956)
XLA Ops:
  2.4 0.8 select_reduce_fusion
  3.9 2.1 concatenate.15
  7.6 1.7 pad_maximum_fusion.3.refs_1_
  9.3 1.0 stack_reshape.9
  11.3 1.4 reshape.508.refs_2_
  12.7 0.9 copy.89
  13.6 1.4 bitcast_select_fusion.grad
  15.5 1.2 reshape_reshape_squeeze.3
  16.9 4.0 fusion.9
  20.9 162.7 %shard_map.297 = (bf16[4,2,2,2,16,128]{5,4,3,2,1,0:T(8,128)(2,1)}, bf16[4,2,2,2,32,4096]{5,4,3,2,1,0:T(8,128)(2,1)}, bf16[4,2,2,2,32,8448]{5,4,3,2,1,0:T(8,128)(2,1)}, bf16[32,48,512]{2,1,0:T(8,128)(2,1)}) custom-call(bf16[16,128]{1,0:T(8,128)(2,1)} %pad.17.refs_0_, bf16[32,4096]{1,0:T(8,128)(2,1)} %pad_maximum_fusion.3.refs_1_, ...), custom_call_target="tpu_custom_call" | custom-call | tf_op jit(solution)/shard_map/pallas_call | solution.py:232
  183.6 1.1 copy.96
  185.9 1.4 fusion.16
  187.4 1.4 fusion.17
  188.8 1.4 pad_maximum_fusion.refs_0_.refs_1_
  190.2 1.5 slice.108.refs_3_.refs_4_
  191.7 3.1 slice.107.refs_2_.refs_3_
  194.7 43.6 %shard_map.298 = (f32[768,1024]{1,0:T(8,128)}, bf16[768,1024]{1,0:T(8,128)(2,1)}, bf16[768,3072]{1,0:T(8,128)(2,1)}, bf16[768,1024]{1,0:T(8,128)(2,1)}, bf16[768...) custom-call(bf16[768,1024]{1,0:T(8,128)(2,1)} %pad_maximum_fusion.re, ...), custom_call_target="tpu_custom_call" | custom-call | tf_op jit(solution)/shard_map/pallas_call | solution.py:553
  238.3 52.2 %shard_map.299 = (bf16[768,1024]{1,0:T(8,128)(2,1)}, bf16[1024,8448]{1,0:T(8,128)(2,1)}, f32[768,1024]{1,0:T(8,128)}, f32[1,1024]{1,0:T(1,128)}) custom-call(f32[768,1024]{1,0:T(8,128)} %get-tuple-element.49.hidden, bf16[768,1024]{1,0:T(8,128)(2,1)} %bitcast_select_fusion.grad, f32[32,1024]{1,0:T(8,128)} %copy-done, f32[768,1]{1,0:T(8,128)} %bitcast.96, ...), custom_call_target="tpu_custom_call" | custom-call | tf_op jit(solution)/shard_map/pallas_call | solution.py:607
  290.5 68.6 %shard_map.300 = (bf16[768,1024]{1,0:T(8,128)(2,1)}, bf16[1024,3072]{1,0:T(8,128)(2,1)}, bf16[1024,1024]{1,0:T(8,128)(2,1)}, f32[32,1024]{1,0:T(8,128)}) custom-call(f32[768,1024]{1,0:T(8,128)} %get-tuple-element.52.refs_0_, bf16[768,1024]{1,0:T(8,128)(2,1)} %pad_maximum_fusion.refs_0_.refs_1_, f32[32,1024]{1,0:T(8,128)} %copy-done, ...), custom_call_target="tpu_custom_call" | custom-call | tf_op jit(solution)/shard_map/pallas_call | solution.py:760
  359.1 1.4 dynamic_update_slice.7
  361.4 0.8 slice.109
  362.2 0.9 slice.111
  364.9 4.0 fusion.8
  368.9 143.8 %shard_map.301 = (f32[16,128]{1,0:T(8,128)}, f32[32,3072]{1,0:T(8,128)}, f32[32,1024]{1,0:T(8,128)}, f32[32,8448]{1,0:T(8,128)}, bf16[32,48,512]{2,1,0:T(8,128)(2,1)}) custom-call(f32[4,2,2,2,16,128]{5,4,3,2,1,0:T(8,128)} %bitcast.99, bf16[4,2,2,2,32,3072]{5,4,3,2,1,0:T(8,128)(2,1)} %bitcast.86, bf16[4,2,2,2,32,1024]{5,4,3,2,1,0:T(8,128)(2,1)} %bitcast.90, ...), custom_call_target="tpu_custom_call" | custom-call | tf_op jit(solution)/shard_map/pallas_call | solution.py:379
  518.6 1.8 fusion.44
  520.4 3.2 fusion.14
  523.5 1.7 fusion.15
  525.3 1.6 copy.85
  527.6 2.8 slice_reduce_fusion
  530.4 0.9 copy.92
  531.4 0.9 copy.91
  532.3 0.9 copy.90
  (104 shorter events, 16.4 us)
Async XLA Ops:
  0.6 9.8 %copy-start.6 = (bf16[2816,32]{0,1:T(8,128)(2,1)S(1)}, bf16[2816,32]{0,1:T(8,128)(2,1)}, u32[]{:S(2)}) copy-start(bf16[2816,32]{0,1:T(8,128)(2,1)} %param.35) | copy-start | bytes 540676
  0.7 9.7 %copy-start.5 = (bf16[32,2816]{1,0:T(8,128)(2,1)S(1)}, bf16[32,2816]{1,0:T(8,128)(2,1)}, u32[]{:S(2)}) copy-start(bf16[32,2816]{1,0:T(8,128)(2,1)} %param.34) | copy-start | bytes 540676
  10.8 2.9 copy-start.1
  13.6 1.8 copy-start.2
  183.6 2.3 copy-start.10
  185.9 1.5 copy-start
  185.9 4.3 slice-start
  187.4 2.8 slice-start.1
  290.5 68.7 %copy-start.8 = (f32[1,1024]{1,0:T(1,128)S(1)}, f32[1,1024]{1,0:T(1,128)}, u32[]{:S(2)}) copy-start(f32[1,1024]{1,0:T(1,128)} %get-tuple-element.66) | copy-start | bytes 12292
  363.4 1.4 copy-start.3
  520.4 3.2 copy-start.9
  525.3 1.6 copy-start.4
  530.4 2.9 copy-start.7

commit v2 on v1

--- a/solution.py
+++ b/solution.py
@@ -137,10 +137,24 @@
 
 def pipelined(jobs, stages, lag):
     for tick in range(len(jobs) + (stages - 1) * lag):
-        for stage in range(stages):
-            i = tick - stage * lag
-            if 0 <= i < len(jobs):
-                jobs[i].step(stage)
+        run_tick(jobs, stages, lag, tick)
+
+
+def run_tick(jobs, stages, lag, tick):
+    for stage in reversed(range(stages)):
+        i = tick - stage * lag
+        if 0 <= i < len(jobs):
+            jobs[i].step(stage)
+
+
+def loop_tick(make, count, stages, lag, tick):
+    for stage in reversed(range(stages)):
+        i = tick - stage * lag
+
+        @pl.when((i >= 0) & (i < count))
+        def _(i=i, stage=stage):
+            for job in make(i):
+                job.step(stage)
 
 
 class Tokens:
@@ -247,11 +261,11 @@
 
 
 class Scatter:
-    def __init__(self, dims, cs, terms, result, low, width, order, scratch, sems):
+    def __init__(self, dims, cs, terms, term_columns, result, columns, order, own, got, sems):
         self.dims, self.cs, self.order = dims, cs, order
-        self.columns = pl.ds(low, width)
+        self.term_columns, self.columns = term_columns, columns
         self.terms, self.result = terms, result
-        self.own, self.got = scratch[0], scratch[1:]
+        self.own, self.got = own, got
         self.send, self.recv, self.local = sems
 
     def slot(self, stage, delta):
@@ -261,7 +275,7 @@
         axis = self.order[stage]
         if stage == 0:
             lead = tuple(at if k == axis else slice(None) for k in range(4))
-            return self.terms.at[lead + (slice(None), self.columns)]
+            return self.terms.at[lead + (slice(None), self.term_columns)]
         left = [k for k in range(4) if k not in self.order[:stage]]
         return self.got[stage - 1].at[(0,) + tuple(at if k == axis else slice(None) for k in left)]
 
@@ -287,7 +301,8 @@
         left = [k for k in range(4) if k not in self.order[: stage + 1]]
         shape = [self.dims[k] for k in left]
         got = self.got[stage]
-        mine = self.own if stage == 0 else self.part(stage, self.cs[axis])
+        whole = stage or self.own is None
+        mine = self.part(stage, self.cs[axis]) if whole else self.own
 
         def one(i, carry):
             at = tuple(coords_of(shape, i)) if shape else ()
@@ -303,95 +318,32 @@
         lax.fori_loop(0, math.prod(shape), one, 0)
 
     def step(self, stage):
-        if stage == 0:
-            self.keep().start()
-        if stage == 1:
-            self.keep().wait()
+        if self.own is not None:
+            if stage == 0:
+                self.keep().start()
+            if stage == 1:
+                self.keep().wait()
         if stage >= 1:
             for c in self.copies(stage - 1):
-                c.wait_recv()
+                c.wait()
             self.total(stage - 1)
         if stage < 4:
             for c in self.copies(stage):
                 c.start()
 
-    def finish(self):
-        for stage in range(4):
-            for c in self.copies(stage):
-                c.wait_send()
-
 
 CXYZ, CYXZ = (C, X, Y, Z), (C, Y, X, Z)
 
 
-def scatter_scratch(dims, rows, width, order, dtype):
-    left = list(dims)
-    out = [pltpu.VMEM(tuple(d for k, d in enumerate(dims) if k != order[0]) + (rows, width), dtype)]
+def scatter_scratch(dims, rows, width, order, dtype, lead=(), keep=True):
+    out = []
+    if keep:
+        rest = tuple(d for k, d in enumerate(dims) if k != order[0])
+        out.append(pltpu.VMEM(lead + rest + (rows, width), dtype))
     for s, axis in enumerate(order):
         rest = tuple(dims[k] for k in range(4) if k not in order[: s + 1])
-        out.append(pltpu.VMEM((dims[axis] - 1,) + rest + (rows, width), dtype))
+        out.append(pltpu.VMEM(lead + (dims[axis] - 1,) + rest + (rows, width), dtype))
     return out
-
-
-def scatter_kernel(dims, plan, lag, count, with_tokens, *refs):
-    n = math.prod(dims)
-    t = 1 if with_tokens else 0
-    ins, outs, scr = refs[: count + t], refs[count + t : 2 * (count + t)], refs[2 * (count + t) :]
-    send, recv, local = scr[:3]
-    scr = scr[3:]
-    me = lax.axis_index("fsdp")
-    cs = coords_of(dims, me)
-    if with_tokens:
-        greet_all(n, me)
-        tokens = Tokens(n, me, ins[count], outs[count], *scr[:3])
-        tokens.start()
-        scr = scr[3:]
-    else:
-        greet_axes(dims, cs)
-    jobs = [
-        Scatter(
-            dims, cs, ins[a], outs[a], low, width, order, scr[5 * i : 5 * i + 5],
-            (send.at[i], recv.at[i], local.at[i]),
-        )
-        for i, (a, low, width, order) in enumerate(plan)
-    ]
-    pipelined(jobs, 5, lag)
-    for j in jobs:
-        j.finish()
-    if with_tokens:
-        tokens.wait()
-
-
-def scatter_call(terms, tokens, plan, lag, collective_id):
-    n = lax.axis_size("fsdp")
-    dims = grid_of(n)
-    k = hops(dims)
-    ins = list(terms) + ([] if tokens is None else [tokens])
-    outs = [jax.ShapeDtypeStruct(s.shape[4:], F32) for s in terms]
-    out_specs = [vmem_spec()] * len(terms)
-    if tokens is not None:
-        outs.append(jax.ShapeDtypeStruct(tokens.shape, tokens.dtype))
-        out_specs.append(any_spec())
-    m = len(plan)
-    scratch = []
-    for a, low, width, order in plan:
-        scratch += scatter_scratch(dims, terms[a].shape[4], width, order, terms[a].dtype)
-    return pl.pallas_call(
-        functools.partial(scatter_kernel, dims, plan, lag, len(terms), tokens is not None),
-        out_shape=outs,
-        in_specs=[any_spec()] * len(ins),
-        out_specs=out_specs,
-        scratch_shapes=[
-            pltpu.SemaphoreType.DMA((m, k)),
-            pltpu.SemaphoreType.DMA((m, k)),
-            pltpu.SemaphoreType.DMA((m,)),
-        ]
-        + ([] if tokens is None else token_sems(n))
-        + scratch,
-        compiler_params=pltpu.CompilerParams(
-            collective_id=collective_id, has_side_effects=True, vmem_limit_bytes=VMEM_LIMIT
-        ),
-    )(*ins)
 
 
 def dot(a, b):
@@ -446,13 +398,14 @@
     return found
 
 
-def project(own, small, weights, attn_low, pre, queries, keys, values, beta, micro, length):
+def project(own, small, weights, attn_low, pre, queries, keys, values, beta, micro, length, tick):
     width = own.shape[1]
     row = lax.broadcasted_iota(jnp.int32, (length, 2 * HEAD), 0)
     gain = small[ROW_ATTN : ROW_ATTN + 1, :]
     beta_rows = low(small[ROW_BETA : ROW_BETA + 16, :])
 
     def one(m, carry):
+        tick(m + 1)
         rows = pl.ds(m * length, length)
         v = own[rows, :].astype(F32)
         r = lax.rsqrt(jnp.mean(v * v, axis=-1, keepdims=True) + NORM_EPS)
@@ -520,14 +473,38 @@
         mixed[rows, lanes(h)] = low(out[h] * r * gain)
 
 
-def forward_kernel(micro, length, *refs):
-    (own, small, weights, out_weight, hidden, attn_low, pre, queries, keys, values, beta,
-     states, inverses, scores, fresh, mix, mixed, state) = refs
-    project(own, small, weights, attn_low, pre, queries, keys, values, beta, micro, length)
+def square_rms(v):
+    return lax.rsqrt(jnp.mean(v * v, axis=-1, keepdims=True) + NORM_EPS)
+
+
+def forward_kernel(dims, micro, length, steps, *refs):
+    (own, small, weights, out_weight, grad, active, feed_shard,
+     result, d_hidden, d_attn, gain_grad, terms, feed, attn_low, pre, queries, keys, values, beta,
+     states, inverses, scores, fresh, mix, mixed,
+     state, hidden, norm, total, w_buf, t_buf, send, recv, local, w_sem, t_sem) = refs
+    me = lax.axis_index("fsdp")
+    cs = coords_of(dims, me)
+    greet_axes(dims, cs)
+    half = 3 * FFW // 2
+
+    def jobs(i):
+        for p, order in enumerate((ZXY, ZYX)):
+            at = pl.multiple_of(i * (3 * FFW) + p * half, half)
+            k = 2 * i + p
+            yield Gather(
+                dims, cs, feed_shard, feed, at, half, order, (send.at[k], recv.at[k], local.at[k])
+            )
+
+    def tick(t):
+        loop_tick(jobs, steps, 5, 2, t)
+
+    tick(0)
+    project(own, small, weights, attn_low, pre, queries, keys, values, beta, micro, length, tick)
     gain = small[ROW_OUT : ROW_OUT + 1, :HEAD]
     blocks = length // SPAN
 
     def one(t, carry):
+        tick(micro + 1 + t)
         delta_block(
             pl.multiple_of(t * SPAN, SPAN), lax.rem(t, blocks) == 0,
             (queries, keys, values, beta, state, states, inverses, scores, fresh, mix, mixed, t), gain,
@@ -537,43 +514,78 @@
         return carry
 
     lax.fori_loop(0, micro * blocks, one, 0)
-
-
-def forward_call(own, small, weights, out_weight, micro):
-    rows, width = own.shape
-    length = rows // micro
-    blocks = rows // SPAN
-    square = jax.ShapeDtypeStruct((blocks, HEADS, SPAN, SPAN), BF16)
-    wide = jax.ShapeDtypeStruct((rows, width), BF16)
-    outs = [
-        jax.ShapeDtypeStruct((rows, width), F32), wide, jax.ShapeDtypeStruct((rows, 3 * width), BF16),
-        wide, wide, wide, jax.ShapeDtypeStruct((rows, 16), F32),
-        jax.ShapeDtypeStruct((blocks, HEADS, HEAD, HEAD), BF16), square, square, wide, wide, wide,
-    ]
-    return pl.pallas_call(
-        functools.partial(forward_kernel, micro, length),
-        out_shape=outs,
-        in_specs=[vmem_spec()] * 4,
-        out_specs=[vmem_spec()] * len(outs),
-        scratch_shapes=[pltpu.VMEM((HEADS, HEAD, HEAD), F32)],
-        compiler_params=pltpu.CompilerParams(vmem_limit_bytes=VMEM_LIMIT),
-    )(own, small, weights, out_weight)
-
-
-def feed_kernel(steps, hidden, grad, small, active, w_ref, result, terms, d_hidden, gain_grad, norm, total, d_norm):
-    t = pl.program_id(0)
-    gain = small[ROW_MLP : ROW_MLP + 1, :]
-
-    @pl.when(t == 0)
-    def _():
-        v = hidden[...]
-        r = lax.rsqrt(jnp.mean(v * v, axis=-1, keepdims=True) + NORM_EPS)
-        norm[...] = low(v * r * gain)
-        total[...] = v
-        d_norm[...] = jnp.zeros_like(d_norm)
-
+    begun = micro + 1 + micro * blocks
+
+    def columns(t):
+        return pl.ds(pl.multiple_of(t * (3 * FFW), 3 * FFW), 3 * FFW)
+
+    def load(t):
+        slot = lax.rem(t, 2)
+        return pltpu.make_async_copy(
+            feed.at[:, :, :, :, :, columns(t)], w_buf.at[slot], w_sem.at[slot]
+        )
+
+    def store(t):
+        slot = lax.rem(t, 2)
+        return pltpu.make_async_copy(t_buf.at[slot], terms.at[:, columns(t)], t_sem.at[slot])
+
+    load(0).start()
+    gain_mlp = small[ROW_MLP : ROW_MLP + 1, :]
+    v = hidden[...]
+    norm[...] = low(v * square_rms(v) * gain_mlp)
+    total[...] = jnp.zeros_like(total)
+    d_hidden[...] = jnp.zeros_like(d_hidden)
+
+    def feed_step(t, carry):
+        tick(begun + t)
+
+        @pl.when(t + 1 < steps)
+        def _():
+            load(t + 1).start()
+
+        load(t).wait()
+
+        @pl.when(t >= 2)
+        def _():
+            store(t - 2).wait()
+
+        slot = lax.rem(t, 2)
+        w = w_buf[slot].reshape(norm.shape[1], 3 * FFW)
+        feed_part(w, norm, grad, total, d_hidden, t_buf.at[slot])
+        store(t).start()
+        return carry
+
+    lax.fori_loop(0, steps, feed_step, 0)
+    store(steps - 2).wait()
+    store(steps - 1).wait()
+    n = norm.shape[1]
+
+    def close(t, carry):
+        rows = pl.ds(pl.multiple_of(t * SPAN, SPAN), SPAN)
+        v, d = hidden[rows, :], d_hidden[rows, :]
+        result[rows, :] = low(jnp.where(active[rows, :] > 0.0, v + total[rows, :], 0.0))
+        r = square_rms(v)
+        vr, gd = v * r, d * gain_mlp
+        gain_grad[...] += jnp.sum(d * vr, axis=0, keepdims=True)
+        whole = grad[rows, :].astype(F32) + r * (gd - vr * jnp.mean(vr * gd, axis=-1, keepdims=True))
+        d_hidden[rows, :] = whole
+        d_attn[rows, :] = low(whole)
+        return carry
+
+    gain_grad[...] = jnp.zeros_like(gain_grad)
+    lax.fori_loop(0, micro * blocks, close, 0)
+
+    def finish(i, carry):
+        for job in jobs(i):
+            job.finish()
+        return carry
+
+    lax.fori_loop(0, steps, finish, 0)
+
+
+def feed_part(w, norm, grad, total, d_norm, terms):
     x, g = norm[...], grad[...]
-    gw, uw, dw = (w_ref[:, lanes(i, FFW)] for i in range(3))
+    gw, uw, dw = (w[:, lanes(i, FFW)] for i in range(3))
     gate, up = dot(x, gw), dot(x, uw)
     d_act = dot(g, dw)
     s = jax.nn.sigmoid(gate)
@@ -587,43 +599,47 @@
     terms[:, lanes(1, FFW)] = low(dot_tn(x, d_up))
     terms[:, lanes(2, FFW)] = low(dot_tn(g, act))
 
-    @pl.when(t == steps - 1)
-    def _():
-        result[...] = low(jnp.where(active[...] > 0.0, total[...], 0.0))
-        v, d = hidden[...], d_norm[...]
-        n = v.shape[1]
-        r = lax.rsqrt(jnp.mean(v * v, axis=-1, keepdims=True) + NORM_EPS)
-        vr = v * r
-        gain_grad[...] = jnp.sum(d * vr, axis=0, keepdims=True)
-        gd = d * gain
-        d_hidden[...] = g.astype(F32) + r * (gd - vr * (jnp.sum(vr * gd, axis=-1, keepdims=True) / n))
-
-
-def feed_call(hidden, grad, small, active, weights):
-    rows, width = hidden.shape
-    steps = weights.shape[1] // (3 * FFW)
-    whole = lambda *shape: pl.BlockSpec(shape, lambda t: (0,) * len(shape))
-    block = pl.BlockSpec((width, 3 * FFW), lambda t: (0, t))
+
+def forward_call(own, small, weights, out_weight, grad, active, feed_shard, micro, collective_id):
+    rows, width = own.shape
+    length = rows // micro
+    blocks = rows // SPAN
+    n = lax.axis_size("fsdp")
+    dims = grid_of(n)
+    k = hops(dims)
+    steps = feed_shard.shape[1] // (3 * FFW)
+    square = jax.ShapeDtypeStruct((blocks, HEADS, SPAN, SPAN), BF16)
+    wide = jax.ShapeDtypeStruct((rows, width), BF16)
+    outs = [
+        wide, jax.ShapeDtypeStruct((rows, width), F32), wide, jax.ShapeDtypeStruct((1, width), F32),
+        jax.ShapeDtypeStruct((width, feed_shard.shape[1]), BF16),
+        jax.ShapeDtypeStruct(dims + feed_shard.shape, BF16),
+        wide, jax.ShapeDtypeStruct((rows, 3 * width), BF16),
+        wide, wide, wide, jax.ShapeDtypeStruct((rows, 16), F32),
+        jax.ShapeDtypeStruct((blocks, HEADS, HEAD, HEAD), BF16), square, square, wide, wide, wide,
+    ]
     return pl.pallas_call(
-        functools.partial(feed_kernel, steps),
-        grid=(steps,),
-        out_shape=[
-            jax.ShapeDtypeStruct((rows, width), BF16),
-            jax.ShapeDtypeStruct(weights.shape, BF16),
-            jax.ShapeDtypeStruct((rows, width), F32),
-            jax.ShapeDtypeStruct((1, width), F32),
-        ],
-        in_specs=[whole(rows, width), whole(rows, width), whole(*small.shape), whole(rows, 1), block],
-        out_specs=[whole(rows, width), block, whole(rows, width), whole(1, width)],
+        functools.partial(forward_kernel, dims, micro, length, steps),
+        out_shape=outs,
+        in_specs=[vmem_spec()] * 6 + [any_spec()],
+        out_specs=[vmem_spec()] * 4 + [any_spec()] * 2 + [vmem_spec()] * (len(outs) - 6),
         scratch_shapes=[
+            pltpu.VMEM((HEADS, HEAD, HEAD), F32),
+            pltpu.VMEM((rows, width), F32),
             pltpu.VMEM((rows, width), BF16),
             pltpu.VMEM((rows, width), F32),
-            pltpu.VMEM((rows, width), F32),
+            pltpu.VMEM((2,) + dims + (width // n, 3 * FFW), BF16),
+            pltpu.VMEM((2, width, 3 * FFW), BF16),
+            pltpu.SemaphoreType.DMA((2 * steps, k)),
+            pltpu.SemaphoreType.DMA((2 * steps, k)),
+            pltpu.SemaphoreType.DMA((2 * steps,)),
+            pltpu.SemaphoreType.DMA((2,)),
+            pltpu.SemaphoreType.DMA((2,)),
         ],
         compiler_params=pltpu.CompilerParams(
-            vmem_limit_bytes=VMEM_LIMIT, dimension_semantics=("arbitrary",)
+            collective_id=collective_id, has_side_effects=True, vmem_limit_bytes=VMEM_LIMIT
         ),
-    )(hidden, grad, small, active, weights)
+    )(own, small, weights, out_weight, grad, active, feed_shard)
 
 
 def delta_back(base, last, refs, gain):
@@ -662,18 +678,847 @@
     dkb = [dot(da[h], k[h]) - dot_nt(dxl[h], s[h]) for h in heads]
     beta_grad = jnp.zeros((SPAN, 16), F32)
     for h in heads:
-        d_q[rows, lanes(h)] = low(dot_nt(do[h], s[h]) + dot(dp[h], k[h]))
-        d_k[rows, lanes(h)] = low(
+        d_q[rows, lanes(h)] = (dot_nt(do[h], s[h]) + dot(dp[h], k[h])).astype(d_q.dtype)
+        d_k[rows, lanes(h)] = (
             dkb[h] * b[h] + dot_tn(da[h], kb[h]) + dot_tn(dp[h], q[h]) + dot_nt(e[h], ds[h])
-        )
-        d_v[rows, lanes(h)] = low(dx[h] * b[h])
+        ).astype(d_k.dtype)
+        d_v[rows, lanes(h)] = (dx[h] * b[h]).astype(d_v.dtype)
         d_state[h] += dot_tn(q[h], do[h]) - dot_tn(kb[h], dxl[h])
         db = head_sum(dkb[h] * k[h].astype(F32) + dx[h] * values[rows, lanes(h)].astype(F32))
         beta_grad += jnp.where(lane == h, db, 0.0)
     d_beta[rows, :] = low(beta_grad * strength * (1.0 - strength))
 
 
-def backward_kernel(micro, length, *refs):
+SLOTS = 6
+
+
+def backward_kernel(dims, micro, length, steps, *refs):
+    (d_attn, small, out_weight, pre, queries, keys, values, beta,
+     states, inverses, scores, fresh, mix, mixed, feed_terms,
+     d_pre, d_beta, out_grad, small_grad, feed_grad,
+     d_state, d_out, d_q, d_k, d_v, gain_grad, send, recv, local, *slots) = refs
+    me = lax.axis_index("fsdp")
+    cs = coords_of(dims, me)
+    greet_axes(dims, cs)
+    half = 3 * FFW // 2
+
+    def jobs(i):
+        slot = lax.rem(i, SLOTS)
+        for p, order in enumerate((CXYZ, CYXZ)):
+            columns = pl.ds(pl.multiple_of(i * (3 * FFW) + p * half, half), half)
+            k = 2 * i + p
+            own, *got = [ref.at[slot] for ref in slots[5 * p : 5 * p + 5]]
+            yield Scatter(
+                dims, cs, feed_terms, columns, feed_grad, columns, order, own, got,
+                (send.at[k], recv.at[k], local.at[k]),
+            )
+
+    def tick(t):
+        loop_tick(jobs, steps, 5, 2, t)
+
+    tick(0)
+    width = d_attn.shape[1]
+    blocks = length // SPAN
+    total = micro * blocks
+    gain = small[ROW_OUT : ROW_OUT + 1, :HEAD]
+    gain_grad[...] = jnp.zeros_like(gain_grad)
+    small_grad[...] = jnp.zeros_like(small_grad)
+
+    def one(step, carry):
+        tick(2 * step + 1)
+        t = total - 1 - step
+        base = pl.multiple_of(t * SPAN, SPAN)
+        d_out[...] = dot(d_attn[pl.ds(base, SPAN), :], out_weight[...])
+        tick(2 * step + 2)
+        delta_back(
+            base, lax.rem(step, blocks) == 0,
+            (queries, keys, values, beta, states, inverses, scores, fresh, mix, d_out,
+             d_state, None, d_q, d_k, d_v, d_beta, gain_grad, t), gain,
+        )
+        return carry
+
+    lax.fori_loop(0, total, one, 0)
+    row = lax.broadcasted_iota(jnp.int32, (length, HEAD), 0)
+
+    def conv_back(m, carry):
+        tick(2 * total + 1 + m)
+        rows = pl.ds(m * length, length)
+        for kind, grads in enumerate((d_q, d_k, d_v)):
+            for h in range(width // HEAD):
+                cols = lanes(h)
+                wide = slice(kind * width + cols.start, kind * width + cols.stop)
+                taps = small[4 * kind : 4 * kind + 4, cols]
+                x = pre[rows, wide].astype(F32)
+                moved = [shifted(x, c, row) for c in range(4)]
+                c = moved[0] * taps[0:1]
+                for o in range(1, 4):
+                    c += moved[o] * taps[o : o + 1]
+                s = jax.nn.sigmoid(c)
+                u = c * s
+                d = grads[rows, cols]
+                if kind < 2:
+                    n = lax.rsqrt(head_sum(u * u) + UNIT_EPS)
+                    un = u * n
+                    d = (d - un * head_sum(un * d)) * n
+                d = d * (s + u * (1.0 - s))
+                for o in range(4):
+                    at = slice(4 * kind + o, 4 * kind + o + 1)
+                    small_grad[at, cols] += jnp.sum(moved[o] * d, axis=0, keepdims=True)
+                back = d * taps[0:1]
+                for o in range(1, 4):
+                    back += shifted(d, -o, row) * taps[o : o + 1]
+                d_pre[rows, wide] = low(back)
+        return carry
+
+    lax.fori_loop(0, micro, conv_back, 0)
+    for b in range(width // 256):
+        cols = lanes(b, 256)
+        out_grad[:, cols] = low(dot_tn(d_attn[...], mixed[:, cols]))
+    small_grad[ROW_OUT : ROW_OUT + 1, :HEAD] = gain_grad[...]
+
+    def rest(t, carry):
+        tick(t)
+        return carry
+
+    lax.fori_loop(2 * total + 1 + micro, steps + 8, rest, 0)
+
+
+def backward_call(d_attn, small, out_weight, saved, feed_terms, micro, collective_id):
+    rows, width = d_attn.shape
+    length = rows // micro
+    n = lax.axis_size("fsdp")
+    dims = grid_of(n)
+    k = hops(dims)
+    share = width // n
+    steps = feed_terms.shape[5] // (3 * FFW)
+    scratch = []
+    for order in (CXYZ, CYXZ):
+        scratch += scatter_scratch(dims, share, 3 * FFW // 2, order, BF16, (SLOTS,))
+    return pl.pallas_call(
+        functools.partial(backward_kernel, dims, micro, length, steps),
+        out_shape=[
+            jax.ShapeDtypeStruct((rows, 3 * width), BF16),
+            jax.ShapeDtypeStruct((rows, 16), BF16),
+            jax.ShapeDtypeStruct((width, width), BF16),
+            jax.ShapeDtypeStruct((SMALL_ROWS, width), F32),
+            jax.ShapeDtypeStruct((share, feed_terms.shape[5]), F32),
+        ],
+        in_specs=[vmem_spec()] * (3 + len(saved)) + [any_spec()],
+        out_specs=[vmem_spec()] * 5,
+        scratch_shapes=[
+            pltpu.VMEM((HEADS, HEAD, HEAD), F32),
+            pltpu.VMEM((SPAN, width), F32),
+            pltpu.VMEM((rows, width), F32),
+            pltpu.VMEM((rows, width), F32),
+            pltpu.VMEM((rows, width), F32),
+            pltpu.VMEM((1, HEAD), F32),
+            pltpu.SemaphoreType.DMA((2 * steps, k)),
+            pltpu.SemaphoreType.DMA((2 * steps, k)),
+            pltpu.SemaphoreType.DMA((2 * steps,)),
+        ]
+        + scratch,
+        compiler_params=pltpu.CompilerParams(
+            collective_id=collective_id, has_side_effects=True, vmem_limit_bytes=VMEM_LIMIT
+        ),
+    )(d_attn, small, out_weight, *saved, feed_terms)
+
+
+TAIL = 512
+
+
+def tail_kernel(dims, micro, length, *refs):
+    n = math.prod(dims)
+    (d_hidden, own, small, weights, attn_low, d_pre, d_beta, back, out_terms, small_terms, gain_mlp,
+     qkv_grad, out_grad, small_grad, returned,
+     d_rows, outgoing, row_sum, small_buf, tok_send, tok_recv, tok_local, send, recv, local,
+     *scr) = refs
+    me = lax.axis_index("fsdp")
+    cs = coords_of(dims, me)
+    greet_all(n, me)
+    width = own.shape[1]
+    share = width // n
+    rows = micro * length
+    tokens = Tokens(n, me, outgoing, returned, tok_send, tok_recv, tok_local)
+    pieces = 3 * width // TAIL
+    job_list, at = [], 0
+    sems = lambda i: (send.at[i], recv.at[i], local.at[i])
+    buffers = []
+    for i in range(width // TAIL):
+        own_buf, *got = scr[at : at + 5]
+        at += 5
+        job_list.append(Scatter(
+            dims, cs, out_terms, pl.ds(i * TAIL, TAIL), out_grad, pl.ds(i * TAIL, TAIL),
+            (CXYZ, CYXZ)[i % 2], own_buf, got, sems(len(job_list)),
+        ))
+    for i in range(pieces):
+        term, *got = scr[at : at + 5]
+        at += 5
+        buffers.append(term)
+        job_list.append(Scatter(
+            dims, cs, term, pl.ds(0, TAIL), qkv_grad, pl.ds(i * TAIL, TAIL),
+            (CXYZ, CYXZ)[i % 2], None, got, sems(len(job_list)),
+        ))
+    job_list.append(Scatter(
+        dims, cs, small_buf, pl.ds(0, HEAD), small_grad, pl.ds(0, HEAD), CXYZ, None, scr[at : at + 4],
+        sems(len(job_list)),
+    ))
+    lead = width // TAIL
+    tick = lambda t: run_tick(job_list, 5, 2, t)
+    for t in range(lead):
+        tick(t)
+    beta_rows = low(small[ROW_BETA : ROW_BETA + 16, :])
+    attn_gain = small[ROW_ATTN : ROW_ATTN + 1, :]
+    row_sum[...] = jnp.zeros_like(row_sum)
+    parts = outgoing.shape[1] * n * own.shape[1] // outgoing.shape[2] // rows
+    thin = outgoing.shape[2]
+
+    def block(t, carry):
+        at = pl.ds(pl.multiple_of(t * SPAN, SPAN), SPAN)
+        d = dot_nt(d_pre[at, :], weights[...]) + dot(d_beta[at, :], beta_rows)
+        v = own[at, :].astype(F32)
+        r = square_rms(v)
+        vr, gd = v * r, d * attn_gain
+        row_sum[...] += jnp.sum(d * vr, axis=0, keepdims=True)
+        d_rows[at, :] = low(d_hidden[at, :] + r * (gd - vr * jnp.mean(vr * gd, axis=-1, keepdims=True)))
+        return carry
+
+    lax.fori_loop(0, rows // SPAN, block, 0)
+    place_tokens(back, d_rows, outgoing)
+    tokens.start()
+    for i in range(pieces):
+        cols = lanes(i, TAIL)
+        grads = low(dot_tn(attn_low[...], d_pre[:, cols]))
+        buffers[i][...] = grads.reshape(dims + (share, TAIL))
+        tick(lead + i)
+    small_part(n, small_terms, gain_mlp, row_sum, dot_tn(d_beta[...], attn_low[...]), small_buf, dims)
+    for t in range(lead + pieces, len(job_list) + 8):
+        tick(t)
+    tokens.wait()
+
+
+def place_tokens(back, rows, outgoing):
+    n, count, thin = outgoing.shape
+    for p in range(rows.shape[1] // thin):
+        hot = lax.broadcasted_iota(jnp.int32, (n * count, rows.shape[0]), 1) == back[:, p : p + 1]
+        pick = dot(low(jnp.where(hot, 1.0, 0.0)), rows[:, lanes(p, thin)])
+        if p == 0:
+            held = pick
+        else:
+            held = held + pick
+    outgoing[...] = low(held).reshape(n, count, thin)
+
+
+def small_part(n, terms, gain_mlp, gain_attn, beta_grad, out, dims):
+    width = terms.shape[1]
+    share, few = width // n, HEAD // n
+    i = lax.broadcasted_iota(jnp.int32, (HEAD, width), 0)
+    c = lax.broadcasted_iota(jnp.int32, (HEAD, width), 1)
+    spread = (lax.rem(c, share) < few) & (i == (c // share) * few + lax.rem(c, share))
+    wide = jnp.broadcast_to(terms[ROW_OUT : ROW_OUT + 1, :HEAD], (HEAD, HEAD)).T[:, 0:1]
+    gain_out = jnp.sum(jnp.where(spread, wide, 0.0), axis=0, keepdims=True)
+    block = jnp.concatenate(
+        [terms[:ROW_ATTN, :], gain_attn[...], gain_mlp[...], gain_out, jnp.zeros((1, width), F32), beta_grad,
+         jnp.zeros((HEAD - SMALL_ROWS, width), F32)], axis=0,
+    )
+    out[...] = block.T.reshape(dims + (share, HEAD))
+
+
+def tail_call(d_hidden, own, small, weights, attn_low, d_pre, d_beta, back, out_terms, small_terms,
+              gain_mlp, token_shape, micro, collective_id):
+    rows, width = own.shape
+    n = lax.axis_size("fsdp")
+    dims = grid_of(n)
+    k = hops(dims)
+    share = width // n
+    scratch = []
+    for i in range(width // TAIL):
+        scratch += scatter_scratch(dims, share, TAIL, (CXYZ, CYXZ)[i % 2], BF16)
+    for i in range(3 * width // TAIL):
+        scratch.append(pltpu.VMEM(dims + (share, TAIL), BF16))
+        scratch += scatter_scratch(dims, share, TAIL, (CXYZ, CYXZ)[i % 2], BF16, keep=False)
+    scratch += scatter_scratch(dims, share, HEAD, CXYZ, F32, keep=False)
+    m = 4 * width // TAIL + 1
+    return pl.pallas_call(
+        functools.partial(tail_kernel, dims, micro, rows // micro),
+        out_shape=[
+            jax.ShapeDtypeStruct((share, 3 * width), F32),
+            jax.ShapeDtypeStruct((share, width), F32),
+            jax.ShapeDtypeStruct((share, HEAD), F32),
+            jax.ShapeDtypeStruct(token_shape, BF16),
+        ],
+        in_specs=[vmem_spec()] * 8 + [any_spec()] + [vmem_spec()] * 2,
+        out_specs=[vmem_spec()] * 3 + [any_spec()],
+        scratch_shapes=[
+            pltpu.VMEM((rows, width), BF16),
+            pltpu.VMEM(token_shape, BF16),
+            pltpu.VMEM((1, width), F32),
+            pltpu.VMEM(dims + (share, HEAD), F32),
+        ]
+        + token_sems(n)
+        + [
+            pltpu.SemaphoreType.DMA((m, k)),
+            pltpu.SemaphoreType.DMA((m, k)),
+            pltpu.SemaphoreType.DMA((m,)),
+        ]
+        + scratch,
+        compiler_params=pltpu.CompilerParams(
+            collective_id=collective_id, has_side_effects=True, vmem_limit_bytes=VMEM_LIMIT
+        ),
+    )(d_hidden, own, small, weights, attn_low, d_pre, d_beta, back, out_terms, small_terms, gain_mlp)
+
+
+def picked(index, source):
+    hot = index[:, None] == jnp.arange(source.shape[0], dtype=jnp.int32)[None, :]
+    return jnp.dot(low(hot), source, preferred_element_type=F32).astype(BF16)
+
+
+def split_rows(values, parts):
+    cut = values.reshape(values.shape[:-1] + (parts, values.shape[-1] // parts))
+    return jnp.moveaxis(cut, -2, 0)
+
+
+def spans(width, size):
+    at = 0
+    while at < width:
+        yield at, min(size, width - at)
+        at += size
+
+
+def local(
+    inputs, cotangent, lengths, owners, attn_gain, query_weight, key_weight, value_weight, beta_weight,
+    query_conv, key_conv, value_conv, out_gain, out_weight, mlp_gain, gate_weight, up_weight, down_weight,
+):
+    n = lax.axis_size("fsdp")
+    dims = grid_of(n)
+    me = lax.axis_index("fsdp")
+    micro, _, length, width = inputs.shape
+    hidden_units = gate_weight.shape[1]
+    share = width // n
+    if share % 16:
+        return local_thin(
+            inputs, cotangent, lengths, owners, attn_gain, query_weight, key_weight, value_weight, beta_weight,
+            query_conv, key_conv, value_conv, out_gain, out_weight, mlp_gain, gate_weight, up_weight, down_weight,
+        )
+    slots = length // n
+    per = micro * slots
+    parts = 16 // math.gcd(per, 16)
+    thin = width // parts
+    i32 = jnp.int32
+    devices = jnp.arange(n, dtype=i32)
+    slot_ids = jnp.arange(slots, dtype=i32)
+    row_ids = jnp.arange(length, dtype=i32)
+    micros = jnp.arange(micro, dtype=i32)
+    part_ids = jnp.arange(parts, dtype=i32)
+
+    before = devices[:, None] < devices[None, :]
+    starts = jnp.sum(jnp.where(before[None], lengths[:, :, None], 0), axis=1)
+    match = owners[:, None, :] == devices[None, :, None]
+    own_start = jnp.sum(jnp.where(match, starts[:, None, :], 0), axis=2)
+    own_len = jnp.sum(jnp.where(match, lengths[:, None, :], 0), axis=2)
+    mine = devices == me
+    my_start = jnp.sum(jnp.where(mine, own_start, 0), axis=1)
+    my_len = jnp.sum(jnp.where(mine, own_len, 0), axis=1)
+
+    first = own_start + (me - own_start) % n
+    pos = first[:, :, None] + n * slot_ids
+    live = pos < (own_start + own_len)[:, :, None]
+    send = jnp.where(live, micros[:, None, None] * length + pos // n, -1)
+    send = jnp.moveaxis(send, 0, 1)[:, None] + jnp.zeros((1, parts, 1, 1), i32)
+    send = jnp.where(send >= 0, send + (part_ids * micro * length)[None, :, None, None], -1)
+    rows_in = split_rows(inputs[:, 0].reshape(micro * length, width), parts).reshape(-1, thin)
+    outgoing = picked(send.reshape(-1), rows_in).reshape(n, parts * per, thin)
+
+    def row_of(v):
+        return jnp.pad(v, ((0, 0), (0, share - v.shape[1])))
+
+    packed = jnp.concatenate([
+        query_conv, key_conv, value_conv, attn_gain[None], mlp_gain[None], row_of(out_gain[None]),
+        jnp.zeros((1, share), BF16), beta_weight.T, jnp.zeros((SMALL_ROWS - 16 - HEADS, share), BF16),
+    ])
+    count = SMALL_ROWS * share // HEAD
+    packed = jnp.pad(packed.reshape(count, HEAD), ((0, -count % 16), (0, 0)))
+
+    attn_shard = jnp.concatenate([query_weight, key_weight, value_weight], axis=1)
+    steps = hidden_units // FFW
+    feed_shard = jnp.stack(
+        [w.reshape(share, steps, FFW) for w in (gate_weight, up_weight, down_weight.T)], axis=2
+    ).reshape(share, 3 * hidden_units)
+
+    plan = [(0, 0, HEAD, ZXY)]
+    for a, w in ((1, 3 * width), (2, width)):
+        for at, wide in spans(w, 512):
+            plan.append((a, at, wide, (ZXY, ZYX)[len(plan) % 2]))
+    small_all, qkv, out_t, incoming = gather_call(
+        [packed, attn_shard, out_weight.T], outgoing, tuple(plan), 2, 1
+    )
+    small = small_all.reshape(n, -1)[:, : SMALL_ROWS * share].reshape(n, SMALL_ROWS, share)
+    small = jnp.moveaxis(small, 1, 0)
+    gain_row = small[ROW_OUT, :, : HEAD // n].reshape(1, HEAD)
+    small = small.reshape(SMALL_ROWS, width).astype(F32)
+    small = lax.dynamic_update_slice(small, gain_row.astype(F32), (ROW_OUT, 0))
+    qkv, out_t = qkv.reshape(width, 3 * width), out_t.reshape(width, width)
+
+    active = row_ids[None] < my_len[:, None]
+    block = (my_start[:, None] + row_ids) % n
+    at = block * (parts * per) + micros[:, None] * slots + row_ids // n
+    take = jnp.where(active, at, -1).reshape(-1)
+    flat = incoming.reshape(n * parts * per, thin)
+    own = jnp.concatenate(
+        [picked(jnp.where(take >= 0, take + p * per, -1), flat) for p in range(parts)], axis=1
+    )
+    active = active.reshape(-1, 1)
+    grad = jnp.where(active, cotangent[:, 0].reshape(-1, width), jnp.zeros((), BF16))
+
+    result, d_hidden, d_attn, mlp_gain_terms, feed_terms, _, attn_low, *saved = forward_call(
+        own, small, qkv, out_t, grad, active.astype(F32), feed_shard, micro, 2
+    )
+    feed_terms = feed_terms.reshape(dims + (share, 3 * hidden_units))
+    d_pre, d_beta, out_terms, small_terms, feed_grad = backward_call(
+        d_attn, small, out_t, saved, feed_terms, micro, 3
+    )
+
+    back = slot_ids * n + (devices[:, None, None] - my_start[None, :, None]) % n
+    back = jnp.where(back < my_len[None, :, None], back + (micros * length)[None, :, None], -1)
+    back = jnp.where(
+        (part_ids[:, None] == part_ids[None, :])[None, :, None, None, :], back[:, None, :, :, None], -1
+    )
+    back = back.reshape(n * parts * per, parts)
+    qkv_grad, out_grad, small_grad, returned = tail_call(
+        d_hidden, own, small, qkv, attn_low, d_pre, d_beta, back,
+        out_terms.reshape(dims + (share, width)), small_terms, mlp_gain_terms,
+        (n, parts * per, thin), micro, 4,
+    )
+
+    place = row_ids * n + me
+    inside = (place[None, :, None] >= own_start[:, None, :]) & (
+        place[None, :, None] < (own_start + own_len)[:, None, :]
+    )
+    at = devices * (parts * per) + micros[:, None, None] * slots + (place[None, :, None] - first[:, None, :]) // n
+    take = (jnp.sum(jnp.where(inside, at + 1, 0), axis=2) - 1).reshape(-1)
+    flat = returned.reshape(n * parts * per, thin)
+    input_rows = jnp.concatenate(
+        [picked(jnp.where(take >= 0, take + p * per, -1), flat) for p in range(parts)], axis=1
+    )
+
+    small_grad = small_grad.T
+    feed_grad = feed_grad.reshape(share, steps, 3, FFW)
+    gate_grad, up_grad, down_grad = (
+        feed_grad[:, :, i].reshape(share, hidden_units) for i in range(3)
+    )
+    return (
+        result.reshape(micro, 1, length, width),
+        input_rows.reshape(micro, 1, length, width),
+        small_grad[ROW_ATTN],
+        qkv_grad[:, :width],
+        qkv_grad[:, width : 2 * width],
+        qkv_grad[:, 2 * width :],
+        small_grad[ROW_BETA : ROW_BETA + HEADS].T,
+        small_grad[0:4],
+        small_grad[4:8],
+        small_grad[8:12],
+        small_grad[ROW_OUT, : HEAD // n],
+        out_grad.T,
+        small_grad[ROW_MLP],
+        gate_grad,
+        up_grad,
+        down_grad.T,
+    )
+
+
+class GatherThin:
+    def __init__(self, dims, cs, shard, out, low, width, order, sems):
+        self.dims, self.cs, self.order = dims, cs, order
+        self.columns = pl.ds(low, width)
+        self.shard, self.out = shard.at[:, self.columns], out
+        self.send, self.recv, self.local_thin = sems
+
+    def slot(self, stage, delta):
+        return sum(self.dims[a] - 1 for a in self.order[:stage]) + delta - 1
+
+    def region(self, stage, cs):
+        done = self.order[:stage]
+        lead = tuple(slice(None) if k in done else cs[k] for k in range(4))
+        return self.out.at[lead + (slice(None), self.columns)]
+
+    def copies(self, stage, incoming):
+        axis = self.order[stage]
+        for delta in range(1, self.dims[axis]):
+            frm = along(self.dims, self.cs, axis, -delta) if incoming else self.cs
+            to = along(self.dims, self.cs, axis, delta)
+            k = self.slot(stage, delta)
+            yield pltpu.make_async_remote_copy(
+                src_ref=self.shard if stage == 0 else self.region(stage, self.cs),
+                dst_ref=self.region(stage, frm),
+                send_sem=self.send.at[k],
+                recv_sem=self.recv.at[k],
+                device_id=(index_of(self.dims, to),),
+                device_id_type=MESH,
+            )
+
+    def keep(self):
+        return pltpu.make_async_copy(self.shard, self.region(0, self.cs), self.local_thin)
+
+    def step(self, stage):
+        if stage == 0:
+            self.keep().start()
+        if stage == 1:
+            self.keep().wait()
+        if stage >= 1:
+            for c in self.copies(stage - 1, True):
+                c.wait_recv()
+        if stage < 4:
+            for c in self.copies(stage, False):
+                c.start()
+
+    def finish(self):
+        for stage in range(4):
+            for c in self.copies(stage, False):
+                c.wait_send()
+
+
+def pipelined_thin(jobs, stages, lag):
+    for tick in range(len(jobs) + (stages - 1) * lag):
+        for stage in range(stages):
+            i = tick - stage * lag
+            if 0 <= i < len(jobs):
+                jobs[i].step(stage)
+
+
+def gather_kernel_thin(dims, plan, lag, count, with_tokens, *refs):
+    n = math.prod(dims)
+    t = 1 if with_tokens else 0
+    ins, outs, scr = refs[: count + t], refs[count + t : 2 * (count + t)], refs[2 * (count + t) :]
+    send, recv, local_thin = scr[:3]
+    me = lax.axis_index("fsdp")
+    cs = coords_of(dims, me)
+    if with_tokens:
+        greet_all(n, me)
+        tokens = Tokens(n, me, ins[count], outs[count], *scr[3:])
+        tokens.start()
+    else:
+        greet_axes(dims, cs)
+    jobs = [
+        GatherThin(dims, cs, ins[a], outs[a], low, width, order, (send.at[i], recv.at[i], local_thin.at[i]))
+        for i, (a, low, width, order) in enumerate(plan)
+    ]
+    pipelined_thin(jobs, 5, lag)
+    for j in jobs:
+        j.finish()
+    if with_tokens:
+        tokens.wait()
+
+
+def gather_call_thin(shards, tokens, plan, lag, collective_id):
+    n = lax.axis_size("fsdp")
+    dims = grid_of(n)
+    k = hops(dims)
+    ins = list(shards) + ([] if tokens is None else [tokens])
+    outs = [jax.ShapeDtypeStruct(dims + s.shape, s.dtype) for s in shards]
+    if tokens is not None:
+        outs.append(jax.ShapeDtypeStruct(tokens.shape, tokens.dtype))
+    m = len(plan)
+    return pl.pallas_call(
+        functools.partial(gather_kernel_thin, dims, plan, lag, len(shards), tokens is not None),
+        out_shape=outs,
+        in_specs=[any_spec()] * len(ins),
+        out_specs=[any_spec()] * len(outs),
+        scratch_shapes=[
+            pltpu.SemaphoreType.DMA((m, k)),
+            pltpu.SemaphoreType.DMA((m, k)),
+            pltpu.SemaphoreType.DMA((m,)),
+        ]
+        + ([] if tokens is None else token_sems(n)),
+        compiler_params=pltpu.CompilerParams(
+            collective_id=collective_id, has_side_effects=True, vmem_limit_bytes=VMEM_LIMIT
+        ),
+    )(*ins)
+
+
+class ScatterThin:
+    def __init__(self, dims, cs, terms, result, low, width, order, scratch, sems):
+        self.dims, self.cs, self.order = dims, cs, order
+        self.columns = pl.ds(low, width)
+        self.terms, self.result = terms, result
+        self.own, self.got = scratch[0], scratch[1:]
+        self.send, self.recv, self.local_thin = sems
+
+    def slot(self, stage, delta):
+        return sum(self.dims[a] - 1 for a in self.order[:stage]) + delta - 1
+
+    def part(self, stage, at):
+        axis = self.order[stage]
+        if stage == 0:
+            lead = tuple(at if k == axis else slice(None) for k in range(4))
+            return self.terms.at[lead + (slice(None), self.columns)]
+        left = [k for k in range(4) if k not in self.order[:stage]]
+        return self.got[stage - 1].at[(0,) + tuple(at if k == axis else slice(None) for k in left)]
+
+    def copies(self, stage):
+        axis = self.order[stage]
+        for delta in range(1, self.dims[axis]):
+            to = along(self.dims, self.cs, axis, delta)
+            k = self.slot(stage, delta)
+            yield pltpu.make_async_remote_copy(
+                src_ref=self.part(stage, to[axis]),
+                dst_ref=self.got[stage].at[delta - 1],
+                send_sem=self.send.at[k],
+                recv_sem=self.recv.at[k],
+                device_id=(index_of(self.dims, to),),
+                device_id_type=MESH,
+            )
+
+    def keep(self):
+        return pltpu.make_async_copy(self.part(0, self.cs[self.order[0]]), self.own, self.local_thin)
+
+    def total(self, stage):
+        axis = self.order[stage]
+        left = [k for k in range(4) if k not in self.order[: stage + 1]]
+        shape = [self.dims[k] for k in left]
+        got = self.got[stage]
+        mine = self.own if stage == 0 else self.part(stage, self.cs[axis])
+
+        def one(i, carry):
+            at = tuple(coords_of(shape, i)) if shape else ()
+            total = mine[at + (slice(None), slice(None))].astype(F32)
+            for delta in range(1, self.dims[axis]):
+                total += got[(delta - 1,) + at + (slice(None), slice(None))].astype(F32)
+            if left:
+                got[(0,) + at + (slice(None), slice(None))] = total.astype(got.dtype)
+            else:
+                self.result[:, self.columns] = total
+            return carry
+
+        lax.fori_loop(0, math.prod(shape), one, 0)
+
+    def step(self, stage):
+        if stage == 0:
+            self.keep().start()
+        if stage == 1:
+            self.keep().wait()
+        if stage >= 1:
+            for c in self.copies(stage - 1):
+                c.wait_recv()
+            self.total(stage - 1)
+        if stage < 4:
+            for c in self.copies(stage):
+                c.start()
+
+    def finish(self):
+        for stage in range(4):
+            for c in self.copies(stage):
+                c.wait_send()
+
+
+def scatter_scratch_thin(dims, rows, width, order, dtype):
+    left = list(dims)
+    out = [pltpu.VMEM(tuple(d for k, d in enumerate(dims) if k != order[0]) + (rows, width), dtype)]
+    for s, axis in enumerate(order):
+        rest = tuple(dims[k] for k in range(4) if k not in order[: s + 1])
+        out.append(pltpu.VMEM((dims[axis] - 1,) + rest + (rows, width), dtype))
+    return out
+
+
+def scatter_kernel_thin(dims, plan, lag, count, with_tokens, *refs):
+    n = math.prod(dims)
+    t = 1 if with_tokens else 0
+    ins, outs, scr = refs[: count + t], refs[count + t : 2 * (count + t)], refs[2 * (count + t) :]
+    send, recv, local_thin = scr[:3]
+    scr = scr[3:]
+    me = lax.axis_index("fsdp")
+    cs = coords_of(dims, me)
+    if with_tokens:
+        greet_all(n, me)
+        tokens = Tokens(n, me, ins[count], outs[count], *scr[:3])
+        tokens.start()
+        scr = scr[3:]
+    else:
+        greet_axes(dims, cs)
+    jobs = [
+        ScatterThin(
+            dims, cs, ins[a], outs[a], low, width, order, scr[5 * i : 5 * i + 5],
+            (send.at[i], recv.at[i], local_thin.at[i]),
+        )
+        for i, (a, low, width, order) in enumerate(plan)
+    ]
+    pipelined_thin(jobs, 5, lag)
+    for j in jobs:
+        j.finish()
+    if with_tokens:
+        tokens.wait()
+
+
+def scatter_call_thin(terms, tokens, plan, lag, collective_id):
+    n = lax.axis_size("fsdp")
+    dims = grid_of(n)
+    k = hops(dims)
+    ins = list(terms) + ([] if tokens is None else [tokens])
+    outs = [jax.ShapeDtypeStruct(s.shape[4:], F32) for s in terms]
+    out_specs = [vmem_spec()] * len(terms)
+    if tokens is not None:
+        outs.append(jax.ShapeDtypeStruct(tokens.shape, tokens.dtype))
+        out_specs.append(any_spec())
+    m = len(plan)
+    scratch = []
+    for a, low, width, order in plan:
+        scratch += scatter_scratch_thin(dims, terms[a].shape[4], width, order, terms[a].dtype)
+    return pl.pallas_call(
+        functools.partial(scatter_kernel_thin, dims, plan, lag, len(terms), tokens is not None),
+        out_shape=outs,
+        in_specs=[any_spec()] * len(ins),
+        out_specs=out_specs,
+        scratch_shapes=[
+            pltpu.SemaphoreType.DMA((m, k)),
+            pltpu.SemaphoreType.DMA((m, k)),
+            pltpu.SemaphoreType.DMA((m,)),
+        ]
+        + ([] if tokens is None else token_sems(n))
+        + scratch,
+        compiler_params=pltpu.CompilerParams(
+            collective_id=collective_id, has_side_effects=True, vmem_limit_bytes=VMEM_LIMIT
+        ),
+    )(*ins)
+
+
+def project_thin(own, small, weights, attn_low, pre, queries, keys, values, beta, micro, length):
+    width = own.shape[1]
+    row = lax.broadcasted_iota(jnp.int32, (length, 2 * HEAD), 0)
+    gain = small[ROW_ATTN : ROW_ATTN + 1, :]
+    beta_rows = low(small[ROW_BETA : ROW_BETA + 16, :])
+
+    def one(m, carry):
+        rows = pl.ds(m * length, length)
+        v = own[rows, :].astype(F32)
+        r = lax.rsqrt(jnp.mean(v * v, axis=-1, keepdims=True) + NORM_EPS)
+        attn_low[rows, :] = low(v * r * gain)
+        a = attn_low[rows, :]
+        beta[rows, :] = jax.nn.sigmoid(dot_nt(a, beta_rows))
+        for kind, out in enumerate((queries, keys, values)):
+            for b in range(width // (2 * HEAD)):
+                cols = lanes(b, 2 * HEAD)
+                wide = slice(kind * width + cols.start, kind * width + cols.stop)
+                x = dot(a, weights[:, wide])
+                pre[rows, wide] = low(x)
+                c = conv(x, small[4 * kind : 4 * kind + 4, cols], row)
+                u = c * jax.nn.sigmoid(c)
+                if kind == 2:
+                    out[rows, cols] = low(u)
+                    continue
+                for h in range(2):
+                    part = u[:, lanes(h)]
+                    n = lax.rsqrt(head_sum(part * part) + UNIT_EPS)
+                    out[rows, slice(cols.start + h * HEAD, cols.start + (h + 1) * HEAD)] = low(part * n)
+        return carry
+
+    lax.fori_loop(0, micro, one, 0)
+
+
+def forward_kernel_thin(micro, length, *refs):
+    (own, small, weights, out_weight, hidden, attn_low, pre, queries, keys, values, beta,
+     states, inverses, scores, fresh, mix, mixed, state) = refs
+    project_thin(own, small, weights, attn_low, pre, queries, keys, values, beta, micro, length)
+    gain = small[ROW_OUT : ROW_OUT + 1, :HEAD]
+    blocks = length // SPAN
+
+    def one(t, carry):
+        delta_block(
+            pl.multiple_of(t * SPAN, SPAN), lax.rem(t, blocks) == 0,
+            (queries, keys, values, beta, state, states, inverses, scores, fresh, mix, mixed, t), gain,
+        )
+        rows = pl.ds(pl.multiple_of(t * SPAN, SPAN), SPAN)
+        hidden[rows, :] = own[rows, :].astype(F32) + dot_nt(mixed[rows, :], out_weight[...])
+        return carry
+
+    lax.fori_loop(0, micro * blocks, one, 0)
+
+
+def forward_call_thin(own, small, weights, out_weight, micro):
+    rows, width = own.shape
+    length = rows // micro
+    blocks = rows // SPAN
+    square = jax.ShapeDtypeStruct((blocks, HEADS, SPAN, SPAN), BF16)
+    wide = jax.ShapeDtypeStruct((rows, width), BF16)
+    outs = [
+        jax.ShapeDtypeStruct((rows, width), F32), wide, jax.ShapeDtypeStruct((rows, 3 * width), BF16),
+        wide, wide, wide, jax.ShapeDtypeStruct((rows, 16), F32),
+        jax.ShapeDtypeStruct((blocks, HEADS, HEAD, HEAD), BF16), square, square, wide, wide, wide,
+    ]
+    return pl.pallas_call(
+        functools.partial(forward_kernel_thin, micro, length),
+        out_shape=outs,
+        in_specs=[vmem_spec()] * 4,
+        out_specs=[vmem_spec()] * len(outs),
+        scratch_shapes=[pltpu.VMEM((HEADS, HEAD, HEAD), F32)],
+        compiler_params=pltpu.CompilerParams(vmem_limit_bytes=VMEM_LIMIT),
+    )(own, small, weights, out_weight)
+
+
+def feed_kernel_thin(steps, hidden, grad, small, active, w_ref, result, terms, d_hidden, gain_grad, norm, total, d_norm):
+    t = pl.program_id(0)
+    gain = small[ROW_MLP : ROW_MLP + 1, :]
+
+    @pl.when(t == 0)
+    def _():
+        v = hidden[...]
+        r = lax.rsqrt(jnp.mean(v * v, axis=-1, keepdims=True) + NORM_EPS)
+        norm[...] = low(v * r * gain)
+        total[...] = v
+        d_norm[...] = jnp.zeros_like(d_norm)
+
+    x, g = norm[...], grad[...]
+    gw, uw, dw = (w_ref[:, lanes(i, FFW)] for i in range(3))
+    gate, up = dot(x, gw), dot(x, uw)
+    d_act = dot(g, dw)
+    s = jax.nn.sigmoid(gate)
+    silu = gate * s
+    act = low(silu * up)
+    d_gate = low(d_act * up * (s + silu * (1.0 - s)))
+    d_up = low(d_act * silu)
+    total[...] += dot_nt(act, dw)
+    d_norm[...] += dot_nt(d_gate, gw) + dot_nt(d_up, uw)
+    terms[:, lanes(0, FFW)] = low(dot_tn(x, d_gate))
+    terms[:, lanes(1, FFW)] = low(dot_tn(x, d_up))
+    terms[:, lanes(2, FFW)] = low(dot_tn(g, act))
+
+    @pl.when(t == steps - 1)
+    def _():
+        result[...] = low(jnp.where(active[...] > 0.0, total[...], 0.0))
+        v, d = hidden[...], d_norm[...]
+        n = v.shape[1]
+        r = lax.rsqrt(jnp.mean(v * v, axis=-1, keepdims=True) + NORM_EPS)
+        vr = v * r
+        gain_grad[...] = jnp.sum(d * vr, axis=0, keepdims=True)
+        gd = d * gain
+        d_hidden[...] = g.astype(F32) + r * (gd - vr * (jnp.sum(vr * gd, axis=-1, keepdims=True) / n))
+
+
+def feed_call_thin(hidden, grad, small, active, weights):
+    rows, width = hidden.shape
+    steps = weights.shape[1] // (3 * FFW)
+    whole = lambda *shape: pl.BlockSpec(shape, lambda t: (0,) * len(shape))
+    block = pl.BlockSpec((width, 3 * FFW), lambda t: (0, t))
+    return pl.pallas_call(
+        functools.partial(feed_kernel_thin, steps),
+        grid=(steps,),
+        out_shape=[
+            jax.ShapeDtypeStruct((rows, width), BF16),
+            jax.ShapeDtypeStruct(weights.shape, BF16),
+            jax.ShapeDtypeStruct((rows, width), F32),
+            jax.ShapeDtypeStruct((1, width), F32),
+        ],
+        in_specs=[whole(rows, width), whole(rows, width), whole(*small.shape), whole(rows, 1), block],
+        out_specs=[whole(rows, width), block, whole(rows, width), whole(1, width)],
+        scratch_shapes=[
+            pltpu.VMEM((rows, width), BF16),
+            pltpu.VMEM((rows, width), F32),
+            pltpu.VMEM((rows, width), F32),
+        ],
+        compiler_params=pltpu.CompilerParams(
+            vmem_limit_bytes=VMEM_LIMIT, dimension_semantics=("arbitrary",)
+        ),
+    )(hidden, grad, small, active, weights)
+
+
+def backward_kernel_thin(micro, length, *refs):
     (d_hidden, own, small, weights, out_weight, attn_low, pre, queries, keys, values, beta,
      states, inverses, scores, fresh, mix, mixed,
      d_own, qkv_grad, out_grad, small_grad,
@@ -754,11 +1599,11 @@
     lax.fori_loop(0, total, finish, 0)
 
 
-def backward_call(d_hidden, own, small, weights, out_weight, saved, micro):
+def backward_call_thin(d_hidden, own, small, weights, out_weight, saved, micro):
     rows, width = own.shape
     length = rows // micro
     return pl.pallas_call(
-        functools.partial(backward_kernel, micro, length),
+        functools.partial(backward_kernel_thin, micro, length),
         out_shape=[
             jax.ShapeDtypeStruct((rows, width), BF16),
             jax.ShapeDtypeStruct((width, 3 * width), BF16),
@@ -782,24 +1627,7 @@
     )(d_hidden, own, small, weights, out_weight, *saved)
 
 
-def picked(index, source):
-    hot = index[:, None] == jnp.arange(source.shape[0], dtype=jnp.int32)[None, :]
-    return jnp.dot(low(hot), source, preferred_element_type=F32).astype(BF16)
-
-
-def split_rows(values, parts):
-    cut = values.reshape(values.shape[:-1] + (parts, values.shape[-1] // parts))
-    return jnp.moveaxis(cut, -2, 0)
-
-
-def spans(width, size):
-    at = 0
-    while at < width:
-        yield at, min(size, width - at)
-        at += size
-
-
-def local(
+def local_thin(
     inputs, cotangent, lengths, owners, attn_gain, query_weight, key_weight, value_weight, beta_weight,
     query_conv, key_conv, value_conv, out_gain, out_weight, mlp_gain, gate_weight, up_weight, down_weight,
 ):
@@ -858,7 +1686,7 @@
     for a, (w, size) in enumerate(((4 * width, 512), (3 * hidden_units, 768)), 1):
         for at, wide in spans(w, size):
             plan.append((a, at, wide, (ZXY, ZYX)[len(plan) % 2]))
-    small_all, attn_all, feed_all, incoming = gather_call(
+    small_all, attn_all, feed_all, incoming = gather_call_thin(
         [packed, attn_shard, feed_shard], outgoing, tuple(plan), 2, 1
     )
     small = small_all.reshape(n, -1)[:, : SMALL_ROWS * share].reshape(n, SMALL_ROWS, share)
@@ -881,11 +1709,11 @@
     active = active.reshape(-1, 1)
     grad = jnp.where(active, cotangent[:, 0].reshape(-1, width), jnp.zeros((), BF16))
 
-    hidden, *saved = forward_call(own, small, qkv, out_t, micro)
-    result, feed_terms, d_hidden, mlp_gain_grad = feed_call(
+    hidden, *saved = forward_call_thin(own, small, qkv, out_t, micro)
+    result, feed_terms, d_hidden, mlp_gain_grad = feed_call_thin(
         hidden, grad, small, active.astype(F32), feed_all
     )
-    d_own, qkv_terms, out_terms, small_terms = backward_call(
+    d_own, qkv_terms, out_terms, small_terms = backward_call_thin(
         d_hidden, own, small, qkv, out_t, saved, micro
     )
 
@@ -914,7 +1742,7 @@
     for a, size in ((3, 768), (2, 512), (1, 512), (0, HEAD)):
         for lo, wide in spans(terms[a].shape[5], size):
             plan.append((a, lo, wide, (CXYZ, CYXZ)[len(plan) % 2]))
-    small_grad, qkv_grad, out_grad, feed_grad, returned = scatter_call(
+    small_grad, qkv_grad, out_grad, feed_grad, returned = scatter_call_thin(
         terms, returning, tuple(plan), 2, 2
     )
 

time: 543 us -> 476 us (0.88)
  Pallas kernels: 471 us -> 422 us
  local copies, waits for them, and re-layouts: 38.8 us -> 24.3 us
    pallas_call x1, Pallas kernels: 163 us -> 91.1 us  [gather_call(): pl.pallas_call(functools.partial(gather_kernel, dims, plan, lag, len(shar...]
    pallas_call x4 -> x3, Pallas kernels: 308 us -> 330 us  [the longest x1 122 us: forward_call(): pl.pallas_call(functools.partial(forward_kernel, dims, micro, length, ste...]
    slice x10 -> x2, local copies, waits for them, and re-layouts: 10.3 us -> 1.39 us  [the longest x1 0.7 us: local(): small_grad[ROW_MLP]]
    dot_general x6 -> x5, matrix products: 15.6 us -> 13.2 us  [picked(): return jnp.dot(low(hot), source, preferred_element_type=F32).astype(BF16)]
where the time goes in v2:
time: 476 us; the launch traced here: 468 us
  Pallas kernels  422 us (89%)
  local copies, waits for them, and re-layouts  24.3 us (5%)
  matrix products  13.2 us (3%)
  other arithmetic  7.06 us (1%)
    pallas_call x1, Pallas kernels, forward_call(): pl.pallas_call(functools.partial(forward_kernel, dims, micro, length, ste...  122 us
    pallas_call x1, Pallas kernels, backward_call(): pl.pallas_call(functools.partial(backward_kernel, dims, micro, length, st...  112 us
    pallas_call x1, Pallas kernels, tail_call(): pl.pallas_call(functools.partial(tail_kernel, dims, micro, rows // micro)...  96.7 us
    pallas_call x1, Pallas kernels, gather_call(): pl.pallas_call(functools.partial(gather_kernel, dims, plan, lag, len(shar...  91.1 us
    dot_general x5, matrix products, picked(): return jnp.dot(low(hot), source, preferred_element_type=F32).astype(BF16)  13.2 us
    unnamed x59, local copies, waits for them, and re-layouts  10 us

profile of v2, /device:TPU:0, one launch (start us, length us, event | category | flops | bytes accessed | tf_op | source)
XLA Modules:
  0.0 467.9 jit_solution(6310934411321417985)
XLA Ops:
  0.7 0.8 select_reduce_fusion.1
  1.4 0.8 select_reduce_fusion
  2.9 2.9 reshape_reshape_squeeze.3
  6.2 4.0 fusion.6
  10.1 0.7 pad_maximum_fusion.3.refs_1_
  11.1 0.6 pad.9.refs_0_
  11.7 91.1 %shard_map.297 = (bf16[4,2,2,2,16,128]{5,4,3,2,1,0:T(8,128)(2,1)}, bf16[4,2,2,2,32,3072]{5,4,3,2,1,0:T(8,128)(2,1)}, bf16[4,2,2,2,32,1024]{5,4,3,2,1,0:T(8,128)(2,1)}, bf16[32,48,512]{2,1,0:T(8,128)(2,1)}) custom-call(bf16[16,128]{1,0:T(8,128)(2,1)} %pad.9.refs_0_, bf16[32,3072]{1,0:T(8,128)(2,1)} %pad_maximum_fusion.3.refs_1_, bf16[32,1024]{1,0:T(8,128)(2,1)} %bitcast.89, ...), custom_call_target="tpu_custom_call" | custom-call | tf_op jit(solution)/shard_map/pallas_call | solution.py:246
  103.3 3.0 fusion.14
  106.3 1.4 fusion.13
  107.7 2.2 pad_maximum_fusion
  111.3 0.9 copy.100
  113.3 1.4 reshape.473.refs_6_
  114.7 122.2 %shard_map.298 = (bf16[768,1024]{1,0:T(8,128)(2,1)}, f32[768,1024]{1,0:T(8,128)}, bf16[768,1024]{1,0:T(8,128)(2,1)}, f32[1,1024]{1,0:T(1,128)}, bf16[1024,8448]{...) custom-call(bf16[768,1024]{1,0:T(8,128)(2,1)} %get-tuple-element.169, ...), custom_call_target="tpu_custom_call" | custom-call | tf_op jit(solution)/shard_map/pallas_call | solution.py:621
  236.9 111.6 %shard_map.299 = (bf16[768,3072]{1,0:T(8,128)(2,1)}, bf16[768,16]{1,0:T(8,128)(2,1)}, bf16[1024,1024]{1,0:T(8,128)(2,1)}, f32[32,1024]{1,0:T(8,128)}, f32[32,8448]{1,0:T(8,128)}) custom-call(bf16[768,1024]{1,0:T(8,128)(2,1)} %get-tuple-element.53.refs_0_, f32[32,1024]{1,0:T(8,128)} %copy-done, bf16[1024,1024]{1,0:T(8,128)(2,1)} %bitcast.66, ...), custom_call_target="tpu_custom_call" | custom-call | tf_op jit(solution)/shard_map/pallas_call | solution.py:797
  349.6 1.2 broadcast_select_fusion.refs_7_
  350.8 96.7 %shard_map.300 = (f32[32,3072]{1,0:T(8,128)}, f32[32,1024]{1,0:T(8,128)}, f32[32,128]{1,0:T(8,128)}, bf16[32,48,512]{2,1,0:T(8,128)(2,1)}) custom-call(f32[768,1024]{1,0:T(8,128)} %get-tuple-element.51.refs_0_, bf16[768,1024]{1,0:T(8,128)(2,1)} %get-tuple-element.169.refs_0_.refs_1_, f32[32,1024]{1,0:T(8,128)} %copy-done, bf16[1024,3072]{1,0:T(8,128)(2,1)} %bitcast.63, ...), custom_call_target="tpu_custom_call" | custom-call | tf_op jit(solution)/shard_map/pallas_call | solution.py:941
  447.8 3.2 fusion.12
  451.0 1.7 fusion.11
  452.8 1.6 copy.97
  454.4 0.8 fusion.41
  455.8 2.8 slice_reduce_fusion
  458.7 0.9 copy.103
  459.6 0.9 copy.101
  460.5 0.9 copy.102
  461.6 0.7 copy.92
  462.2 0.7 copy.93
  462.9 0.7 copy.94
  463.6 0.7 copy.91
  464.3 0.7 slice_reduce_fusion.3
  465.0 0.7 slice_reduce_fusion.5
  465.7 1.1 copy.109
  466.8 0.7 copy.110
  (112 shorter events, 6.0 us)
Async XLA Ops:
  6.0 4.1 copy-start.11
  6.1 4.1 copy-start.12
  6.1 4.1 copy-start.13
  6.1 4.8 %copy-start.22 = (bf16[4]{0:T(256)(128)(2,1)S(1)}, bf16[4]{0:T(256)(128)(2,1)}, u32[]{:S(2)}) copy-start(bf16[4]{0:T(256)(128)(2,1)} %param.30) | copy-start | bytes 28
  6.1 4.8 %copy-start.14 = (bf16[32,8]{0,1:T(8,128)(2,1)S(1)}, bf16[32,8]{0,1:T(8,128)(2,1)}, u32[]{:S(2)}) copy-start(bf16[32,8]{0,1:T(8,128)(2,1)} %param.26) | copy-start | bytes 1540
  6.1 4.8 %copy-start.15 = (bf16[4,32]{1,0:T(4,128)(2,1)S(1)}, bf16[4,32]{1,0:T(4,128)(2,1)}, u32[]{:S(2)}) copy-start(bf16[4,32]{1,0:T(4,128)(2,1)} %param.27) | copy-start | bytes 772
  6.1 4.8 %copy-start.16 = (bf16[4,32]{1,0:T(4,128)(2,1)S(1)}, bf16[4,32]{1,0:T(4,128)(2,1)}, u32[]{:S(2)}) copy-start(bf16[4,32]{1,0:T(4,128)(2,1)} %param.28) | copy-start | bytes 772
  6.1 4.8 %copy-start.17 = (bf16[4,32]{1,0:T(4,128)(2,1)S(1)}, bf16[4,32]{1,0:T(4,128)(2,1)}, u32[]{:S(2)}) copy-start(bf16[4,32]{1,0:T(4,128)(2,1)} %param.29) | copy-start | bytes 772
  6.1 4.8 %copy-start.18 = (bf16[32]{0:T(256)(128)(2,1)S(1)}, bf16[32]{0:T(256)(128)(2,1)}, u32[]{:S(2)}) copy-start(bf16[32]{0:T(256)(128)(2,1)} %param.22) | copy-start | bytes 196
  6.2 4.8 %copy-start.19 = (bf16[32]{0:T(256)(128)(2,1)S(1)}, bf16[32]{0:T(256)(128)(2,1)}, u32[]{:S(2)}) copy-start(bf16[32]{0:T(256)(128)(2,1)} %param.32) | copy-start | bytes 196
  103.3 3.0 copy-start.21
  106.3 1.4 copy-start.2
  107.7 2.2 copy-start.10
  110.0 2.2 copy-start.6
  110.2 2.2 copy-start.7
  110.2 2.2 copy-start.8
  111.2 1.5 copy-start
  447.8 3.2 copy-start.20
  452.8 1.6 copy-start.5
  452.8 2.4 copy-start.3
  458.6 2.9 copy-start.4
  458.6 7.0 %copy-start.1 = (bf16[768,1024]{1,0:T(8,128)(2,1)S(1)}, bf16[768,1024]{1,0:T(8,128)(2,1)}, u32[]{:S(2)}) copy-start(bf16[768,1024]{1,0:T(8,128)(2,1)} %get-tuple-element.50) | copy-start | bytes 4718596
  465.7 1.1 copy-start.9

commit v3 on v1

--- a/solution.py
+++ b/solution.py
@@ -15,9 +15,16 @@
 UNIT_EPS = 1e-06
 MESH = pl.DeviceIdType.MESH
 F32, BF16 = jnp.float32, jnp.bfloat16
-VMEM_LIMIT = 61440 * 1024
+VMEM_LIMIT = 62 * 1024 * 1024
 FFW = 256
+WIDE = 3 * FFW
+HALF = WIDE // 2
 Z, Y, X, C = 0, 1, 2, 3
+ZXY, ZYX = (Z, X, Y, C), (Z, Y, X, C)
+CXYZ, CYXZ = (C, X, Y, Z), (C, Y, X, Z)
+GATHER_TICKS = (0, 2, 4, 6, 8)
+SCATTER_TICKS = (0, 1, 3, 5, 7)
+SLOTS = (4, 6, 6, 4)
 
 ROW_CONV, ROW_ATTN, ROW_MLP, ROW_OUT, ROW_BETA, SMALL_ROWS = 0, 12, 13, 14, 16, 32
 
@@ -53,6 +60,10 @@
     return moved
 
 
+def axis_peers(dims, cs):
+    return [index_of(dims, along(dims, cs, a, d)) for a in range(4) for d in range(1, dims[a])]
+
+
 def greet_all(n, me):
     barrier = pltpu.get_barrier_semaphore()
 
@@ -66,26 +77,35 @@
     pl.semaphore_wait(barrier, n - 1)
 
 
-def greet_axes(dims, cs):
-    barrier = pltpu.get_barrier_semaphore()
-    count = 0
-    for axis in range(4):
-        for delta in range(1, dims[axis]):
-            to = index_of(dims, along(dims, cs, axis, delta))
-            pl.semaphore_signal(barrier, inc=1, device_id=(to,), device_id_type=MESH)
-            count += 1
-    pl.semaphore_wait(barrier, count)
-
-
 def hops(dims):
     return sum(d - 1 for d in dims)
 
 
+def guard(condition, act):
+    if isinstance(condition, bool):
+        if condition:
+            act()
+    else:
+        pl.when(condition)(act)
+
+
+def run_tick(segments, ticks, tick):
+    for stage in reversed(range(len(ticks))):
+        i = tick - ticks[stage]
+        for make, first, end in segments:
+            inside = (first <= i < end) if isinstance(i, int) else (i >= first) & (i < end)
+
+            def act(make=make, i=i, stage=stage):
+                for job in make(i):
+                    job.step(stage)
+
+            guard(inside, act)
+
+
 class Gather:
-    def __init__(self, dims, cs, shard, out, low, width, order, sems):
-        self.dims, self.cs, self.order = dims, cs, order
-        self.columns = pl.ds(low, width)
-        self.shard, self.out = shard.at[:, self.columns], out
+    def __init__(self, dims, cs, shard, out, columns, order, sems):
+        self.dims, self.cs, self.order, self.columns = dims, cs, order, columns
+        self.shard, self.out = shard.at[:, columns], out
         self.send, self.recv, self.local = sems
 
     def slot(self, stage, delta):
@@ -132,127 +152,12 @@
                 c.wait_send()
 
 
-ZXY, ZYX, XYZ, YXZ = (Z, X, Y, C), (Z, Y, X, C), (X, Y, Z, C), (Y, X, Z, C)
-
-
-def pipelined(jobs, stages, lag):
-    for tick in range(len(jobs) + (stages - 1) * lag):
-        for stage in range(stages):
-            i = tick - stage * lag
-            if 0 <= i < len(jobs):
-                jobs[i].step(stage)
-
-
-class Tokens:
-    def __init__(self, n, me, a, b, send, recv, local):
-        self.n, self.me, self.a, self.b = n, me, a, b
-        self.send, self.recv, self.local = send, recv, local
-
-    def copy(self, d, incoming):
-        to = lax.rem(self.me + d, self.n)
-        frm = lax.rem(self.me - d + self.n, self.n)
-        return pltpu.make_async_remote_copy(
-            src_ref=self.a.at[to],
-            dst_ref=self.b.at[frm if incoming else self.me],
-            send_sem=self.send.at[d],
-            recv_sem=self.recv.at[d],
-            device_id=(to,),
-            device_id_type=MESH,
-        )
-
-    def keep(self):
-        return pltpu.make_async_copy(self.a.at[self.me], self.b.at[self.me], self.local)
-
-    def each(self, act):
-        def body(d, carry):
-            act(d)
-            return carry
-
-        lax.fori_loop(1, self.n, body, 0)
-
-    def start(self):
-        self.keep().start()
-        self.each(lambda d: self.copy(d, False).start())
-
-    def wait(self):
-        self.keep().wait()
-        self.each(lambda d: self.copy(d, True).wait_recv())
-        self.each(lambda d: self.copy(d, False).wait_send())
-
-
-def gather_kernel(dims, plan, lag, count, with_tokens, *refs):
-    n = math.prod(dims)
-    t = 1 if with_tokens else 0
-    ins, outs, scr = refs[: count + t], refs[count + t : 2 * (count + t)], refs[2 * (count + t) :]
-    send, recv, local = scr[:3]
-    me = lax.axis_index("fsdp")
-    cs = coords_of(dims, me)
-    if with_tokens:
-        greet_all(n, me)
-        tokens = Tokens(n, me, ins[count], outs[count], *scr[3:])
-        tokens.start()
-    else:
-        greet_axes(dims, cs)
-    jobs = [
-        Gather(dims, cs, ins[a], outs[a], low, width, order, (send.at[i], recv.at[i], local.at[i]))
-        for i, (a, low, width, order) in enumerate(plan)
-    ]
-    pipelined(jobs, 5, lag)
-    for j in jobs:
-        j.finish()
-    if with_tokens:
-        tokens.wait()
-
-
-def any_spec():
-    return pl.BlockSpec(memory_space=pl.ANY)
-
-
-def vmem_spec():
-    return pl.BlockSpec(memory_space=pltpu.VMEM)
-
-
-def token_sems(n):
-    return [
-        pltpu.SemaphoreType.DMA((n,)),
-        pltpu.SemaphoreType.DMA((n,)),
-        pltpu.SemaphoreType.DMA,
-    ]
-
-
-def gather_call(shards, tokens, plan, lag, collective_id):
-    n = lax.axis_size("fsdp")
-    dims = grid_of(n)
-    k = hops(dims)
-    ins = list(shards) + ([] if tokens is None else [tokens])
-    outs = [jax.ShapeDtypeStruct(dims + s.shape, s.dtype) for s in shards]
-    if tokens is not None:
-        outs.append(jax.ShapeDtypeStruct(tokens.shape, tokens.dtype))
-    m = len(plan)
-    return pl.pallas_call(
-        functools.partial(gather_kernel, dims, plan, lag, len(shards), tokens is not None),
-        out_shape=outs,
-        in_specs=[any_spec()] * len(ins),
-        out_specs=[any_spec()] * len(outs),
-        scratch_shapes=[
-            pltpu.SemaphoreType.DMA((m, k)),
-            pltpu.SemaphoreType.DMA((m, k)),
-            pltpu.SemaphoreType.DMA((m,)),
-        ]
-        + ([] if tokens is None else token_sems(n)),
-        compiler_params=pltpu.CompilerParams(
-            collective_id=collective_id, has_side_effects=True, vmem_limit_bytes=VMEM_LIMIT
-        ),
-    )(*ins)
-
-
 class Scatter:
-    def __init__(self, dims, cs, terms, result, low, width, order, scratch, sems):
+    def __init__(self, dims, cs, terms, term_columns, result, columns, order, got, sems):
         self.dims, self.cs, self.order = dims, cs, order
-        self.columns = pl.ds(low, width)
-        self.terms, self.result = terms, result
-        self.own, self.got = scratch[0], scratch[1:]
-        self.send, self.recv, self.local = sems
+        self.term_columns, self.columns = term_columns, columns
+        self.terms, self.result, self.got = terms, result, got
+        self.send, self.recv = sems
 
     def slot(self, stage, delta):
         return sum(self.dims[a] - 1 for a in self.order[:stage]) + delta - 1
@@ -261,7 +166,7 @@
         axis = self.order[stage]
         if stage == 0:
             lead = tuple(at if k == axis else slice(None) for k in range(4))
-            return self.terms.at[lead + (slice(None), self.columns)]
+            return self.terms.at[lead + (slice(None), self.term_columns)]
         left = [k for k in range(4) if k not in self.order[:stage]]
         return self.got[stage - 1].at[(0,) + tuple(at if k == axis else slice(None) for k in left)]
 
@@ -279,8 +184,1030 @@
                 device_id_type=MESH,
             )
 
+    def total(self, stage):
+        axis = self.order[stage]
+        left = [k for k in range(4) if k not in self.order[: stage + 1]]
+        shape = [self.dims[k] for k in left]
+        got = self.got[stage]
+        mine = self.part(stage, self.cs[axis])
+
+        def one(i, carry):
+            at = tuple(coords_of(shape, i)) if shape else ()
+            total = mine[at + (slice(None), slice(None))].astype(F32)
+            for delta in range(1, self.dims[axis]):
+                total += got[(delta - 1,) + at + (slice(None), slice(None))].astype(F32)
+            if left:
+                got[(0,) + at + (slice(None), slice(None))] = total.astype(got.dtype)
+            else:
+                self.result[:, self.columns] = total
+            return carry
+
+        lax.fori_loop(0, math.prod(shape), one, 0)
+
+    def step(self, stage):
+        if stage >= 1:
+            for c in self.copies(stage - 1):
+                c.wait()
+            self.total(stage - 1)
+        if stage < 4:
+            for c in self.copies(stage):
+                c.start()
+
+
+def scatter_scratch(dims, rows, width, order, dtype, slots=None):
+    out = []
+    for s, axis in enumerate(order):
+        rest = tuple(dims[k] for k in range(4) if k not in order[: s + 1])
+        lead = () if slots is None else (slots[s],)
+        out.append(pltpu.VMEM(lead + (dims[axis] - 1,) + rest + (rows, width), dtype))
+    return out
+
+
+class Tokens:
+    def __init__(self, n, me, rows, a, b, send, recv, local):
+        self.n, self.me, self.rows, self.a, self.b = n, me, rows, a, b
+        self.send, self.recv, self.local = send, recv, local
+
+    def block(self, d):
+        return pl.ds(pl.multiple_of(d * self.rows, self.rows), self.rows)
+
+    def copy(self, d, incoming):
+        to = lax.rem(self.me + d, self.n)
+        frm = lax.rem(self.me - d + self.n, self.n)
+        return pltpu.make_async_remote_copy(
+            src_ref=self.a.at[self.block(to)],
+            dst_ref=self.b.at[self.block(frm if incoming else self.me)],
+            send_sem=self.send.at[d],
+            recv_sem=self.recv.at[d],
+            device_id=(to,),
+            device_id_type=MESH,
+        )
+
     def keep(self):
-        return pltpu.make_async_copy(self.part(0, self.cs[self.order[0]]), self.own, self.local)
+        at = self.block(self.me)
+        return pltpu.make_async_copy(self.a.at[at], self.b.at[at], self.local)
+
+    def each(self, act):
+        def body(d, carry):
+            act(d)
+            return carry
+
+        lax.fori_loop(1, self.n, body, 0)
+
+    def start(self):
+        self.keep().start()
+        self.each(lambda d: self.copy(d, False).start())
+
+    def wait(self):
+        self.keep().wait()
+        self.each(lambda d: self.copy(d, True).wait_recv())
+        self.each(lambda d: self.copy(d, False).wait_send())
+
+
+def any_spec():
+    return pl.BlockSpec(memory_space=pl.ANY)
+
+
+def vmem_spec():
+    return pl.BlockSpec(memory_space=pltpu.VMEM)
+
+
+def dot(a, b):
+    return lax.dot_general(a, b, (((1,), (0,)), ((), ())), preferred_element_type=F32)
+
+
+def dot_nt(a, b):
+    return lax.dot_general(a, b, (((1,), (1,)), ((), ())), preferred_element_type=F32)
+
+
+def dot_tn(a, b):
+    return lax.dot_general(a, b, (((0,), (0,)), ((), ())), preferred_element_type=F32)
+
+
+def low(v):
+    return v.astype(BF16)
+
+
+def lanes(i, width=HEAD):
+    return slice(i * width, (i + 1) * width)
+
+
+def place(kind, h):
+    at = (h // 2) * WIDE + kind * 2 * HEAD + (h % 2) * HEAD
+    return slice(at, at + HEAD)
+
+
+def shifted(values, by, row):
+    if by == 0:
+        return values
+    rows = values.shape[0]
+    moved = pltpu.roll(values, by % rows, 0)
+    return jnp.where(row >= by if by > 0 else row < rows + by, moved, 0.0)
+
+
+def head_sum(values):
+    return jnp.sum(values, axis=-1, keepdims=True)
+
+
+def rms(v):
+    return lax.rsqrt(jnp.mean(v * v, axis=-1, keepdims=True) + NORM_EPS)
+
+
+def rms_back(d, v, r, gain):
+    vr, gd = v * r, d * gain
+    return r * (gd - vr * jnp.mean(vr * gd, axis=-1, keepdims=True)), d * vr
+
+
+def iotas(shape):
+    return lax.broadcasted_iota(jnp.int32, shape, 0), lax.broadcasted_iota(jnp.int32, shape, 1)
+
+
+def level_masks():
+    i, j = iotas((SPAN, SPAN))
+    found = []
+    for level in range(SPAN.bit_length() - 1):
+        a, b = i >> level, j >> level
+        found.append(((a >> 1) == (b >> 1)) & ((a & 1) == 1) & ((b & 1) == 0))
+    return found
+
+
+def column(row):
+    return jnp.broadcast_to(row, (HEAD, HEAD)).T
+
+
+def hot(index, count):
+    lane = lax.broadcasted_iota(jnp.int32, (HEAD, HEAD), 1).astype(F32)
+    return jnp.concatenate(
+        [low(jnp.where(lane + float(HEAD * b) == index, 1.0, 0.0)) for b in range(count // HEAD)], axis=1
+    )
+
+
+def prepare(x, taps, unit, row):
+    c = x * taps[0:1]
+    for o in range(1, taps.shape[0]):
+        c += shifted(x, o, row) * taps[o : o + 1]
+    u = c * jax.nn.sigmoid(c)
+    if unit:
+        u = jnp.concatenate(
+            [
+                u[:, lanes(h)] * lax.rsqrt(head_sum(u[:, lanes(h)] * u[:, lanes(h)]) + UNIT_EPS)
+                for h in range(x.shape[1] // HEAD)
+            ],
+            axis=1,
+        )
+    return u
+
+
+def prepare_back(x, d, taps, unit, row):
+    moved = [shifted(x, o, row) for o in range(taps.shape[0])]
+    c = moved[0] * taps[0:1]
+    for o in range(1, taps.shape[0]):
+        c += moved[o] * taps[o : o + 1]
+    s = jax.nn.sigmoid(c)
+    u = c * s
+    if unit:
+        n = lax.rsqrt(head_sum(u * u) + UNIT_EPS)
+        un = u * n
+        d = (d - un * head_sum(un * d)) * n
+    d = d * (s + u * (1.0 - s))
+    grads = [jnp.sum(m * d, axis=0, keepdims=True) for m in moved]
+    back = d * taps[0:1]
+    for o in range(1, taps.shape[0]):
+        back += shifted(d, -o, row) * taps[o : o + 1]
+    return back, grads
+
+
+def delta_block(base, first, refs, gain):
+    qkv, beta, state, states, inverses, scores, fresh, mix, mixed, at = refs
+    rows = pl.ds(base, SPAN)
+    i, j = iotas((SPAN, SPAN))
+    masks = level_masks()
+    eye = jnp.where(i == j, 1.0, 0.0).astype(F32)
+    heads = range(HEADS)
+
+    @pl.when(first)
+    def _():
+        state[...] = jnp.zeros_like(state)
+
+    strength = beta[rows, :]
+    q, k = ([qkv[rows, place(kind, h)] for h in heads] for kind in range(2))
+    b = [strength[:, h : h + 1] for h in heads]
+    strict = [low(jnp.where(i > j, dot_nt(k[h], k[h]) * b[h], 0.0)) for h in heads]
+    for h in heads:
+        scores[at, h] = low(jnp.where(i >= j, dot_nt(q[h], k[h]), 0.0))
+    zero = jnp.zeros((), BF16)
+    inv = [eye - jnp.where(masks[0], strict[h], zero).astype(F32) for h in heads]
+    for level in range(1, len(masks)):
+        t = [low(inv[h]) for h in heads]
+        f = [low(dot(jnp.where(masks[level], strict[h], zero), t[h])) for h in heads]
+        inv = [inv[h] - dot(t[h], f[h]) for h in heads]
+    for h in heads:
+        inverses[at, h] = low(inv[h])
+    s = [low(state[h]) for h in heads]
+    for h in heads:
+        states[at, h] = s[h]
+    rest = [low((qkv[rows, place(2, h)].astype(F32) - dot(k[h], s[h])) * b[h]) for h in heads]
+    new = [low(dot(inverses[at, h], rest[h])) for h in heads]
+    out = [dot(q[h], s[h]) + dot(scores[at, h], new[h]) for h in heads]
+    for h in heads:
+        fresh[rows, lanes(h)] = new[h]
+        state[h] += dot_tn(k[h], new[h])
+        mix[rows, lanes(h)] = low(out[h])
+        mixed[rows, lanes(h)] = low(out[h] * rms(out[h]) * gain)
+
+
+def delta_back(base, last, refs, gain):
+    (qkv, beta, states, inverses, scores, fresh, mix, d_mixed,
+     d_state, d_q, d_k, d_v, d_beta, gain_grad, at) = refs
+    rows = pl.ds(base, SPAN)
+    i, j = iotas((SPAN, SPAN))
+    lane = lax.broadcasted_iota(jnp.int32, (SPAN, 16), 1)
+    heads = range(HEADS)
+
+    @pl.when(last)
+    def _():
+        d_state[...] = jnp.zeros_like(d_state)
+
+    strength = beta[rows, :]
+    q, k = ([qkv[rows, place(kind, h)] for h in heads] for kind in range(2))
+    e = [fresh[rows, lanes(h)] for h in heads]
+    b = [strength[:, h : h + 1] for h in heads]
+    kb = [low(k[h].astype(F32) * b[h]) for h in heads]
+    do = []
+    for h in heads:
+        v = mix[rows, lanes(h)].astype(F32)
+        d, terms = rms_back(d_mixed[:, lanes(h)], v, rms(v), gain)
+        gain_grad[...] += jnp.sum(terms, axis=0, keepdims=True)
+        do.append(low(d))
+    s = [states[at, h] for h in heads]
+    p = [scores[at, h] for h in heads]
+    ds = [low(d_state[h]) for h in heads]
+    de = [low(dot_tn(p[h], do[h]) + dot(k[h], ds[h])) for h in heads]
+    dx = [dot_tn(inverses[at, h], de[h]) for h in heads]
+    dxl = [low(dx[h]) for h in heads]
+    dp = [low(jnp.where(i >= j, dot_nt(do[h], e[h]), 0.0)) for h in heads]
+    da = [low(jnp.where(i > j, -dot_nt(dxl[h], e[h]), 0.0)) for h in heads]
+    dkb = [dot(da[h], k[h]) - dot_nt(dxl[h], s[h]) for h in heads]
+    beta_grad = jnp.zeros((SPAN, 16), F32)
+    for h in heads:
+        d_q[rows, lanes(h)] = dot_nt(do[h], s[h]) + dot(dp[h], k[h])
+        d_k[rows, lanes(h)] = (
+            dkb[h] * b[h] + dot_tn(da[h], kb[h]) + dot_tn(dp[h], q[h]) + dot_nt(e[h], ds[h])
+        )
+        d_v[rows, lanes(h)] = low(dx[h] * b[h])
+        d_state[h] += dot_tn(q[h], do[h]) - dot_tn(kb[h], dxl[h])
+        v = qkv[rows, place(2, h)].astype(F32)
+        db = head_sum(dkb[h] * k[h].astype(F32) + dx[h] * v)
+        beta_grad += jnp.where(lane == h, db, 0.0)
+    d_beta[rows, :] = low(beta_grad * strength * (1.0 - strength))
+
+
+def block_kernel(dims, micro, length, steps, token_rows, *refs):
+    (tokens_in, take, back, grad_in, small_shard, qkv_shard, out_shard, feed_shard,
+     result, returned, feed_grad, qkv_grad, out_grad, small_grad,
+     small_all, qkv_all, out_all, feed_all,
+     own, attn_low, pre, qkv, beta, states, inverses, scores, fresh, mix, mixed,
+     hidden, total, d_hidden, norm, grad, bufs, w_out, state, d_out, tok_buf, small_buf, small, small_terms,
+     gain_out, d_beta, small_out,
+     g_send, g_recv, g_local, s_send, s_recv, t_send, t_recv, t_local, load_sem, ready, *got) = refs
+    n = math.prod(dims)
+    me = lax.axis_index("fsdp")
+    cs = coords_of(dims, me)
+    width = own.shape[1]
+    share = width // n
+    thin = tok_buf.shape[2]
+    parts = width // thin
+    slots = token_rows // parts
+    pieces = 3 * width // WIDE
+    blocks = length // SPAN
+    rows_total = micro * length
+    flat = dims + (share,)
+
+    def g_sems(i):
+        return g_send.at[i], g_recv.at[i], g_local.at[i]
+
+    def s_sems(i):
+        return s_send.at[i], s_recv.at[i]
+
+    def feed_columns(i, p=0, wide=WIDE):
+        return pl.ds(pl.multiple_of(i * WIDE + p * HALF, HALF), wide)
+
+    def feed_gather(i):
+        for p, order in enumerate((ZXY, ZYX)):
+            yield Gather(dims, cs, feed_shard, feed_all, feed_columns(i, p, HALF), order, g_sems(2 * i + p))
+
+    first_gather = 2 * steps
+    attn_gather = [Gather(dims, cs, small_shard, small_all, pl.ds(0, HEAD), ZXY, g_sems(first_gather))]
+    for i in range(2 * pieces):
+        attn_gather.append(Gather(
+            dims, cs, qkv_shard, qkv_all, pl.ds(i * HALF, HALF), (ZXY, ZYX)[i % 2],
+            g_sems(first_gather + 1 + i),
+        ))
+    half_out = width // 2
+    out_gather = [
+        Gather(dims, cs, out_shard, out_all, pl.ds(i * half_out, half_out), (ZXY, ZYX)[i],
+               g_sems(first_gather + 1 + 2 * pieces + i))
+        for i in range(2)
+    ]
+    gathers = [(feed_gather, 0, steps)]
+
+    def slot_views(i, p, wide):
+        for s in range(4):
+            ref = got[4 * p + s]
+            lead = (lax.rem(i, SLOTS[s]),) + (slice(None),) * (len(ref.shape) - 2)
+            yield ref.at[lead + (pl.ds(0, wide),)]
+
+    def scatter(i, source, source_at, target, at, wide, sem):
+        for p, order in enumerate((CXYZ, CYXZ)):
+            yield Scatter(
+                dims, cs, source, pl.ds(source_at + p * wide, wide), target,
+                pl.ds(pl.multiple_of(at + p * wide, HEAD), wide), order,
+                list(slot_views(i, p, wide)), s_sems(sem + p),
+            )
+
+    def feed_scatter(i):
+        return scatter(i, bufs.at[lax.rem(i, 2)], 0, feed_grad, i * WIDE, HALF, 2 * i)
+
+    rest = width - WIDE
+    first_out = 2 * steps
+
+    def out_scatter(i):
+        return scatter(steps, bufs.at[steps % 2], 0, out_grad, 0, HALF, first_out)
+
+    def out_scatter_rest(i):
+        return scatter(steps + 1, bufs.at[(steps + 1) % 2], 0, out_grad, WIDE, rest // 2, first_out + 2)
+
+    scatters = [
+        (feed_scatter, 0, steps), (out_scatter, steps, steps + 1), (out_scatter_rest, steps + 1, steps + 2)
+    ]
+    first_qkv = first_out + 4
+
+    def qkv_scatter(i):
+        yield from scatter(i, bufs.at[i], 0, qkv_grad, i * WIDE, HALF, first_qkv + 2 * i)
+
+    def small_scatter(i):
+        yield Scatter(
+            dims, cs, small_out, pl.ds(0, HEAD), small_grad, pl.ds(0, HEAD), CXYZ, got[8:12],
+            s_sems(first_qkv + 2 * pieces),
+        )
+
+    tail_scatters = [(qkv_scatter, 0, pieces), (small_scatter, pieces, pieces + 1)]
+
+    def tokens_to(m):
+        return Tokens(n, me, token_rows, tokens_in.at[m], tok_buf.at[m], t_send.at[m], t_recv.at[m], t_local.at[m])
+
+    def tokens_back(m):
+        k = micro + m
+        return Tokens(n, me, token_rows, tok_buf.at[m], returned.at[m], t_send.at[k], t_recv.at[k], t_local.at[k])
+
+    def load_qkv(i):
+        return pltpu.make_async_copy(
+            qkv_all.at[:, :, :, :, :, pl.ds(i * WIDE, WIDE)], bufs.at[i], load_sem.at[i]
+        )
+
+    load_out = pltpu.make_async_copy(out_all, w_out, load_sem.at[pieces])
+    load_small = pltpu.make_async_copy(small_all, small_buf, load_sem.at[pieces + 1])
+    load_grad = pltpu.make_async_copy(grad_in, grad, load_sem.at[pieces + 2])
+    store_result = pltpu.make_async_copy(grad, result, load_sem.at[pieces + 2])
+
+    def load_feed(t):
+        slot = lax.rem(t, 2)
+        return pltpu.make_async_copy(
+            feed_all.at[:, :, :, :, :, feed_columns(t)], bufs.at[2 + slot], load_sem.at[pieces + 3 + slot]
+        )
+
+    load_grad.start()
+    greet_all(n, me)
+    tokens_to(0).start()
+    segment = [(lambda i: [attn_gather[i]], 0, len(attn_gather))]
+    last = len(attn_gather) + GATHER_TICKS[-1]
+    early = 0
+    for t in range(last):
+        run_tick(segment, GATHER_TICKS, t)
+        if t == len(attn_gather) - 1:
+            for m in range(1, micro):
+                tokens_to(m).start()
+        if t >= len(attn_gather) and (last - 1 - t) % 2 == 0 and early < EARLY:
+            run_tick(gathers, GATHER_TICKS, early)
+            early += 1
+        if t == GATHER_TICKS[-1]:
+            load_small.start()
+        for i in range(pieces):
+            if t == 2 * i + 2 + GATHER_TICKS[-1]:
+                load_qkv(i).start()
+    load_small.wait()
+    blockwise = small_buf[...].reshape(width, HEAD).astype(F32)
+    small[...] = blockwise.T[:SMALL_ROWS]
+    i, j = iotas((width, HEAD))
+    few = HEAD // n
+    mine = (lax.rem(i, share) < few) & ((i // share) * few + lax.rem(i, share) == j)
+    gain_out[...] = jnp.sum(
+        jnp.where(mine, blockwise[:, ROW_OUT : ROW_OUT + 1], 0.0), axis=0, keepdims=True
+    )
+    for i in range(pieces):
+        load_qkv(i).wait()
+
+    gain_attn = small[ROW_ATTN : ROW_ATTN + 1, :]
+    gain_mlp = small[ROW_MLP : ROW_MLP + 1, :]
+    beta_rows = low(small[ROW_BETA : ROW_BETA + 16, :])
+    row2 = lax.broadcasted_iota(jnp.int32, (length, 2 * HEAD), 0)
+    row1 = lax.broadcasted_iota(jnp.int32, (length, HEAD), 0)
+
+    def project(m, carry):
+        run_tick(gathers, GATHER_TICKS, early + m)
+        tokens_to(m).wait()
+
+        def arrive(t, carry):
+            at = pl.ds(pl.multiple_of(t * SPAN, SPAN), SPAN)
+            index = column(take[pl.ds(t, 1), :])
+            for p in range(parts):
+                cols = lanes(p, thin)
+                pick = hot(jnp.where(index >= 0.0, index + float(p * slots), -1.0), n * token_rows)
+                own[at, cols] = low(dot(pick, tok_buf[m]))
+            v = own[at, :].astype(F32)
+            attn_low[at, :] = low(v * rms(v) * gain_attn)
+            return carry
+
+        lax.fori_loop(m * blocks, (m + 1) * blocks, arrive, 0)
+        rows = pl.ds(pl.multiple_of(m * length, SPAN), length)
+        a = attn_low[rows, :]
+        beta[rows, :] = jax.nn.sigmoid(dot_nt(a, beta_rows))
+        for b in range(pieces):
+            for kind in range(3):
+                cols = lanes(kind, 2 * HEAD)
+                wide = slice(b * WIDE + cols.start, b * WIDE + cols.stop)
+                x = dot(a, bufs[b, :, :, :, :, :, cols].reshape(width, 2 * HEAD))
+                pre[rows, wide] = low(x)
+                taps = small[4 * kind : 4 * kind + 4, lanes(b, 2 * HEAD)]
+                qkv[rows, wide] = low(prepare(x, taps, kind < 2, row2))
+        return carry
+
+    lax.fori_loop(0, micro, project, 0)
+
+    def forward(t, carry):
+        run_tick(gathers, GATHER_TICKS, early + micro + t)
+        for s in range(5):
+
+            @pl.when(t == s)
+            def _(s=s):
+                for g in out_gather:
+                    g.step(s)
+
+        base = pl.multiple_of(t * SPAN, SPAN)
+        delta_block(
+            base, lax.rem(t, blocks) == 0,
+            (qkv, beta, state, states, inverses, scores, fresh, mix, mixed, t), gain_out[...],
+        )
+        return carry
+
+    lax.fori_loop(0, micro * blocks, forward, 0)
+    load_out.start()
+    begun = early + micro + micro * blocks
+    load_feed(0).start()
+    load_out.wait()
+
+    def enter(t, carry):
+        at = pl.ds(pl.multiple_of(t * SPAN, SPAN), SPAN)
+        v = own[at, :].astype(F32) + dot_nt(mixed[at, :], w_out[...].reshape(width, width))
+        hidden[at, :] = v
+        norm[at, :] = low(v * rms(v) * gain_mlp)
+        return carry
+
+    lax.fori_loop(0, micro * blocks, enter, 0)
+    load_grad.wait()
+    total[...] = jnp.zeros_like(total)
+    d_hidden[...] = jnp.zeros_like(d_hidden)
+
+    def feed(t, carry):
+        run_tick(gathers, GATHER_TICKS, begun + t)
+
+        @pl.when(t + 1 < steps)
+        def _():
+            load_feed(t + 1).start()
+
+        load_feed(t).wait()
+        w = bufs.at[2 + lax.rem(t, 2)]
+        terms = bufs.at[lax.rem(t, 2)]
+        gw, uw, dw = (w[:, :, :, :, :, lanes(i, FFW)].reshape(width, FFW) for i in range(3))
+        x, g = norm[...], grad[...]
+        gate, up = dot(x, gw), dot(x, uw)
+        d_act = dot(g, dw)
+        s = jax.nn.sigmoid(gate)
+        silu = gate * s
+        act = low(silu * up)
+        d_gate = low(d_act * up * (s + silu * (1.0 - s)))
+        d_up = low(d_act * silu)
+        for b in range(width // FFW):
+            cols = lanes(b, FFW)
+            total[:, cols] += dot_nt(act, dw[cols])
+            d_hidden[:, cols] += dot_nt(d_gate, gw[cols]) + dot_nt(d_up, uw[cols])
+        for i, (left, right) in enumerate(((x, d_gate), (x, d_up), (g, act))):
+            terms[:, :, :, :, :, lanes(i, FFW)] = low(dot_tn(left, right)).reshape(flat + (FFW,))
+        run_tick(scatters, SCATTER_TICKS, t)
+        return carry
+
+    lax.fori_loop(0, steps, feed, 0)
+    small_terms[...] = jnp.zeros_like(small_terms)
+
+    def leave(t, carry):
+        at = pl.ds(pl.multiple_of(t * SPAN, SPAN), SPAN)
+        v, g = hidden[at, :], grad[at, :].astype(F32)
+        grad[at, :] = low(v + total[at, :])
+        d, terms = rms_back(d_hidden[at, :], v, rms(v), gain_mlp)
+        small_terms[ROW_MLP : ROW_MLP + 1, :] += jnp.sum(terms, axis=0, keepdims=True)
+        d_hidden[at, :] = g + d
+        norm[at, :] = low(g + d)
+        return carry
+
+    lax.fori_loop(0, micro * blocks, leave, 0)
+    store_result.start()
+    d_attn = d_v = norm
+
+    for b in range(width // 256):
+        slot, at = (steps + b * 256 // WIDE) % 2, b * 256 % WIDE
+        grads = low(dot_tn(d_attn[...], mixed[:, lanes(b, 256)]))
+        bufs[slot, :, :, :, :, :, at : at + 256] = grads.reshape(flat + (256,))
+        if b == WIDE // 256 - 1:
+            run_tick(scatters, SCATTER_TICKS, steps)
+    run_tick(scatters, SCATTER_TICKS, steps + 1)
+    d_q, d_k = hidden, total
+    begun_back = steps + 2
+
+    def backward(turn, carry):
+        m = micro - 1 - turn
+
+        def one(b, carry):
+            run_tick(scatters, SCATTER_TICKS, begun_back + turn * (blocks + 1) + b)
+            t = m * blocks + blocks - 1 - b
+            base = pl.multiple_of(t * SPAN, SPAN)
+            d_out[...] = dot(d_attn[pl.ds(base, SPAN), :], w_out[...].reshape(width, width))
+            delta_back(
+                base, b == 0,
+                (qkv, beta, states, inverses, scores, fresh, mix, d_out,
+                 state, d_q, d_k, d_v, d_beta, small_terms.at[ROW_OUT : ROW_OUT + 1, 0:HEAD], t),
+                gain_out[...],
+            )
+            return carry
+
+        lax.fori_loop(0, blocks, one, 0)
+        run_tick(scatters, SCATTER_TICKS, begun_back + turn * (blocks + 1) + blocks)
+
+        @pl.when(turn == 0)
+        def _():
+            for i in range(pieces):
+                load_qkv(i).start()
+
+        rows = pl.ds(pl.multiple_of(m * length, SPAN), length)
+        for kind, grads in enumerate((d_q, d_k, d_v)):
+            for h in range(HEADS):
+                at = place(kind, h)
+                back_rows, taps = prepare_back(
+                    pre[rows, at].astype(F32), grads[rows, lanes(h)].astype(F32),
+                    small[4 * kind : 4 * kind + 4, lanes(h)], kind < 2, row1,
+                )
+                qkv[rows, at] = low(back_rows)
+                for o, terms in enumerate(taps):
+                    small_terms[4 * kind + o : 4 * kind + o + 1, lanes(h)] += terms
+
+        @pl.when(turn == 0)
+        def _():
+            for i in range(pieces):
+                load_qkv(i).wait()
+
+        def depart(b, carry):
+            at = pl.ds(pl.multiple_of(m * length + b * SPAN, SPAN), SPAN)
+            d = dot(d_beta[at, :], beta_rows)
+            for i in range(pieces):
+                d += dot_nt(qkv[at, lanes(i, WIDE)], bufs[i].reshape(width, WIDE))
+            v = own[at, :].astype(F32)
+            d, terms = rms_back(d, v, rms(v), gain_attn)
+            small_terms[ROW_ATTN : ROW_ATTN + 1, :] += jnp.sum(terms, axis=0, keepdims=True)
+            own[at, :] = low(d_hidden[at, :] + d)
+            return carry
+
+        lax.fori_loop(0, blocks, depart, 0)
+        line = lax.broadcasted_iota(jnp.int32, (HEAD, length), 0)
+
+        def pack(b, carry):
+            pick = hot(column(back[pl.ds(m * (n * token_rows // HEAD) + b, 1), :]), length)
+            part = lax.rem(line + b * HEAD, token_rows) // slots
+            held = jnp.zeros((HEAD, thin), F32)
+            for p in range(parts):
+                held += dot(jnp.where(part == p, pick, jnp.zeros((), BF16)), own[rows, lanes(p, thin)])
+            tok_buf[m, pl.ds(pl.multiple_of(b * HEAD, HEAD), HEAD), :] = low(held)
+            return carry
+
+        lax.fori_loop(0, n * token_rows // HEAD, pack, 0)
+        tokens_back(m).start()
+        return carry
+
+    lax.fori_loop(0, micro, backward, 0)
+
+    for peer in axis_peers(dims, cs):
+        pl.semaphore_signal(ready, inc=1, device_id=(peer,), device_id_type=MESH)
+    for i in range(pieces):
+        for kind in range(3):
+            cols = lanes(kind, FFW)
+            grads = low(dot_tn(attn_low[...], qkv[:, i * WIDE + cols.start : i * WIDE + cols.stop]))
+            bufs[i, :, :, :, :, :, cols] = grads.reshape(flat + (FFW,))
+        if i == 0:
+            pl.semaphore_wait(ready, hops(dims))
+        run_tick(tail_scatters, SCATTER_TICKS, i)
+    i, j = iotas((HEAD, width))
+    mine = (lax.rem(j, share) < few) & ((j // share) * few + lax.rem(j, share) == i)
+    gain_column = column(small_terms[ROW_OUT : ROW_OUT + 1, :HEAD])[:, 0:1]
+    gain_row = jnp.sum(jnp.where(mine, gain_column, 0.0), axis=0, keepdims=True)
+    block = jnp.concatenate(
+        [small_terms[:ROW_OUT, :], gain_row, jnp.zeros((1, width), F32),
+         dot_tn(d_beta[...], attn_low[...]), jnp.zeros((HEAD - SMALL_ROWS, width), F32)], axis=0,
+    )
+    small_out[...] = block.T.reshape(flat + (HEAD,))
+    for t in range(pieces, pieces + 1 + SCATTER_TICKS[-1]):
+        run_tick(tail_scatters, SCATTER_TICKS, t)
+    for g in attn_gather + out_gather:
+        g.finish()
+
+    def finish(i, carry):
+        for g in feed_gather(i):
+            g.finish()
+        return carry
+
+    lax.fori_loop(0, steps, finish, 0)
+    store_result.wait()
+    for m in range(micro):
+        tokens_back(m).wait()
+
+
+EARLY = 3
+
+
+def block_call(tokens, take, back, grad, small_shard, qkv_shard, out_shard, feed_shard, micro):
+    rows, width = grad.shape
+    length, blocks = rows // micro, rows // SPAN
+    n = lax.axis_size("fsdp")
+    dims = grid_of(n)
+    k = hops(dims)
+    share = width // n
+    steps = feed_shard.shape[1] // WIDE
+    pieces = 3 * width // WIDE
+    token_rows = tokens.shape[1] // n
+    flat = dims + (share,)
+    shape = jax.ShapeDtypeStruct
+    outs = [
+        shape((rows, width), BF16), shape(tokens.shape, BF16),
+        shape(feed_shard.shape, F32), shape(qkv_shard.shape, F32), shape(out_shard.shape, F32), shape((share, HEAD), F32),
+        shape(dims + small_shard.shape, BF16), shape(dims + qkv_shard.shape, BF16), shape(dims + out_shard.shape, BF16),
+        shape(dims + feed_shard.shape, BF16),
+    ]
+    wide, full = pltpu.VMEM((rows, width), BF16), pltpu.VMEM((rows, width), F32)
+    square = pltpu.VMEM((blocks, HEADS, SPAN, SPAN), BF16)
+    gathers = 2 * steps + 1 + 2 * pieces + 2
+    scatters = 2 * steps + 4 + 2 * pieces + 1
+    dma = pltpu.SemaphoreType.DMA
+    scratch = [
+        wide, wide, pltpu.VMEM((rows, 3 * width), BF16), pltpu.VMEM((rows, 3 * width), BF16),
+        pltpu.VMEM((rows, 16), F32), pltpu.VMEM((blocks, HEADS, HEAD, HEAD), BF16), square, square, wide, wide, wide,
+        full, full, full, wide, wide, pltpu.VMEM((pieces,) + flat + (WIDE,), BF16), pltpu.VMEM(flat + (width,), BF16),
+        pltpu.VMEM((HEADS, HEAD, HEAD), F32), pltpu.VMEM((SPAN, width), F32), pltpu.VMEM(tokens.shape, BF16),
+        pltpu.VMEM(flat + (HEAD,), BF16), pltpu.VMEM((SMALL_ROWS, width), F32), pltpu.VMEM((SMALL_ROWS // 2, width), F32),
+        pltpu.VMEM((1, HEAD), F32), pltpu.VMEM((rows, 16), BF16),
+        pltpu.VMEM(flat + (HEAD,), F32),
+        dma((gathers, k)), dma((gathers, k)), dma((gathers,)), dma((scatters, k)), dma((scatters, k)),
+        dma((2 * micro, n)), dma((2 * micro, n)), dma((2 * micro,)), dma((pieces + 5,)), pltpu.SemaphoreType.REGULAR,
+    ]
+    for order in (CXYZ, CYXZ):
+        scratch += scatter_scratch(dims, share, HALF, order, BF16, SLOTS)
+    scratch += scatter_scratch(dims, share, HEAD, CXYZ, F32)
+    return pl.pallas_call(
+        functools.partial(block_kernel, dims, micro, length, steps, token_rows),
+        out_shape=outs,
+        in_specs=[any_spec(), vmem_spec(), vmem_spec()] + [any_spec()] * 5,
+        out_specs=[any_spec()] * 2 + [vmem_spec()] * 4 + [any_spec()] * 4,
+        scratch_shapes=scratch,
+        compiler_params=pltpu.CompilerParams(
+            collective_id=1, has_side_effects=True, vmem_limit_bytes=VMEM_LIMIT
+        ),
+    )(tokens, take, back, grad, small_shard, qkv_shard, out_shard, feed_shard)[:6]
+
+
+def picked(index, source):
+    hot_rows = index[:, None] == jnp.arange(source.shape[0], dtype=jnp.int32)[None, :]
+    return jnp.dot(low(hot_rows), source, preferred_element_type=F32).astype(BF16)
+
+
+def split_rows(values, parts):
+    cut = values.reshape(values.shape[:-1] + (parts, values.shape[-1] // parts))
+    return jnp.moveaxis(cut, -2, 0)
+
+
+def spans(width, size):
+    at = 0
+    while at < width:
+        yield at, min(size, width - at)
+        at += size
+
+
+def local(
+    inputs, cotangent, lengths, owners, attn_gain, query_weight, key_weight, value_weight, beta_weight,
+    query_conv, key_conv, value_conv, out_gain, out_weight, mlp_gain, gate_weight, up_weight, down_weight,
+):
+    n = lax.axis_size("fsdp")
+    me = lax.axis_index("fsdp")
+    micro, _, length, width = inputs.shape
+    hidden_units = gate_weight.shape[1]
+    share = width // n
+    if share % 16:
+        return local_thin(
+            inputs, cotangent, lengths, owners, attn_gain, query_weight, key_weight, value_weight, beta_weight,
+            query_conv, key_conv, value_conv, out_gain, out_weight, mlp_gain, gate_weight, up_weight, down_weight,
+        )
+    slots = length // n
+    parts = 16 // math.gcd(slots, 16)
+    thin = width // parts
+    token_rows = parts * slots
+    i32 = jnp.int32
+    devices = jnp.arange(n, dtype=i32)
+    slot_ids = jnp.arange(slots, dtype=i32)
+    row_ids = jnp.arange(length, dtype=i32)
+    part_ids = jnp.arange(parts, dtype=i32)
+
+    before = devices[:, None] < devices[None, :]
+    starts = jnp.sum(jnp.where(before[None], lengths[:, :, None], 0), axis=1)
+    match = owners[:, None, :] == devices[None, :, None]
+    own_start = jnp.sum(jnp.where(match, starts[:, None, :], 0), axis=2)
+    own_len = jnp.sum(jnp.where(match, lengths[:, None, :], 0), axis=2)
+    mine = devices == me
+    my_start = jnp.sum(jnp.where(mine, own_start, 0), axis=1)
+    my_len = jnp.sum(jnp.where(mine, own_len, 0), axis=1)
+
+    first = own_start + (me - own_start) % n
+    pos = first[:, :, None] + n * slot_ids
+    live = pos < (own_start + own_len)[:, :, None]
+    send = jnp.where(live, pos // n, -1)[:, :, None, :]
+    send = jnp.where(send >= 0, send + (part_ids * length)[:, None], -1)
+    outgoing = jnp.stack(
+        [picked(send[m].reshape(-1), split_rows(inputs[m, 0], parts).reshape(-1, thin)) for m in range(micro)]
+    )
+
+    active = row_ids[None] < my_len[:, None]
+    block = (my_start[:, None] + row_ids) % n
+    take = jnp.where(active, block * token_rows + row_ids // n, -1).astype(F32).reshape(-1, HEAD)
+    grad = jnp.where(active.reshape(-1, 1), cotangent[:, 0].reshape(-1, width), jnp.zeros((), BF16))
+
+    back = slot_ids * n + (devices[:, None] - my_start[:, None, None]) % n
+    back = jnp.where(back < my_len[:, None, None], back, -1)[:, :, None, :]
+    back = (back + jnp.zeros((parts, 1), i32)).astype(F32).reshape(-1, HEAD)
+
+    def fill(v):
+        return jnp.pad(v, ((0, 0), (0, share - v.shape[1])))
+
+    small_shard = jnp.concatenate([
+        query_conv, key_conv, value_conv, attn_gain[None], mlp_gain[None], fill(out_gain[None]),
+        jnp.zeros((1, share), BF16), beta_weight.T, jnp.zeros((HEAD - 16 - HEADS, share), BF16),
+    ]).T
+    pieces = width // (2 * HEAD)
+    qkv_shard = jnp.stack(
+        [w.reshape(share, pieces, 2 * HEAD) for w in (query_weight, key_weight, value_weight)], axis=2
+    ).reshape(share, 3 * width)
+    steps = hidden_units // FFW
+    feed_shard = jnp.stack(
+        [w.reshape(share, steps, FFW) for w in (gate_weight, up_weight, down_weight.T)], axis=2
+    ).reshape(share, 3 * hidden_units)
+
+    result, returned, feed_grad, qkv_grad, out_grad, small_grad = block_call(
+        outgoing, take, back, grad, small_shard, qkv_shard, out_weight.T, feed_shard, micro
+    )
+    result = jnp.where(active.reshape(-1, 1), result, jnp.zeros((), BF16))
+
+    at_row = row_ids * n + me
+    inside = (at_row[None, :, None] >= own_start[:, None, :]) & (
+        at_row[None, :, None] < (own_start + own_len)[:, None, :]
+    )
+    at = devices * token_rows + (at_row[None, :, None] - first[:, None, :]) // n
+    put = jnp.sum(jnp.where(inside, at + 1, 0), axis=2) - 1
+    input_rows = jnp.stack([
+        jnp.concatenate(
+            [picked(jnp.where(put[m] >= 0, put[m] + p * slots, -1), returned[m]) for p in range(parts)], axis=1
+        )
+        for m in range(micro)
+    ])
+
+    small_grad = small_grad.T
+    feed_grad = feed_grad.reshape(share, steps, 3, FFW)
+    gate_grad, up_grad, down_grad = (
+        feed_grad[:, :, i].reshape(share, hidden_units) for i in range(3)
+    )
+    qkv_grad = qkv_grad.reshape(share, pieces, 3, 2 * HEAD)
+    query_grad, key_grad, value_grad = (qkv_grad[:, :, i].reshape(share, width) for i in range(3))
+    return (
+        result.reshape(micro, 1, length, width),
+        input_rows.reshape(micro, 1, length, width),
+        small_grad[ROW_ATTN],
+        query_grad,
+        key_grad,
+        value_grad,
+        small_grad[ROW_BETA : ROW_BETA + HEADS].T,
+        small_grad[0:4],
+        small_grad[4:8],
+        small_grad[8:12],
+        small_grad[ROW_OUT, : HEAD // n],
+        out_grad.T,
+        small_grad[ROW_MLP],
+        gate_grad,
+        up_grad,
+        down_grad.T,
+    )
+
+
+class GatherThin:
+    def __init__(self, dims, cs, shard, out, low, width, order, sems):
+        self.dims, self.cs, self.order = dims, cs, order
+        self.columns = pl.ds(low, width)
+        self.shard, self.out = shard.at[:, self.columns], out
+        self.send, self.recv, self.local_thin = sems
+
+    def slot(self, stage, delta):
+        return sum(self.dims[a] - 1 for a in self.order[:stage]) + delta - 1
+
+    def region(self, stage, cs):
+        done = self.order[:stage]
+        lead = tuple(slice(None) if k in done else cs[k] for k in range(4))
+        return self.out.at[lead + (slice(None), self.columns)]
+
+    def copies(self, stage, incoming):
+        axis = self.order[stage]
+        for delta in range(1, self.dims[axis]):
+            frm = along(self.dims, self.cs, axis, -delta) if incoming else self.cs
+            to = along(self.dims, self.cs, axis, delta)
+            k = self.slot(stage, delta)
+            yield pltpu.make_async_remote_copy(
+                src_ref=self.shard if stage == 0 else self.region(stage, self.cs),
+                dst_ref=self.region(stage, frm),
+                send_sem=self.send.at[k],
+                recv_sem=self.recv.at[k],
+                device_id=(index_of(self.dims, to),),
+                device_id_type=MESH,
+            )
+
+    def keep(self):
+        return pltpu.make_async_copy(self.shard, self.region(0, self.cs), self.local_thin)
+
+    def step(self, stage):
+        if stage == 0:
+            self.keep().start()
+        if stage == 1:
+            self.keep().wait()
+        if stage >= 1:
+            for c in self.copies(stage - 1, True):
+                c.wait_recv()
+        if stage < 4:
+            for c in self.copies(stage, False):
+                c.start()
+
+    def finish(self):
+        for stage in range(4):
+            for c in self.copies(stage, False):
+                c.wait_send()
+
+
+def pipelined_thin(jobs, stages, lag):
+    for tick in range(len(jobs) + (stages - 1) * lag):
+        for stage in range(stages):
+            i = tick - stage * lag
+            if 0 <= i < len(jobs):
+                jobs[i].step(stage)
+
+
+class TokensThin:
+    def __init__(self, n, me, a, b, send, recv, local_thin):
+        self.n, self.me, self.a, self.b = n, me, a, b
+        self.send, self.recv, self.local_thin = send, recv, local_thin
+
+    def copy(self, d, incoming):
+        to = lax.rem(self.me + d, self.n)
+        frm = lax.rem(self.me - d + self.n, self.n)
+        return pltpu.make_async_remote_copy(
+            src_ref=self.a.at[to],
+            dst_ref=self.b.at[frm if incoming else self.me],
+            send_sem=self.send.at[d],
+            recv_sem=self.recv.at[d],
+            device_id=(to,),
+            device_id_type=MESH,
+        )
+
+    def keep(self):
+        return pltpu.make_async_copy(self.a.at[self.me], self.b.at[self.me], self.local_thin)
+
+    def each(self, act):
+        def body(d, carry):
+            act(d)
+            return carry
+
+        lax.fori_loop(1, self.n, body, 0)
+
+    def start(self):
+        self.keep().start()
+        self.each(lambda d: self.copy(d, False).start())
+
+    def wait(self):
+        self.keep().wait()
+        self.each(lambda d: self.copy(d, True).wait_recv())
+        self.each(lambda d: self.copy(d, False).wait_send())
+
+
+def gather_kernel_thin(dims, plan, lag, count, with_tokens, *refs):
+    n = math.prod(dims)
+    t = 1 if with_tokens else 0
+    ins, outs, scr = refs[: count + t], refs[count + t : 2 * (count + t)], refs[2 * (count + t) :]
+    send, recv, local_thin = scr[:3]
+    me = lax.axis_index("fsdp")
+    cs = coords_of(dims, me)
+    if with_tokens:
+        greet_all(n, me)
+        tokens = TokensThin(n, me, ins[count], outs[count], *scr[3:])
+        tokens.start()
+    else:
+        greet_axes(dims, cs)
+    jobs = [
+        GatherThin(dims, cs, ins[a], outs[a], low, width, order, (send.at[i], recv.at[i], local_thin.at[i]))
+        for i, (a, low, width, order) in enumerate(plan)
+    ]
+    pipelined_thin(jobs, 5, lag)
+    for j in jobs:
+        j.finish()
+    if with_tokens:
+        tokens.wait()
+
+
+def token_sems_thin(n):
+    return [
+        pltpu.SemaphoreType.DMA((n,)),
+        pltpu.SemaphoreType.DMA((n,)),
+        pltpu.SemaphoreType.DMA,
+    ]
+
+
+def gather_call_thin(shards, tokens, plan, lag, collective_id):
+    n = lax.axis_size("fsdp")
+    dims = grid_of(n)
+    k = hops(dims)
+    ins = list(shards) + ([] if tokens is None else [tokens])
+    outs = [jax.ShapeDtypeStruct(dims + s.shape, s.dtype) for s in shards]
+    if tokens is not None:
+        outs.append(jax.ShapeDtypeStruct(tokens.shape, tokens.dtype))
+    m = len(plan)
+    return pl.pallas_call(
+        functools.partial(gather_kernel_thin, dims, plan, lag, len(shards), tokens is not None),
+        out_shape=outs,
+        in_specs=[any_spec()] * len(ins),
+        out_specs=[any_spec()] * len(outs),
+        scratch_shapes=[
+            pltpu.SemaphoreType.DMA((m, k)),
+            pltpu.SemaphoreType.DMA((m, k)),
+            pltpu.SemaphoreType.DMA((m,)),
+        ]
+        + ([] if tokens is None else token_sems_thin(n)),
+        compiler_params=pltpu.CompilerParams(
+            collective_id=collective_id, has_side_effects=True, vmem_limit_bytes=VMEM_LIMIT
+        ),
+    )(*ins)
+
+
+class ScatterThin:
+    def __init__(self, dims, cs, terms, result, low, width, order, scratch, sems):
+        self.dims, self.cs, self.order = dims, cs, order
+        self.columns = pl.ds(low, width)
+        self.terms, self.result = terms, result
+        self.own, self.got = scratch[0], scratch[1:]
+        self.send, self.recv, self.local_thin = sems
+
+    def slot(self, stage, delta):
+        return sum(self.dims[a] - 1 for a in self.order[:stage]) + delta - 1
+
+    def part(self, stage, at):
+        axis = self.order[stage]
+        if stage == 0:
+            lead = tuple(at if k == axis else slice(None) for k in range(4))
+            return self.terms.at[lead + (slice(None), self.columns)]
+        left = [k for k in range(4) if k not in self.order[:stage]]
+        return self.got[stage - 1].at[(0,) + tuple(at if k == axis else slice(None) for k in left)]
+
+    def copies(self, stage):
+        axis = self.order[stage]
+        for delta in range(1, self.dims[axis]):
+            to = along(self.dims, self.cs, axis, delta)
+            k = self.slot(stage, delta)
+            yield pltpu.make_async_remote_copy(
+                src_ref=self.part(stage, to[axis]),
+                dst_ref=self.got[stage].at[delta - 1],
+                send_sem=self.send.at[k],
+                recv_sem=self.recv.at[k],
+                device_id=(index_of(self.dims, to),),
+                device_id_type=MESH,
+            )
+
+    def keep(self):
+        return pltpu.make_async_copy(self.part(0, self.cs[self.order[0]]), self.own, self.local_thin)
 
     def total(self, stage):
         axis = self.order[stage]
@@ -321,10 +1248,7 @@
                 c.wait_send()
 
 
-CXYZ, CYXZ = (C, X, Y, Z), (C, Y, X, Z)
-
-
-def scatter_scratch(dims, rows, width, order, dtype):
+def scatter_scratch_thin(dims, rows, width, order, dtype):
     left = list(dims)
     out = [pltpu.VMEM(tuple(d for k, d in enumerate(dims) if k != order[0]) + (rows, width), dtype)]
     for s, axis in enumerate(order):
@@ -333,36 +1257,36 @@
     return out
 
 
-def scatter_kernel(dims, plan, lag, count, with_tokens, *refs):
+def scatter_kernel_thin(dims, plan, lag, count, with_tokens, *refs):
     n = math.prod(dims)
     t = 1 if with_tokens else 0
     ins, outs, scr = refs[: count + t], refs[count + t : 2 * (count + t)], refs[2 * (count + t) :]
-    send, recv, local = scr[:3]
+    send, recv, local_thin = scr[:3]
     scr = scr[3:]
     me = lax.axis_index("fsdp")
     cs = coords_of(dims, me)
     if with_tokens:
         greet_all(n, me)
-        tokens = Tokens(n, me, ins[count], outs[count], *scr[:3])
+        tokens = TokensThin(n, me, ins[count], outs[count], *scr[:3])
         tokens.start()
         scr = scr[3:]
     else:
         greet_axes(dims, cs)
     jobs = [
-        Scatter(
+        ScatterThin(
             dims, cs, ins[a], outs[a], low, width, order, scr[5 * i : 5 * i + 5],
-            (send.at[i], recv.at[i], local.at[i]),
+            (send.at[i], recv.at[i], local_thin.at[i]),
         )
         for i, (a, low, width, order) in enumerate(plan)
     ]
-    pipelined(jobs, 5, lag)
+    pipelined_thin(jobs, 5, lag)
     for j in jobs:
         j.finish()
     if with_tokens:
         tokens.wait()
 
 
-def scatter_call(terms, tokens, plan, lag, collective_id):
+def scatter_call_thin(terms, tokens, plan, lag, collective_id):
     n = lax.axis_size("fsdp")
     dims = grid_of(n)
     k = hops(dims)
@@ -375,9 +1299,9 @@
     m = len(plan)
     scratch = []
     for a, low, width, order in plan:
-        scratch += scatter_scratch(dims, terms[a].shape[4], width, order, terms[a].dtype)
+        scratch += scatter_scratch_thin(dims, terms[a].shape[4], width, order, terms[a].dtype)
     return pl.pallas_call(
-        functools.partial(scatter_kernel, dims, plan, lag, len(terms), tokens is not None),
+        functools.partial(scatter_kernel_thin, dims, plan, lag, len(terms), tokens is not None),
         out_shape=outs,
         in_specs=[any_spec()] * len(ins),
         out_specs=out_specs,
@@ -386,7 +1310,7 @@
             pltpu.SemaphoreType.DMA((m, k)),
             pltpu.SemaphoreType.DMA((m,)),
         ]
-        + ([] if tokens is None else token_sems(n))
+        + ([] if tokens is None else token_sems_thin(n))
         + scratch,
         compiler_params=pltpu.CompilerParams(
             collective_id=collective_id, has_side_effects=True, vmem_limit_bytes=VMEM_LIMIT
@@ -394,59 +1318,14 @@
     )(*ins)
 
 
-def dot(a, b):
-    return lax.dot_general(a, b, (((1,), (0,)), ((), ())), preferred_element_type=F32)
-
-
-def dot_nt(a, b):
-    return lax.dot_general(a, b, (((1,), (1,)), ((), ())), preferred_element_type=F32)
-
-
-def dot_tn(a, b):
-    return lax.dot_general(a, b, (((0,), (0,)), ((), ())), preferred_element_type=F32)
-
-
-def low(v):
-    return v.astype(BF16)
-
-
-def lanes(i, width=HEAD):
-    return slice(i * width, (i + 1) * width)
-
-
-def shifted(values, by, row):
-    if by == 0:
-        return values
-    rows = values.shape[0]
-    moved = pltpu.roll(values, by % rows, 0)
-    return jnp.where(row >= by if by > 0 else row < rows + by, moved, 0.0)
-
-
-def conv(values, taps, row):
+def conv_thin(values, taps, row):
     total = values * taps[0:1]
     for c in range(1, taps.shape[0]):
         total += shifted(values, c, row) * taps[c : c + 1]
     return total
 
 
-def head_sum(values):
-    return jnp.sum(values, axis=-1, keepdims=True)
-
-
-def iotas(shape):
-    return lax.broadcasted_iota(jnp.int32, shape, 0), lax.broadcasted_iota(jnp.int32, shape, 1)
-
-
-def level_masks():
-    i, j = iotas((SPAN, SPAN))
-    found = []
-    for level in range(SPAN.bit_length() - 1):
-        a, b = i >> level, j >> level
-        found.append(((a >> 1) == (b >> 1)) & ((a & 1) == 1) & ((b & 1) == 0))
-    return found
-
-
-def project(own, small, weights, attn_low, pre, queries, keys, values, beta, micro, length):
+def project_thin(own, small, weights, attn_low, pre, queries, keys, values, beta, micro, length):
     width = own.shape[1]
     row = lax.broadcasted_iota(jnp.int32, (length, 2 * HEAD), 0)
     gain = small[ROW_ATTN : ROW_ATTN + 1, :]
@@ -465,7 +1344,7 @@
                 wide = slice(kind * width + cols.start, kind * width + cols.stop)
                 x = dot(a, weights[:, wide])
                 pre[rows, wide] = low(x)
-                c = conv(x, small[4 * kind : 4 * kind + 4, cols], row)
+                c = conv_thin(x, small[4 * kind : 4 * kind + 4, cols], row)
                 u = c * jax.nn.sigmoid(c)
                 if kind == 2:
                     out[rows, cols] = low(u)
@@ -479,7 +1358,7 @@
     lax.fori_loop(0, micro, one, 0)
 
 
-def delta_block(base, first, refs, gain):
+def delta_block_thin(base, first, refs, gain):
     queries, keys, values, beta, state, states, inverses, scores, fresh, mix, mixed, at = refs
     rows = pl.ds(base, SPAN)
     i, j = iotas((SPAN, SPAN))
@@ -520,15 +1399,15 @@
         mixed[rows, lanes(h)] = low(out[h] * r * gain)
 
 
-def forward_kernel(micro, length, *refs):
+def forward_kernel_thin(micro, length, *refs):
     (own, small, weights, out_weight, hidden, attn_low, pre, queries, keys, values, beta,
      states, inverses, scores, fresh, mix, mixed, state) = refs
-    project(own, small, weights, attn_low, pre, queries, keys, values, beta, micro, length)
+    project_thin(own, small, weights, attn_low, pre, queries, keys, values, beta, micro, length)
     gain = small[ROW_OUT : ROW_OUT + 1, :HEAD]
     blocks = length // SPAN
 
     def one(t, carry):
-        delta_block(
+        delta_block_thin(
             pl.multiple_of(t * SPAN, SPAN), lax.rem(t, blocks) == 0,
             (queries, keys, values, beta, state, states, inverses, scores, fresh, mix, mixed, t), gain,
         )
@@ -539,7 +1418,7 @@
     lax.fori_loop(0, micro * blocks, one, 0)
 
 
-def forward_call(own, small, weights, out_weight, micro):
+def forward_call_thin(own, small, weights, out_weight, micro):
     rows, width = own.shape
     length = rows // micro
     blocks = rows // SPAN
@@ -551,7 +1430,7 @@
         jax.ShapeDtypeStruct((blocks, HEADS, HEAD, HEAD), BF16), square, square, wide, wide, wide,
     ]
     return pl.pallas_call(
-        functools.partial(forward_kernel, micro, length),
+        functools.partial(forward_kernel_thin, micro, length),
         out_shape=outs,
         in_specs=[vmem_spec()] * 4,
         out_specs=[vmem_spec()] * len(outs),
@@ -560,7 +1439,7 @@
     )(own, small, weights, out_weight)
 
 
-def feed_kernel(steps, hidden, grad, small, active, w_ref, result, terms, d_hidden, gain_grad, norm, total, d_norm):
+def feed_kernel_thin(steps, hidden, grad, small, active, w_ref, result, terms, d_hidden, gain_grad, norm, total, d_norm):
     t = pl.program_id(0)
     gain = small[ROW_MLP : ROW_MLP + 1, :]
 
@@ -599,13 +1478,13 @@
         d_hidden[...] = g.astype(F32) + r * (gd - vr * (jnp.sum(vr * gd, axis=-1, keepdims=True) / n))
 
 
-def feed_call(hidden, grad, small, active, weights):
+def feed_call_thin(hidden, grad, small, active, weights):
     rows, width = hidden.shape
     steps = weights.shape[1] // (3 * FFW)
     whole = lambda *shape: pl.BlockSpec(shape, lambda t: (0,) * len(shape))
     block = pl.BlockSpec((width, 3 * FFW), lambda t: (0, t))
     return pl.pallas_call(
-        functools.partial(feed_kernel, steps),
+        functools.partial(feed_kernel_thin, steps),
         grid=(steps,),
         out_shape=[
             jax.ShapeDtypeStruct((rows, width), BF16),
@@ -626,7 +1505,7 @@
     )(hidden, grad, small, active, weights)
 
 
-def delta_back(base, last, refs, gain):
+def delta_back_thin(base, last, refs, gain):
     (queries, keys, values, beta, states, inverses, scores, fresh, mix, d_mixed,
      d_state, d_out, d_q, d_k, d_v, d_beta, gain_grad, at) = refs
     rows = pl.ds(base, SPAN)
@@ -673,7 +1552,7 @@
     d_beta[rows, :] = low(beta_grad * strength * (1.0 - strength))
 
 
-def backward_kernel(micro, length, *refs):
+def backward_kernel_thin(micro, length, *refs):
     (d_hidden, own, small, weights, out_weight, attn_low, pre, queries, keys, values, beta,
      states, inverses, scores, fresh, mix, mixed,
      d_own, qkv_grad, out_grad, small_grad,
@@ -690,7 +1569,7 @@
         t = total - 1 - step
         base = pl.multiple_of(t * SPAN, SPAN)
         d_out[...] = dot(d_attn[pl.ds(base, SPAN), :], out_weight[...])
-        delta_back(
+        delta_back_thin(
             base, lax.rem(step, blocks) == 0,
             (queries, keys, values, beta, states, inverses, scores, fresh, mix, d_out,
              d_state, None, d_q, d_k, d_v, d_beta, gain_grad, t), gain,
@@ -754,11 +1633,11 @@
     lax.fori_loop(0, total, finish, 0)
 
 
-def backward_call(d_hidden, own, small, weights, out_weight, saved, micro):
+def backward_call_thin(d_hidden, own, small, weights, out_weight, saved, micro):
     rows, width = own.shape
     length = rows // micro
     return pl.pallas_call(
-        functools.partial(backward_kernel, micro, length),
+        functools.partial(backward_kernel_thin, micro, length),
         out_shape=[
             jax.ShapeDtypeStruct((rows, width), BF16),
             jax.ShapeDtypeStruct((width, 3 * width), BF16),
@@ -782,24 +1661,7 @@
     )(d_hidden, own, small, weights, out_weight, *saved)
 
 
-def picked(index, source):
-    hot = index[:, None] == jnp.arange(source.shape[0], dtype=jnp.int32)[None, :]
-    return jnp.dot(low(hot), source, preferred_element_type=F32).astype(BF16)
-
-
-def split_rows(values, parts):
-    cut = values.reshape(values.shape[:-1] + (parts, values.shape[-1] // parts))
-    return jnp.moveaxis(cut, -2, 0)
-
-
-def spans(width, size):
-    at = 0
-    while at < width:
-        yield at, min(size, width - at)
-        at += size
-
-
-def local(
+def local_thin(
     inputs, cotangent, lengths, owners, attn_gain, query_weight, key_weight, value_weight, beta_weight,
     query_conv, key_conv, value_conv, out_gain, out_weight, mlp_gain, gate_weight, up_weight, down_weight,
 ):
@@ -858,7 +1720,7 @@
     for a, (w, size) in enumerate(((4 * width, 512), (3 * hidden_units, 768)), 1):
         for at, wide in spans(w, size):
             plan.append((a, at, wide, (ZXY, ZYX)[len(plan) % 2]))
-    small_all, attn_all, feed_all, incoming = gather_call(
+    small_all, attn_all, feed_all, incoming = gather_call_thin(
         [packed, attn_shard, feed_shard], outgoing, tuple(plan), 2, 1
     )
     small = small_all.reshape(n, -1)[:, : SMALL_ROWS * share].reshape(n, SMALL_ROWS, share)
@@ -881,11 +1743,11 @@
     active = active.reshape(-1, 1)
     grad = jnp.where(active, cotangent[:, 0].reshape(-1, width), jnp.zeros((), BF16))
 
-    hidden, *saved = forward_call(own, small, qkv, out_t, micro)
-    result, feed_terms, d_hidden, mlp_gain_grad = feed_call(
+    hidden, *saved = forward_call_thin(own, small, qkv, out_t, micro)
+    result, feed_terms, d_hidden, mlp_gain_grad = feed_call_thin(
         hidden, grad, small, active.astype(F32), feed_all
     )
-    d_own, qkv_terms, out_terms, small_terms = backward_call(
+    d_own, qkv_terms, out_terms, small_terms = backward_call_thin(
         d_hidden, own, small, qkv, out_t, saved, micro
     )
 
@@ -914,7 +1776,7 @@
     for a, size in ((3, 768), (2, 512), (1, 512), (0, HEAD)):
         for lo, wide in spans(terms[a].shape[5], size):
             plan.append((a, lo, wide, (CXYZ, CYXZ)[len(plan) % 2]))
-    small_grad, qkv_grad, out_grad, feed_grad, returned = scatter_call(
+    small_grad, qkv_grad, out_grad, feed_grad, returned = scatter_call_thin(
         terms, returning, tuple(plan), 2, 2
     )
 

time: 543 us -> 420 us (0.77)
  Pallas kernels: 471 us -> 366 us
  local copies, waits for them, and re-layouts: 38.8 us -> 25.4 us
    pallas_call x5 -> x1, Pallas kernels: 471 us -> 366 us  [block_call(): pl.pallas_call(functools.partial(block_kernel, dims, micro, length, steps...]
    slice x12 -> x6, local copies, waits for them, and re-layouts: 12.1 us -> 4.01 us  [the longest x1 1.49 us: local(): inputs[m, 0]]
    dot_general x6 -> x10, matrix products: 15.6 us -> 11.2 us  [picked(): jnp.dot(low(hot_rows), source, preferred_element_type=F32).astype(BF16)]
    unnamed x34 -> x58, local copies, waits for them, and re-layouts: 7.7 us -> 11.1 us
where the time goes in v3:
time: 420 us; the launch traced here: 412 us
  Pallas kernels  366 us (87%)
  local copies, waits for them, and re-layouts  25.4 us (6%)
  matrix products  11.2 us (3%)
  other arithmetic  8.1 us (2%)
    pallas_call x1, Pallas kernels, block_call(): pl.pallas_call(functools.partial(block_kernel, dims, micro, length, steps...  366 us
    dot_general x10, matrix products, picked(): jnp.dot(low(hot_rows), source, preferred_element_type=F32).astype(BF16)  11.2 us
    unnamed x58, local copies, waits for them, and re-layouts  11.1 us

profile of v3, /device:TPU:0, one launch (start us, length us, event | category | flops | bytes accessed | tf_op | source)
XLA Modules:
  0.0 412.2 jit_solution(10522751488619356509)
XLA Ops:
  0.7 0.8 select_reduce_fusion.1
  1.4 0.8 select_reduce_fusion.2
  3.0 1.5 fusion.73
  5.2 1.8 fusion.6
  7.8 1.8 fusion.7
  9.6 1.3 pad_maximum_fusion.refs_0_
  10.9 0.8 reshape.309.refs_2_
  12.8 1.4 bitcast_select_fusion.refs_3_
  15.4 1.5 reshape.311.refs_7_
  17.6 0.9 reshape.310.refs_5_
  19.2 0.7 concatenate.9
  19.9 366.2 %shard_map.297 = (bf16[768,1024]{1,0:T(8,128)(2,1)}, bf16[2,1536,256]{2,1,0:T(8,128)(2,1)}, f32[32,8448]{1,0:T(8,128)}, f32[32,3072]{1,0:T(8,128)}, f32[32,1024]...) custom-call(bf16[2,1536,256]{2,1,0:T(8,128)(2,1)} %pad_maximum_fusio, ...), custom_call_target="tpu_custom_call" | custom-call | tf_op jit(solution)/shard_map/pallas_call | solution.py:881
  386.3 2.1 fusion.28
  388.4 0.8 fusion.29
  389.2 0.8 fusion.30
  390.0 0.8 fusion.31
  390.9 0.8 fusion.24
  391.7 0.8 fusion.25
  392.5 0.8 fusion.26
  393.3 0.8 fusion.27
  394.3 1.8 copy.107
  396.7 2.8 slice_reduce_fusion
  399.6 0.9 copy.119
  400.5 0.9 copy.117
  401.5 0.9 copy.118
  402.4 1.3 broadcast_select_fusion
  404.0 1.1 slice_reduce_fusion.3
  405.1 0.7 copy.114
  405.8 0.7 copy.115
  406.5 0.7 copy.116
  409.9 0.7 slice_reduce_fusion.6
  410.6 0.7 slice_reduce_fusion.8
  (107 shorter events, 10.5 us)
Async XLA Ops:
  9.6 3.2 copy-start
  12.8 1.5 copy-start.5
  12.8 1.6 copy-start.6
  12.8 1.7 copy-start.7
  14.8 2.1 copy-start.9
  14.8 2.1 copy-start.10
  14.8 2.2 copy-start.11
  15.3 3.1 copy-start.19
  15.4 3.2 copy-start.12
  15.4 3.3 copy-start.16
  15.4 3.4 copy-start.17
  15.4 3.5 copy-start.13
  15.4 3.6 copy-start.14
  15.4 3.7 copy-start.15
  386.1 2.3 copy-start.18
  394.3 1.8 copy-start.2
  399.6 2.9 copy-start.1
  402.4 1.3 copy-start.4
  403.7 3.4 copy-start.3
  403.7 7.6 %copy-start.8 = (f32[32,1024]{1,0:T(8,128)S(1)}, f32[32,1024]{1,0:T(8,128)}, u32[]{:S(2)}) copy-start(f32[32,1024]{1,0:T(8,128)} %get-tuple-element.26) | copy-start | bytes 393220

commit v4 on v3

--- a/solution.py
+++ b/solution.py
@@ -23,6 +23,7 @@
 ZXY, ZYX = (Z, X, Y, C), (Z, Y, X, C)
 CXYZ, CYXZ = (C, X, Y, Z), (C, Y, X, Z)
 GATHER_TICKS = (0, 2, 4, 6, 8)
+FEED_TICKS = (0, 2, 4, 6, 7)
 SCATTER_TICKS = (0, 1, 3, 5, 7)
 SLOTS = (4, 6, 6, 4)
 
@@ -463,12 +464,13 @@
 
 
 def block_kernel(dims, micro, length, steps, token_rows, *refs):
-    (tokens_in, take, back, grad_in, small_shard, qkv_shard, out_shard, feed_shard,
+    (tokens_in, take, back, query_conv, key_conv, value_conv, attn_gain, mlp_gain, out_gain, beta_weight,
+     grad_in, qkv_shard, out_shard, feed_shard,
      result, returned, feed_grad, qkv_grad, out_grad, small_grad,
      small_all, qkv_all, out_all, feed_all,
      own, attn_low, pre, qkv, beta, states, inverses, scores, fresh, mix, mixed,
      hidden, total, d_hidden, norm, grad, bufs, w_out, state, d_out, tok_buf, small_buf, small, small_terms,
-     gain_out, d_beta, small_out,
+     gain_out, d_beta, small_out, small_rows, small_shard,
      g_send, g_recv, g_local, s_send, s_recv, t_send, t_recv, t_local, load_sem, ready, *got) = refs
     n = math.prod(dims)
     me = lax.axis_index("fsdp")
@@ -577,24 +579,34 @@
         )
 
     load_grad.start()
+    small_rows[...] = jnp.zeros_like(small_rows)
+    for at, part in (
+        (ROW_CONV, query_conv), (ROW_CONV + 4, key_conv), (ROW_CONV + 8, value_conv),
+        (ROW_ATTN, attn_gain), (ROW_MLP, mlp_gain), (ROW_OUT, out_gain),
+    ):
+        small_rows[at : at + part.shape[0], : part.shape[1]] = part[...].astype(F32)
+    turned = small_rows[...].T[:share]
+    small_rows[:share, :] = turned
+    small_rows[:share, ROW_BETA : ROW_BETA + HEADS] = beta_weight[...].astype(F32)
+    small_shard[...] = low(small_rows[:share, :])
     greet_all(n, me)
-    tokens_to(0).start()
     segment = [(lambda i: [attn_gather[i]], 0, len(attn_gather))]
     last = len(attn_gather) + GATHER_TICKS[-1]
     early = 0
     for t in range(last):
         run_tick(segment, GATHER_TICKS, t)
-        if t == len(attn_gather) - 1:
-            for m in range(1, micro):
-                tokens_to(m).start()
+        if t == TOKENS_AT:
+            tokens_to(0).start()
         if t >= len(attn_gather) and (last - 1 - t) % 2 == 0 and early < EARLY:
-            run_tick(gathers, GATHER_TICKS, early)
+            run_tick(gathers, FEED_TICKS, early)
             early += 1
         if t == GATHER_TICKS[-1]:
             load_small.start()
         for i in range(pieces):
             if t == 2 * i + 2 + GATHER_TICKS[-1]:
                 load_qkv(i).start()
+    for m in range(1, micro):
+        tokens_to(m).start()
     load_small.wait()
     blockwise = small_buf[...].reshape(width, HEAD).astype(F32)
     small[...] = blockwise.T[:SMALL_ROWS]
@@ -614,7 +626,7 @@
     row1 = lax.broadcasted_iota(jnp.int32, (length, HEAD), 0)
 
     def project(m, carry):
-        run_tick(gathers, GATHER_TICKS, early + m)
+        run_tick(gathers, FEED_TICKS, early + m)
         tokens_to(m).wait()
 
         def arrive(t, carry):
@@ -645,7 +657,7 @@
     lax.fori_loop(0, micro, project, 0)
 
     def forward(t, carry):
-        run_tick(gathers, GATHER_TICKS, early + micro + t)
+        run_tick(gathers, FEED_TICKS, early + micro + t)
         for s in range(5):
 
             @pl.when(t == s)
@@ -666,20 +678,25 @@
     load_feed(0).start()
     load_out.wait()
 
+    load_grad.wait()
+
+    def live(t):
+        return column(take[pl.ds(t, 1), :])[:, 0:1] >= 0.0
+
     def enter(t, carry):
         at = pl.ds(pl.multiple_of(t * SPAN, SPAN), SPAN)
         v = own[at, :].astype(F32) + dot_nt(mixed[at, :], w_out[...].reshape(width, width))
         hidden[at, :] = v
         norm[at, :] = low(v * rms(v) * gain_mlp)
+        grad[at, :] = jnp.where(live(t), grad[at, :], jnp.zeros((), BF16))
         return carry
 
     lax.fori_loop(0, micro * blocks, enter, 0)
-    load_grad.wait()
     total[...] = jnp.zeros_like(total)
     d_hidden[...] = jnp.zeros_like(d_hidden)
 
     def feed(t, carry):
-        run_tick(gathers, GATHER_TICKS, begun + t)
+        run_tick(gathers, FEED_TICKS, begun + t)
 
         @pl.when(t + 1 < steps)
         def _():
@@ -712,7 +729,7 @@
     def leave(t, carry):
         at = pl.ds(pl.multiple_of(t * SPAN, SPAN), SPAN)
         v, g = hidden[at, :], grad[at, :].astype(F32)
-        grad[at, :] = low(v + total[at, :])
+        grad[at, :] = low(jnp.where(live(t), v + total[at, :], 0.0))
         d, terms = rms_back(d_hidden[at, :], v, rms(v), gain_mlp)
         small_terms[ROW_MLP : ROW_MLP + 1, :] += jnp.sum(terms, axis=0, keepdims=True)
         d_hidden[at, :] = g + d
@@ -786,14 +803,15 @@
             return carry
 
         lax.fori_loop(0, blocks, depart, 0)
-        line = lax.broadcasted_iota(jnp.int32, (HEAD, length), 0)
+        line = lax.broadcasted_iota(jnp.int32, (HEAD, thin), 0)
 
         def pack(b, carry):
             pick = hot(column(back[pl.ds(m * (n * token_rows // HEAD) + b, 1), :]), length)
             part = lax.rem(line + b * HEAD, token_rows) // slots
-            held = jnp.zeros((HEAD, thin), F32)
-            for p in range(parts):
-                held += dot(jnp.where(part == p, pick, jnp.zeros((), BF16)), own[rows, lanes(p, thin)])
+            wide_rows = dot(pick, own[rows, :])
+            held = wide_rows[:, lanes(0, thin)]
+            for p in range(1, parts):
+                held = jnp.where(part == p, wide_rows[:, lanes(p, thin)], held)
             tok_buf[m, pl.ds(pl.multiple_of(b * HEAD, HEAD), HEAD), :] = low(held)
             return carry
 
@@ -839,9 +857,10 @@
 
 
 EARLY = 3
-
-
-def block_call(tokens, take, back, grad, small_shard, qkv_shard, out_shard, feed_shard, micro):
+TOKENS_AT = 8
+
+
+def block_call(tokens, take, back, smalls, grad, qkv_shard, out_shard, feed_shard, micro):
     rows, width = grad.shape
     length, blocks = rows // micro, rows // SPAN
     n = lax.axis_size("fsdp")
@@ -856,7 +875,7 @@
     outs = [
         shape((rows, width), BF16), shape(tokens.shape, BF16),
         shape(feed_shard.shape, F32), shape(qkv_shard.shape, F32), shape(out_shard.shape, F32), shape((share, HEAD), F32),
-        shape(dims + small_shard.shape, BF16), shape(dims + qkv_shard.shape, BF16), shape(dims + out_shard.shape, BF16),
+        shape(flat + (HEAD,), BF16), shape(dims + qkv_shard.shape, BF16), shape(dims + out_shard.shape, BF16),
         shape(dims + feed_shard.shape, BF16),
     ]
     wide, full = pltpu.VMEM((rows, width), BF16), pltpu.VMEM((rows, width), F32)
@@ -871,7 +890,7 @@
         pltpu.VMEM((HEADS, HEAD, HEAD), F32), pltpu.VMEM((SPAN, width), F32), pltpu.VMEM(tokens.shape, BF16),
         pltpu.VMEM(flat + (HEAD,), BF16), pltpu.VMEM((SMALL_ROWS, width), F32), pltpu.VMEM((SMALL_ROWS // 2, width), F32),
         pltpu.VMEM((1, HEAD), F32), pltpu.VMEM((rows, 16), BF16),
-        pltpu.VMEM(flat + (HEAD,), F32),
+        pltpu.VMEM(flat + (HEAD,), F32), pltpu.VMEM((HEAD, HEAD), F32), pltpu.VMEM((share, HEAD), BF16),
         dma((gathers, k)), dma((gathers, k)), dma((gathers,)), dma((scatters, k)), dma((scatters, k)),
         dma((2 * micro, n)), dma((2 * micro, n)), dma((2 * micro,)), dma((pieces + 5,)), pltpu.SemaphoreType.REGULAR,
     ]
@@ -881,13 +900,13 @@
     return pl.pallas_call(
         functools.partial(block_kernel, dims, micro, length, steps, token_rows),
         out_shape=outs,
-        in_specs=[any_spec(), vmem_spec(), vmem_spec()] + [any_spec()] * 5,
+        in_specs=[any_spec()] + [vmem_spec()] * (2 + len(smalls)) + [any_spec()] * 4,
         out_specs=[any_spec()] * 2 + [vmem_spec()] * 4 + [any_spec()] * 4,
         scratch_shapes=scratch,
         compiler_params=pltpu.CompilerParams(
             collective_id=1, has_side_effects=True, vmem_limit_bytes=VMEM_LIMIT
         ),
-    )(tokens, take, back, grad, small_shard, qkv_shard, out_shard, feed_shard)[:6]
+    )(tokens, take, back, *smalls, grad, qkv_shard, out_shard, feed_shard)[:6]
 
 
 def picked(index, source):
@@ -952,19 +971,15 @@
     active = row_ids[None] < my_len[:, None]
     block = (my_start[:, None] + row_ids) % n
     take = jnp.where(active, block * token_rows + row_ids // n, -1).astype(F32).reshape(-1, HEAD)
-    grad = jnp.where(active.reshape(-1, 1), cotangent[:, 0].reshape(-1, width), jnp.zeros((), BF16))
+    grad = cotangent[:, 0].reshape(-1, width)
 
     back = slot_ids * n + (devices[:, None] - my_start[:, None, None]) % n
     back = jnp.where(back < my_len[:, None, None], back, -1)[:, :, None, :]
     back = (back + jnp.zeros((parts, 1), i32)).astype(F32).reshape(-1, HEAD)
 
-    def fill(v):
-        return jnp.pad(v, ((0, 0), (0, share - v.shape[1])))
-
-    small_shard = jnp.concatenate([
-        query_conv, key_conv, value_conv, attn_gain[None], mlp_gain[None], fill(out_gain[None]),
-        jnp.zeros((1, share), BF16), beta_weight.T, jnp.zeros((HEAD - 16 - HEADS, share), BF16),
-    ]).T
+    smalls = (
+        query_conv, key_conv, value_conv, attn_gain[None], mlp_gain[None], out_gain[None], beta_weight
+    )
     pieces = width // (2 * HEAD)
     qkv_shard = jnp.stack(
         [w.reshape(share, pieces, 2 * HEAD) for w in (query_weight, key_weight, value_weight)], axis=2
@@ -975,9 +990,8 @@
     ).reshape(share, 3 * hidden_units)
 
     result, returned, feed_grad, qkv_grad, out_grad, small_grad = block_call(
-        outgoing, take, back, grad, small_shard, qkv_shard, out_weight.T, feed_shard, micro
-    )
-    result = jnp.where(active.reshape(-1, 1), result, jnp.zeros((), BF16))
+        outgoing, take, back, smalls, grad, qkv_shard, out_weight.T, feed_shard, micro
+    )
 
     at_row = row_ids * n + me
     inside = (at_row[None, :, None] >= own_start[:, None, :]) & (
@@ -985,12 +999,17 @@
     )
     at = devices * token_rows + (at_row[None, :, None] - first[:, None, :]) // n
     put = jnp.sum(jnp.where(inside, at + 1, 0), axis=2) - 1
-    input_rows = jnp.stack([
-        jnp.concatenate(
-            [picked(jnp.where(put[m] >= 0, put[m] + p * slots, -1), returned[m]) for p in range(parts)], axis=1
-        )
-        for m in range(micro)
-    ])
+    sources = jnp.arange(n * token_rows, dtype=i32)
+    input_rows = jnp.concatenate(
+        [
+            jnp.einsum(
+                "mrs,msc->mrc", low(jnp.where(put >= 0, put + p * slots, -1)[:, :, None] == sources), returned,
+                preferred_element_type=F32,
+            ).astype(BF16)
+            for p in range(parts)
+        ],
+        axis=2,
+    )
 
     small_grad = small_grad.T
     feed_grad = feed_grad.reshape(share, steps, 3, FFW)

time: 420 us -> 413 us (0.983)
    dot_general x10 -> x2, matrix products: 11.2 us -> 3.61 us  [picked(): jnp.dot(low(hot_rows), source, preferred_element_type=F32).astype(BF16)]
    dot_general x0 -> x4, matrix products: none -> 7.1 us  [local(): jnp.einsum('mrs,msc->mrc', low(jnp.where(put >= 0, put + p * slots, -1)[:...]
    unnamed x58 -> x42, local copies, waits for them, and re-layouts: 11.1 us -> 12.5 us
where the time goes in v4:
time: 413 us; the launch traced here: 406 us
  Pallas kernels  364 us (88%)
  local copies, waits for them, and re-layouts  25.6 us (6%)
  matrix products  10.7 us (3%)
  other arithmetic  5.08 us (1%)
    pallas_call x1, Pallas kernels, block_call(): pl.pallas_call(functools.partial(block_kernel, dims, micro, length, steps...  364 us
    unnamed x42, local copies, waits for them, and re-layouts  12.5 us

profile of v4, /device:TPU:0, one launch (start us, length us, event | category | flops | bytes accessed | tf_op | source)
XLA Modules:
  0.0 406.4 jit_solution(4208848885205414870)
XLA Ops:
  0.7 0.8 select_reduce_fusion.2
  1.4 0.8 select_reduce_fusion
  3.0 1.5 fusion.45
  5.1 1.8 fusion.10
  7.7 1.8 fusion.11
  9.6 1.3 pad_maximum_fusion.refs_0_
  10.9 0.8 reshape.244.refs_2_
  12.0 0.7 fusion.40.refs_1_
  13.8 1.4 reshape.246.refs_13_
  15.9 0.9 reshape.245.refs_11_
  16.8 0.7 copy.93.refs_9_
  17.4 363.7 %shard_map.297 = (bf16[768,1024]{1,0:T(8,128)(2,1)}, bf16[2,1536,256]{2,1,0:T(8,128)(2,1)}, f32[32,8448]{1,0:T(8,128)}, f32[32,3072]{1,0:T(8,128)}, f32[32,1024]...) custom-call(bf16[2,1536,256]{2,1,0:T(8,128)(2,1)} %pad_maximum_fusio, ...), custom_call_target="tpu_custom_call" | custom-call | tf_op jit(solution)/shard_map/pallas_call | solution.py:900
  381.4 2.9 fusion.16
  384.3 1.4 fusion.17
  385.7 1.4 fusion.18
  387.1 1.4 fusion.19
  388.7 1.8 copy.99
  391.1 2.8 slice_reduce_fusion
  393.9 0.9 copy.115
  394.9 0.9 copy.113
  395.8 0.9 copy.114
  397.1 1.1 slice_reduce_fusion.3
  398.2 0.7 copy.110
  398.9 0.7 copy.111
  399.5 0.7 copy.112
  400.3 0.7 copy.101
  401.0 0.7 copy.102
  402.3 0.7 copy.100
  403.0 0.7 slice_reduce_fusion.6
  403.7 0.7 slice_reduce_fusion.8
  404.4 1.1 copy.118
  405.5 0.7 copy.119
  (72 shorter events, 6.1 us)
Async XLA Ops:
  9.5 3.1 copy-start.4
  9.5 3.3 copy-start.5
  9.6 3.4 copy-start.6
  13.2 2.0 copy-start.8
  13.2 2.0 copy-start.9
  13.3 2.1 copy-start.10
  13.8 3.0 copy-start.11
  381.4 2.9 copy-start.12
  388.7 1.8 copy-start.1
  393.9 2.9 copy-start.3
  395.8 4.4 %copy-start.2 = (f32[32,128]{1,0:T(8,128)S(1)}, f32[32,128]{1,0:T(8,128)}, u32[]{:S(2)}) copy-start(f32[32,128]{1,0:T(8,128)} %get-tuple-element.24) | copy-start | bytes 49156
  396.8 7.6 %copy-start = (bf16[768,1024]{1,0:T(8,128)(2,1)S(1)}, bf16[768,1024]{1,0:T(8,128)(2,1)}, u32[]{:S(2)}) copy-start(bf16[768,1024]{1,0:T(8,128)(2,1)} %get-tuple-element.22) | copy-start | bytes 4718596
  404.4 1.1 copy-start.7

commit v5 on v4

--- a/solution.py
+++ b/solution.py
@@ -24,8 +24,8 @@
 CXYZ, CYXZ = (C, X, Y, Z), (C, Y, X, Z)
 GATHER_TICKS = (0, 2, 4, 6, 8)
 FEED_TICKS = (0, 2, 4, 6, 7)
-SCATTER_TICKS = (0, 1, 3, 5, 7)
-SLOTS = (4, 6, 6, 4)
+SCATTER_TICKS = (0, 1, 3, 4, 5)
+SLOTS = (4, 5, 3, 2)
 
 ROW_CONV, ROW_ATTN, ROW_MLP, ROW_OUT, ROW_BETA, SMALL_ROWS = 0, 12, 13, 14, 16, 32
 
@@ -856,8 +856,8 @@
         tokens_back(m).wait()
 
 
-EARLY = 3
-TOKENS_AT = 8
+EARLY = 4
+TOKENS_AT = 6
 
 
 def block_call(tokens, take, back, smalls, grad, qkv_shard, out_shard, feed_shard, micro):

time: 413 us -> 406 us (0.983)
  Pallas kernels: 364 us -> 356 us
    pallas_call x1, Pallas kernels: 364 us -> 356 us  [block_call(): pl.pallas_call(functools.partial(block_kernel, dims, micro, length, steps...]
where the time goes in v5:
time: 406 us; the launch traced here: 399 us
  Pallas kernels  356 us (88%)
  local copies, waits for them, and re-layouts  25.6 us (6%)
  matrix products  10.7 us (3%)
  other arithmetic  5.08 us (1%)
    pallas_call x1, Pallas kernels, block_call(): pl.pallas_call(functools.partial(block_kernel, dims, micro, length, steps...  356 us
    unnamed x42, local copies, waits for them, and re-layouts  12.5 us

profile of v5, /device:TPU:0, one launch (start us, length us, event | category | flops | bytes accessed | tf_op | source)
XLA Modules:
  0.0 399.0 jit_solution(1146860500230701259)
XLA Ops:
  0.7 0.8 select_reduce_fusion.2
  1.4 0.8 select_reduce_fusion
  3.0 1.5 fusion.45
  5.1 1.8 fusion.10
  7.7 1.8 fusion.11
  9.6 1.3 pad_maximum_fusion.refs_0_
  10.9 0.8 reshape.244.refs_2_
  12.0 0.7 fusion.40.refs_1_
  13.8 1.4 reshape.246.refs_13_
  15.9 0.9 reshape.245.refs_11_
  16.8 0.7 copy.93.refs_9_
  17.4 356.4 %shard_map.297 = (bf16[768,1024]{1,0:T(8,128)(2,1)}, bf16[2,1536,256]{2,1,0:T(8,128)(2,1)}, f32[32,8448]{1,0:T(8,128)}, f32[32,3072]{1,0:T(8,128)}, f32[32,1024]...) custom-call(bf16[2,1536,256]{2,1,0:T(8,128)(2,1)} %pad_maximum_fusio, ...), custom_call_target="tpu_custom_call" | custom-call | tf_op jit(solution)/shard_map/pallas_call | solution.py:900
  374.1 2.9 fusion.16
  377.0 1.4 fusion.17
  378.4 1.4 fusion.18
  379.8 1.4 fusion.19
  381.4 1.8 copy.99
  383.8 2.8 slice_reduce_fusion
  386.6 0.9 copy.115
  387.6 0.9 copy.113
  388.5 0.9 copy.114
  389.8 1.1 slice_reduce_fusion.3
  390.8 0.7 copy.110
  391.5 0.7 copy.111
  392.2 0.7 copy.112
  393.0 0.7 copy.101
  393.6 0.7 copy.102
  395.0 0.7 copy.100
  395.7 0.7 slice_reduce_fusion.6
  396.4 0.7 slice_reduce_fusion.8
  397.1 1.1 copy.118
  398.2 0.7 copy.119
  (72 shorter events, 6.1 us)
Async XLA Ops:
  9.5 3.1 copy-start.4
  9.5 3.3 copy-start.5
  9.6 3.4 copy-start.6
  13.2 2.0 copy-start.8
  13.2 2.0 copy-start.9
  13.3 2.1 copy-start.10
  13.8 3.0 copy-start.11
  374.1 2.9 copy-start.12
  381.4 1.8 copy-start.1
  386.6 2.9 copy-start.3
  388.5 4.4 %copy-start.2 = (f32[32,128]{1,0:T(8,128)S(1)}, f32[32,128]{1,0:T(8,128)}, u32[]{:S(2)}) copy-start(f32[32,128]{1,0:T(8,128)} %get-tuple-element.24) | copy-start | bytes 49156
  389.5 7.6 %copy-start = (bf16[768,1024]{1,0:T(8,128)(2,1)S(1)}, bf16[768,1024]{1,0:T(8,128)(2,1)}, u32[]{:S(2)}) copy-start(bf16[768,1024]{1,0:T(8,128)(2,1)} %get-tuple-element.22) | copy-start | bytes 4718596
  397.1 1.1 copy-start.7
